TPU v7x, 32 devices: a whole 2x2x4 slice. The times are simulated.
32 devices in a mesh: fsdp: 4 (over z), ctx: 2 (over x), tp: 4 (over y, core).
Axes of the slice: x: 2, y: 2, z: 4, core: 2. Of those that a mesh axis runs over, the one named last changes fastest.
Arguments:
- inputs: bfloat16 [2, 4, 512, 2048], P(None, 'fsdp', 'ctx'), may hold values from -6 to 6
- out_grad: bfloat16 [2, 4, 512, 2048], P(None, 'fsdp', 'ctx'), may hold values from -6 to 6
- segments: int32 [2, 4, 512], P(None, 'fsdp'), may hold values from 0 to 3, never falling along the last dimension, each value on 1 to 384 neighbouring positions
- w_query: bfloat16 [2048, 2048], P('fsdp', 'tp'), may hold values from -0.125 to 0.125
- w_key: bfloat16 [2048, 2048], P('fsdp', 'tp'), may hold values from -0.125 to 0.125
- w_value: bfloat16 [2048, 2048], P('fsdp', 'tp'), may hold values from -0.125 to 0.125
- w_out: bfloat16 [2048, 2048], P('tp', 'fsdp'), may hold values from -0.125 to 0.125
- w_gate: bfloat16 [2048, 8192], P('fsdp', 'tp'), may hold values from -0.125 to 0.125
- w_up: bfloat16 [2048, 8192], P('fsdp', 'tp'), may hold values from -0.125 to 0.125
- w_down: bfloat16 [8192, 2048], P('tp', 'fsdp'), may hold values from -0.0625 to 0.0625
- query_gain: bfloat16 [16, 128], P('tp', 'fsdp'), may hold values from 0.099609375 to 1.8984375
- key_gain: bfloat16 [16, 128], P('tp', 'fsdp'), may hold values from 0.099609375 to 1.8984375
- attn_gain: bfloat16 [2048], P('fsdp'), may hold values from 0.099609375 to 1.8984375
- mlp_gain: bfloat16 [2048], P('fsdp'), may hold values from 0.099609375 to 1.8984375
Outputs:
- output: bfloat16 [2, 4, 512, 2048], P(None, 'fsdp', 'ctx')
- input_grad: float32 [2, 4, 512, 2048], P(None, 'fsdp', 'ctx')
- w_query_grad: float32 [2048, 2048], P('fsdp', 'tp')
- w_key_grad: float32 [2048, 2048], P('fsdp', 'tp')
- w_value_grad: float32 [2048, 2048], P('fsdp', 'tp')
- w_out_grad: float32 [2048, 2048], P('tp', 'fsdp')
- w_gate_grad: float32 [2048, 8192], P('fsdp', 'tp')
- w_up_grad: float32 [2048, 8192], P('fsdp', 'tp')
- w_down_grad: float32 [8192, 2048], P('tp', 'fsdp')
- query_gain_grad: float32 [16, 128], P('tp', 'fsdp')
- key_gain_grad: float32 [16, 128], P('tp', 'fsdp')
- attn_gain_grad: float32 [2048], P('fsdp')
- mlp_gain_grad: float32 [2048], P('fsdp')
Inputs may be any that keep to these rules, and one draw needn't show every extreme that they name: `segments`: segment numbers never fall along a sequence; a run of equal numbers is one document, of at most 384 tokens, and one document of each sequence has exactly that many.
All inputs are finite; a program needn't handle non-finite values.
Results may differ from a plain program's by a relative error of at most 0.02.
Values may be sent and summed in bfloat16 or wider, within the bound.
No kernel may reach another device: no remote copies, remote signals or barrier semaphores. Data moves between devices by JAX's collectives and lax.ppermute only.
A program may use at most 192 MiB of HBM per device.

v0:
```python
import math

import jax
import jax.numpy as jnp
from jax import lax
from jax.sharding import PartitionSpec as P

D = 2048
HD = 128


EPSILON = 1e-06
ROTARY_BASE = 500000.0
MASKED = -1e30


def product(left_side, right_side):
    return jnp.dot(left_side, right_side, preferred_element_type=jnp.float32)


def product_back(left_side, right_side):
    return lax.dot_general(
        left_side, right_side, (((1,), (1,)), ((), ())), preferred_element_type=jnp.float32
    )


def product_left(left_side, right_side):
    return lax.dot_general(
        left_side, right_side, (((0,), (0,)), ((), ())), preferred_element_type=jnp.float32
    )


def rms_norm(values, gain_row):
    return (
        values * lax.rsqrt(jnp.mean(values * values, axis=-1, keepdims=True) + EPSILON) * gain_row
    )


def doc_positions(segment_row):
    earlier = (segment_row[None, :] < segment_row[:, None]).astype(jnp.int32)
    return jnp.arange(segment_row.shape[0], dtype=jnp.int32) - jnp.sum(earlier, axis=1)


def rotary_tables(positions):
    half_size = HD // 2
    frequency = ROTARY_BASE ** (-(jnp.arange(half_size, dtype=jnp.float32) * 2.0 / HD))
    angle_table = positions.astype(jnp.float32)[:, None] * frequency[None, :]
    return (jnp.cos(angle_table)[:, None, :], jnp.sin(angle_table)[:, None, :])


def rotate(values, cosine, sine_table):
    half_size = values.shape[-1] // 2
    first_half = values[..., :half_size]
    second_half = values[..., half_size:]
    return jnp.concatenate(
        [
            first_half * cosine - second_half * sine_table,
            second_half * cosine + first_half * sine_table,
        ],
        axis=-1,
    )


def rotate_back(values, cosine, sine_table):
    half_size = values.shape[-1] // 2
    first_half = values[..., :half_size]
    second_half = values[..., half_size:]
    return jnp.concatenate(
        [
            first_half * cosine + second_half * sine_table,
            second_half * cosine - first_half * sine_table,
        ],
        axis=-1,
    )


def attention_mask(segment_row):
    places = jnp.arange(segment_row.shape[0])
    return (segment_row[:, None] == segment_row[None, :]) & (places[None, :] <= places[:, None])


def head_scores(query_heads, key_heads, allowed):
    raw_scores = jnp.einsum(
        "qhd,khd->hqk", query_heads, key_heads, preferred_element_type=jnp.float32
    ) * (1.0 / math.sqrt(HD))
    return jnp.where(allowed[None], raw_scores, MASKED)


def fetch_forward(shards):
    (
        w_query,
        w_key,
        w_value,
        w_gate,
        w_up,
        w_out,
        w_down,
        query_gain,
        key_gain,
        attn_gain,
        mlp_gain,
    ) = shards
    return (
        lax.all_gather(w_query, "fsdp", axis=0, tiled=True),
        lax.all_gather(w_key, "fsdp", axis=0, tiled=True),
        lax.all_gather(w_value, "fsdp", axis=0, tiled=True),
        lax.all_gather(w_gate, "fsdp", axis=0, tiled=True),
        lax.all_gather(w_up, "fsdp", axis=0, tiled=True),
        lax.all_gather(w_out, "fsdp", axis=1, tiled=True),
        lax.all_gather(w_down, "fsdp", axis=1, tiled=True),
        lax.all_gather(query_gain, "fsdp", axis=1, tiled=True),
        lax.all_gather(key_gain, "fsdp", axis=1, tiled=True),
        lax.all_gather(attn_gain, "fsdp", axis=0, tiled=True),
        lax.all_gather(mlp_gain, "fsdp", axis=0, tiled=True),
    )


def fetch_backward(shards):
    (
        w_query,
        w_key,
        w_value,
        w_gate,
        w_up,
        w_out,
        w_down,
        query_gain,
        key_gain,
        attn_gain,
        mlp_gain,
    ) = shards
    return (
        lax.all_gather(w_query, "fsdp", axis=0, tiled=True),
        lax.all_gather(w_key, "fsdp", axis=0, tiled=True),
        lax.all_gather(w_value, "fsdp", axis=0, tiled=True),
        lax.all_gather(w_gate, "fsdp", axis=0, tiled=True),
        lax.all_gather(w_up, "fsdp", axis=0, tiled=True),
        lax.all_gather(w_out, "fsdp", axis=1, tiled=True),
        lax.all_gather(w_down, "fsdp", axis=1, tiled=True),
        lax.all_gather(query_gain, "fsdp", axis=1, tiled=True),
        lax.all_gather(key_gain, "fsdp", axis=1, tiled=True),
        lax.all_gather(attn_gain, "fsdp", axis=0, tiled=True),
        lax.all_gather(mlp_gain, "fsdp", axis=0, tiled=True),
    )


def local(
    inputs,
    out_grad,
    segments,
    w_query,
    w_key,
    w_value,
    w_out,
    w_gate,
    w_up,
    w_down,
    query_gain,
    key_gain,
    attn_gain,
    mlp_gain,
):
    micro_count = inputs.shape[0]
    local_len = inputs.shape[2]
    ctx_place = lax.axis_index("ctx")
    shards = (
        w_query,
        w_key,
        w_value,
        w_gate,
        w_up,
        w_out,
        w_down,
        query_gain,
        key_gain,
        attn_gain,
        mlp_gain,
    )
    scale_factor = 1.0 / math.sqrt(HD)
    totals = None
    outputs = []
    input_grads = []
    for micro_step in range(micro_count):
        (
            query_full,
            key_full,
            value_full,
            gate_full,
            up_full,
            out_full,
            down_full,
            query_gains,
            key_gains,
            attn_gains,
            mlp_gains,
        ) = fetch_forward(shards)
        heads_here = query_gains.shape[0]
        query_gain_row = query_gains.astype(jnp.float32).reshape(-1)
        key_gain_row = key_gains.astype(jnp.float32).reshape(-1)
        tokens_in = inputs[micro_step, 0]
        tokens_wide = tokens_in.astype(jnp.float32)
        cotangent = out_grad[micro_step, 0].astype(jnp.float32)
        segment_row = segments[micro_step, 0]
        allowed = attention_mask(segment_row)
        positions = lax.dynamic_slice_in_dim(
            doc_positions(segment_row), ctx_place * local_len, local_len
        )
        cosine, sine_table = rotary_tables(positions)
        query_raw = product(tokens_in, query_full)
        key_raw = product(tokens_in, key_full)
        value_low = product(tokens_in, value_full).astype(jnp.bfloat16)
        query_sq, key_sq = lax.psum(
            (jnp.sum(query_raw * query_raw, axis=1), jnp.sum(key_raw * key_raw, axis=1)), "tp"
        )
        query_scale = lax.rsqrt(query_sq / D + EPSILON)[:, None]
        key_scale = lax.rsqrt(key_sq / D + EPSILON)[:, None]
        query_rot = rotate(
            (query_raw * query_scale * query_gain_row).reshape(local_len, heads_here, HD),
            cosine,
            sine_table,
        ).astype(jnp.bfloat16)
        key_rot = rotate(
            (key_raw * key_scale * key_gain_row).reshape(local_len, heads_here, HD),
            cosine,
            sine_table,
        ).astype(jnp.bfloat16)
        query_heads, key_heads, value_heads = (
            lax.all_to_all(query_rot, "ctx", split_axis=1, concat_axis=0, tiled=True),
            lax.all_to_all(key_rot, "ctx", split_axis=1, concat_axis=0, tiled=True),
            lax.all_to_all(
                value_low.reshape(local_len, heads_here, HD),
                "ctx",
                split_axis=1,
                concat_axis=0,
                tiled=True,
            ),
        )
        scores = head_scores(query_heads, key_heads, allowed)
        top_score = jnp.max(scores, axis=-1, keepdims=True)
        log_total = top_score + jnp.log(
            jnp.sum(jnp.exp(scores - top_score), axis=-1, keepdims=True)
        )
        probs_low = jnp.exp(scores - log_total).astype(jnp.bfloat16)
        head_out = jnp.einsum(
            "hqk,khd->qhd", probs_low, value_heads, preferred_element_type=jnp.float32
        ).astype(jnp.bfloat16)
        attended = lax.all_to_all(head_out, "ctx", split_axis=0, concat_axis=1, tiled=True).reshape(
            local_len, -1
        )
        branch = lax.psum(product(attended, out_full), "tp")
        attn_norm, attn_pull = jax.vjp(rms_norm, branch, attn_gains.astype(jnp.float32))
        hidden_in = tokens_wide + attn_norm
        hidden_low = hidden_in.astype(jnp.bfloat16)
        gate_value = product(hidden_low, gate_full)
        up_value = product(hidden_low, up_full)
        swish_out, swish_pull = jax.vjp(
            lambda gate_arg, up_arg: jax.nn.silu(gate_arg) * up_arg, gate_value, up_value
        )
        activated = swish_out.astype(jnp.bfloat16)
        down_value = lax.psum(product(activated, down_full), "tp")
        mlp_norm, mlp_pull = jax.vjp(rms_norm, down_value, mlp_gains.astype(jnp.float32))
        outputs.append((hidden_in + mlp_norm).astype(jnp.bfloat16))
        (
            query_full,
            key_full,
            value_full,
            gate_full,
            up_full,
            out_full,
            down_full,
            query_gains,
            key_gains,
            attn_gains,
            mlp_gains,
        ) = fetch_backward(shards)
        down_grad, mlp_gain_grad = mlp_pull(cotangent)
        down_low = down_grad.astype(jnp.bfloat16)
        act_grad = product_back(down_low, down_full)
        gate_grad, up_grad = swish_pull(act_grad)
        gate_low = gate_grad.astype(jnp.bfloat16)
        up_low = up_grad.astype(jnp.bfloat16)
        hidden_grad = cotangent + lax.psum(
            product_back(gate_low, gate_full) + product_back(up_low, up_full), "tp"
        )
        branch_grad, attn_gain_grad = attn_pull(hidden_grad)
        branch_low = branch_grad.astype(jnp.bfloat16)
        attended_grad = (
            product_back(branch_low, out_full)
            .astype(jnp.bfloat16)
            .reshape(local_len, heads_here, HD)
        )
        out_heads_grad = lax.all_to_all(
            attended_grad, "ctx", split_axis=1, concat_axis=0, tiled=True
        )
        scores = head_scores(query_heads, key_heads, allowed)
        attn_probs = jnp.exp(scores - log_total)
        probs_again = attn_probs.astype(jnp.bfloat16)
        value_grad = jnp.einsum(
            "hqk,qhd->khd", probs_again, out_heads_grad, preferred_element_type=jnp.float32
        )
        probs_grad = jnp.einsum(
            "qhd,khd->hqk", out_heads_grad, value_heads, preferred_element_type=jnp.float32
        )
        score_grad = (
            attn_probs * (probs_grad - jnp.sum(attn_probs * probs_grad, axis=-1, keepdims=True))
        ).astype(jnp.bfloat16)
        query_grad = (
            jnp.einsum("hqk,khd->qhd", score_grad, key_heads, preferred_element_type=jnp.float32)
            * scale_factor
        ).astype(jnp.bfloat16)
        key_grad = (
            jnp.einsum("hqk,qhd->khd", score_grad, query_heads, preferred_element_type=jnp.float32)
            * scale_factor
        ).astype(jnp.bfloat16)
        query_back, key_back, value_back = (
            lax.all_to_all(query_grad, "ctx", split_axis=0, concat_axis=1, tiled=True),
            lax.all_to_all(key_grad, "ctx", split_axis=0, concat_axis=1, tiled=True),
            lax.all_to_all(
                value_grad.astype(jnp.bfloat16), "ctx", split_axis=0, concat_axis=1, tiled=True
            ),
        )
        query_norm_grad = rotate_back(query_back.astype(jnp.float32), cosine, sine_table).reshape(
            local_len, -1
        )
        key_norm_grad = rotate_back(key_back.astype(jnp.float32), cosine, sine_table).reshape(
            local_len, -1
        )
        query_term = query_norm_grad * query_gain_row
        key_term = key_norm_grad * key_gain_row
        query_dot, key_dot = lax.psum(
            (jnp.sum(query_term * query_raw, axis=1), jnp.sum(key_term * key_raw, axis=1)), "tp"
        )
        query_cube = query_scale * query_scale * query_scale
        key_cube = key_scale * key_scale * key_scale
        query_raw_grad = (
            query_scale * query_term - query_raw * query_cube * query_dot[:, None] / D
        ).astype(jnp.bfloat16)
        key_raw_grad = (key_scale * key_term - key_raw * key_cube * key_dot[:, None] / D).astype(
            jnp.bfloat16
        )
        value_low_grad = value_back.reshape(local_len, -1)
        query_gain_grad = jnp.sum(query_norm_grad * query_raw * query_scale, axis=0).reshape(
            heads_here, HD
        )
        key_gain_grad = jnp.sum(key_norm_grad * key_raw * key_scale, axis=0).reshape(heads_here, HD)
        input_part = (
            product_back(query_raw_grad, query_full)
            + product_back(key_raw_grad, key_full)
            + product_back(value_low_grad, value_full)
        )
        input_grads.append(
            hidden_grad + lax.psum(input_part.astype(jnp.bfloat16), "tp").astype(jnp.float32)
        )
        step_grads = (
            product_left(tokens_in, query_raw_grad),
            product_left(tokens_in, key_raw_grad),
            product_left(tokens_in, value_low_grad),
            product_left(hidden_low, gate_low),
            product_left(hidden_low, up_low),
            product_left(attended, branch_low),
            product_left(activated, down_low),
            query_gain_grad,
            key_gain_grad,
            attn_gain_grad,
            mlp_gain_grad,
        )
        if totals is None:
            totals = step_grads
        else:
            totals = tuple((running + addend for running, addend in zip(totals, step_grads)))
    (
        grad_query,
        grad_key,
        grad_value,
        grad_gate,
        grad_up,
        grad_out,
        grad_down,
        grad_qgain,
        grad_kgain,
        grad_again,
        grad_mgain,
    ) = totals
    (
        part_query,
        part_key,
        part_value,
        part_gate,
        part_up,
        part_out,
        part_down,
        part_qgain,
        part_kgain,
        part_again,
        part_mgain,
    ) = (
        lax.psum_scatter(
            grad_query.astype(jnp.bfloat16), "fsdp", scatter_dimension=0, tiled=True
        ).astype(jnp.float32),
        lax.psum_scatter(
            grad_key.astype(jnp.bfloat16), "fsdp", scatter_dimension=0, tiled=True
        ).astype(jnp.float32),
        lax.psum_scatter(
            grad_value.astype(jnp.bfloat16), "fsdp", scatter_dimension=0, tiled=True
        ).astype(jnp.float32),
        lax.psum_scatter(
            grad_gate.astype(jnp.bfloat16), "fsdp", scatter_dimension=0, tiled=True
        ).astype(jnp.float32),
        lax.psum_scatter(
            grad_up.astype(jnp.bfloat16), "fsdp", scatter_dimension=0, tiled=True
        ).astype(jnp.float32),
        lax.psum_scatter(
            grad_out.astype(jnp.bfloat16), "fsdp", scatter_dimension=1, tiled=True
        ).astype(jnp.float32),
        lax.psum_scatter(
            grad_down.astype(jnp.bfloat16), "fsdp", scatter_dimension=1, tiled=True
        ).astype(jnp.float32),
        lax.psum_scatter(
            grad_qgain.astype(jnp.bfloat16), "fsdp", scatter_dimension=1, tiled=True
        ).astype(jnp.float32),
        lax.psum_scatter(
            grad_kgain.astype(jnp.bfloat16), "fsdp", scatter_dimension=1, tiled=True
        ).astype(jnp.float32),
        lax.psum_scatter(
            grad_again.astype(jnp.bfloat16), "fsdp", scatter_dimension=0, tiled=True
        ).astype(jnp.float32),
        lax.psum_scatter(
            grad_mgain.astype(jnp.bfloat16), "fsdp", scatter_dimension=0, tiled=True
        ).astype(jnp.float32),
    )
    (
        sum_query,
        sum_key,
        sum_value,
        sum_gate,
        sum_up,
        sum_out,
        sum_down,
        sum_qgain,
        sum_kgain,
        sum_again,
        sum_mgain,
    ) = (
        lax.psum(part_query.astype(jnp.bfloat16), "ctx").astype(jnp.float32),
        lax.psum(part_key.astype(jnp.bfloat16), "ctx").astype(jnp.float32),
        lax.psum(part_value.astype(jnp.bfloat16), "ctx").astype(jnp.float32),
        lax.psum(part_gate.astype(jnp.bfloat16), "ctx").astype(jnp.float32),
        lax.psum(part_up.astype(jnp.bfloat16), "ctx").astype(jnp.float32),
        lax.psum(part_out.astype(jnp.bfloat16), "ctx").astype(jnp.float32),
        lax.psum(part_down.astype(jnp.bfloat16), "ctx").astype(jnp.float32),
        lax.psum(part_qgain.astype(jnp.bfloat16), "ctx").astype(jnp.float32),
        lax.psum(part_kgain.astype(jnp.bfloat16), "ctx").astype(jnp.float32),
        lax.psum(part_again.astype(jnp.bfloat16), "ctx").astype(jnp.float32),
        lax.psum(part_mgain.astype(jnp.bfloat16), "ctx").astype(jnp.float32),
    )
    layer_out = jnp.stack(outputs)[:, None]
    layer_in_grad = jnp.stack(input_grads)[:, None]
    return (
        layer_out,
        layer_in_grad,
        sum_query,
        sum_key,
        sum_value,
        sum_out,
        sum_gate,
        sum_up,
        sum_down,
        sum_qgain,
        sum_kgain,
        sum_again,
        sum_mgain,
    )


def solution(mesh):
    placed = (
        P(None, "fsdp", "ctx", None),
        P(None, "fsdp", "ctx", None),
        P(None, "fsdp", None),
        P("fsdp", "tp"),
        P("fsdp", "tp"),
        P("fsdp", "tp"),
        P("tp", "fsdp"),
        P("fsdp", "tp"),
        P("fsdp", "tp"),
        P("tp", "fsdp"),
        P("tp", "fsdp"),
        P("tp", "fsdp"),
        P("fsdp"),
        P("fsdp"),
    )
    return jax.shard_map(
        local,
        mesh=mesh,
        in_specs=placed,
        out_specs=(
            P(None, "fsdp", "ctx", None),
            P(None, "fsdp", "ctx", None),
            P("fsdp", "tp"),
            P("fsdp", "tp"),
            P("fsdp", "tp"),
            P("tp", "fsdp"),
            P("fsdp", "tp"),
            P("fsdp", "tp"),
            P("tp", "fsdp"),
            P("tp", "fsdp"),
            P("tp", "fsdp"),
            P("fsdp"),
            P("fsdp"),
        ),
        check_vma=False,
    )
```

profile of v0, /device:TPU:0, one launch (start us, length us, event | category | flops | bytes accessed | tf_op | source)
XLA Modules:
  0.0 1978.6 jit_solution(3820029467599799475)
XLA Ops:
  10.0 12.6 all-gather
  22.8 7.7 all-gather.1
  32.6 25.7 %all-gather.12.cloned.1.call-done = bf16[2048,512]{1,0:T(8,128)(2,1)} async-done(((bf16[512,512]{1,0:T(8,128)(2,1)}), bf16[2048,512]{1,0:T(8,128)(2,1)}) %all-gather.12.cloned.1.call-update) | async-done | bytes 2097168 | tf_op jit(solution)/shard_map/all_gather | solution.py:106
  61.4 4.1 all-to-all-start.4
  65.5 39.1 %all-gather.16.cloned.1.call-done = bf16[2048,512]{1,0:T(8,128)(2,1)} async-done(((bf16[512,512]{1,0:T(8,128)(2,1)}), bf16[2048,512]{1,0:T(8,128)(2,1)}) %all-gather.16.cloned.1.call-update) | async-done | bytes 2097168 | tf_op jit(solution)/shard_map/all_gather | solution.py:105
  104.6 3.8 multiply_reduce_fusion.14
  110.5 40.4 %all-gather.14.cloned.1.call-done = bf16[2048,512]{1,0:T(8,128)(2,1)} async-done(((bf16[512,512]{1,0:T(8,128)(2,1)}), bf16[2048,512]{1,0:T(8,128)(2,1)}) %all-gather.14.cloned.1.call-update) | async-done | bytes 2097168 | tf_op jit(solution)/shard_map/all_gather | solution.py:104
  155.3 7.5 all-reduce.3
  175.4 3.6 all-to-all-start
  180.4 3.8 all-to-all-done
  193.5 3.4 all-to-all-start.1
  202.1 3.4 all-to-all-start.6
  223.8 14.3 all-to-all-start.7
  243.7 3.4 all-to-all-start.3
  247.4 4.9 all-to-all-done.3
  252.5 3.8 fusion.105
  260.5 11.9 all-gather.2
  272.4 68.6 %all-reduce.21.cloned.1.call-done = (f32[256,2048]{1,0:T(8,128)}, f32[256,2048]{1,0:T(8,128)}) async-done(((f32[256,2048]{1,0:T(8,128)}, f32[256,2048]{1,0:T(8,128)}), (f32[256,2048]{1,0:T(8,128)}, f32[256,2048]{1,0:T(8,128)})) %all-reduce.21.cloned.1.call-update) | async-done | bytes 4194320 | tf_op jit(solution)/shard_map/psum | solution.py:250
  348.5 143.9 %all-gather.20.cloned.1.call-done = bf16[2048,2048]{1,0:T(8,128)(2,1)} async-done(((bf16[512,2048]{1,0:T(8,128)(2,1)}), bf16[2048,2048]{1,0:T(8,128)(2,1)}) %all-gather.20.cloned.1.call-update) | async-done | bytes 8388624 | tf_op jit(solution)/shard_map/all_gather | solution.py:107
  492.3 7.5 fusion.109
  499.8 3.8 fusion.106
  503.6 138.3 %all-gather.22.cloned.1.call-done = bf16[2048,2048]{1,0:T(8,128)(2,1)} async-done(((bf16[512,2048]{1,0:T(8,128)(2,1)}), bf16[2048,2048]{1,0:T(8,128)(2,1)}) %all-gather.22.cloned.1.call-update) | async-done | bytes 8388624 | tf_op jit(solution)/shard_map/all_gather | solution.py:108
  641.9 8.3 multiply_convert_fusion.5
  650.2 4.2 multiply_convert_fusion.4
  654.4 137.0 %all-gather.24.cloned.1.call-done = bf16[2048,2048]{1,0:T(8,128)(2,1)} async-done(((bf16[2048,512]{1,0:T(8,128)(2,1)}), bf16[2048,2048]{1,0:T(8,128)(2,1)}) %all-gather.24.cloned.1.call-update) | async-done | bytes 8388624 | tf_op jit(solution)/shard_map/all_gather | solution.py:110
  791.4 7.2 fusion.107
  798.6 4.2 fusion.110
  803.5 11.9 all-gather.3
  815.4 71.5 %all-reduce.19.cloned.1.call-done = (f32[256,2048]{1,0:T(8,128)}, f32[256,2048]{1,0:T(8,128)}) async-done(((f32[256,2048]{1,0:T(8,128)}, f32[256,2048]{1,0:T(8,128)}), (f32[256,2048]{1,0:T(8,128)}, f32[256,2048]{1,0:T(8,128)})) %all-reduce.19.cloned.1.call-update) | async-done | bytes 4194320 | tf_op jit(solution)/shard_map/psum | solution.py:260
  890.7 3.7 fusion.21
  897.3 6.9 multiply_convert_fusion.3
  907.2 6.5 multiply_convert_fusion.1
  916.4 7.2 convolution_add_fusion.4
  923.6 3.7 convolution_add_fusion.5
  927.4 85.9 %all-reduce.17.cloned.1.call-done = (f32[256,2048]{1,0:T(8,128)}, f32[256,2048]{1,0:T(8,128)}) async-done(((f32[256,2048]{1,0:T(8,128)}, f32[256,2048]{1,0:T(8,128)}), (f32[256,2048]{1,0:T(8,128)}, f32[256,2048]{1,0:T(8,128)})) %all-reduce.17.cloned.1.call-update) | async-done | bytes 4194320 | tf_op jit(solution)/shard_map/psum | solution.py:282
  1013.5 9.7 fusion.45
  1031.0 3.5 all-to-all-start.8
  1043.2 5.1 all-to-all-done.12
  1049.8 3.8 all-to-all-start.15
  1058.7 3.4 all-to-all-start.11
  1062.2 3.4 multiply_reduce_fusion.4
  1076.9 3.5 all-to-all-start.10
  1090.2 3.9 all-to-all-done.9
  1099.0 3.8 all-to-all-done.13
  1102.8 3.4 all-to-all-start.14
  1107.4 4.0 all-to-all-done.14
  1116.2 5.8 all-reduce.2
  1134.6 8.2 fusion.117
  1142.8 11.7 add_convert_fusion.1
  1155.6 8.2 fusion.116
  1163.9 11.6 add_convert_fusion.2
  1177.0 8.2 fusion.118
  1185.2 11.6 add_convert_fusion
  1207.0 9.8 reduce-scatter.14.cloned.1.call-done
  1216.8 146.1 %reduce-scatter.24.cloned.1.call-done = bf16[512,2048]{1,0:T(8,128)(2,1)} async-done(((bf16[2048,2048]{1,0:T(8,128)(2,1)}), bf16[512,2048]{1,0:T(8,128)(2,1)}) %reduce-scatter.24.cloned.1.call-update) | async-done | bytes 2097168 | tf_op jit(solution)/shard_map/reduce_scatter | solution.py:409
  1362.9 147.6 %reduce-scatter.22.cloned.1.call-done = bf16[512,2048]{1,0:T(8,128)(2,1)} async-done(((bf16[2048,2048]{1,0:T(8,128)(2,1)}), bf16[512,2048]{1,0:T(8,128)(2,1)}) %reduce-scatter.22.cloned.1.call-update) | async-done | bytes 2097168 | tf_op jit(solution)/shard_map/reduce_scatter | solution.py:406
  1510.5 147.5 %reduce-scatter.26.cloned.1.call-done = bf16[2048,512]{1,0:T(8,128)(2,1)} async-done(((bf16[2048,2048]{1,0:T(8,128)(2,1)}), bf16[2048,512]{1,0:T(8,128)(2,1)}) %reduce-scatter.26.cloned.1.call-update) | async-done | bytes 2097168 | tf_op jit(solution)/shard_map/reduce_scatter | solution.py:415
  1660.0 11.3 all-reduce.8
  1674.4 6.1 reduce-scatter.28.cloned.1.call-done
  1681.3 18.6 reduce-scatter.30.cloned.1.call-done
  1700.6 5.1 all-reduce.9
  1708.1 44.5 %all-reduce.23.cloned.1.call-done = (bf16[256,2048]{1,0:T(8,128)(2,1)}, bf16[256,2048]{1,0:T(8,128)(2,1)}) async-done(((bf16[256,2048]{1,0:T(8,128)(2,1)}, bf16[256,2048]{1,0:T(8,128)(2,1)}), (bf16[256,2048]{1,0:T(8,128)(2,1)}, bf16[256,2048]{1,0:T(8,128)(2,1)})) %all-reduce.23.cloned.1.call-update) | async-done | bytes 2097168 | tf_op jit(solution)/shard_map/psum | solution.py:352
  1752.6 3.8 add_bitcast_fusion.1
  1758.6 198.2 %all-reduce.25.cloned.1.call-done = (bf16[512,512]{0,1:T(8,128)(2,1)}, bf16[512,512]{0,1:T(8,128)(2,1)}, bf16[512,512]{0,1:T(8,128)(2,1)}, bf16[512,512]{1,0:T(8...) async-done(((bf16[512,512]{0,1:T(8,128)(2,1)}, bf16[512,512]{0,1:T(8,128)(2,1)}, bf16[512,512]{0,1:T(8,128)(2,1)}, ...) | async-done | bytes 8388624 | tf_op jit(solution)/shard_map/psum | solution.py:444
  (537 shorter events, 196.0 us)
Async XLA Ops:
  7.2 15.6 copy-start.143
  7.2 23.4 %copy-start.141 = (s32[2,1,512]{2,1,0:T(1,128)S(1)}, s32[2,1,512]{2,1,0:T(1,128)}, u32[]{:S(2)}) copy-start(s32[2,1,512]{2,1,0:T(1,128)} %param.16) | copy-start | bytes 12292
  7.2 51.1 %copy-start.4 = (bf16[2,1,256,2048]{3,2,1,0:T(8,128)(2,1)S(1)}, bf16[2,1,256,2048]{3,2,1,0:T(8,128)(2,1)}, u32[]{:S(2)}) copy-start(bf16[2,1,256,2048]{3,2,1,0:T(8,128)(2,1)} %param.14) | copy-start | bytes 6291460
  7.2 51.1 %all-gather.12.cloned.1.call-start = ((), (), s32[]{:S(2)}) async-start(), calls=%async_computation.25 | async-start | bytes 2621440 | tf_op jit(solution)/shard_map/all_gather | solution.py:106
  8.0 96.6 %all-gather.16.cloned.1.call-start = ((), (), s32[]{:S(2)}) async-start(), calls=%async_computation.27 | async-start | bytes 2621440 | tf_op jit(solution)/shard_map/all_gather | solution.py:105
  8.7 142.2 %all-gather.14.cloned.1.call-start = ((), (), s32[]{:S(2)}) async-start(), calls=%async_computation.26 | async-start | bytes 2621440 | tf_op jit(solution)/shard_map/all_gather | solution.py:104
  9.4 243.1 %all-gather.18.cloned.1.call-start = ((), (), s32[]{:S(2)}) async-start(), calls=%async_computation.28 | async-start | bytes 2621440 | tf_op jit(solution)/shard_map/all_gather | solution.py:109
  22.8 141.4 %copy-start.107 = (f32[128,4]{0,1:T(4,128)}, f32[128,4]{0,1:T(4,128)S(1)}, u32[]{:S(2)}) copy-start(f32[128,4]{0,1:T(4,128)S(1)} %reshape.449) | copy-start | bytes 6148
  30.6 138.6 %copy-start.109 = (f32[128,4]{0,1:T(4,128)}, f32[128,4]{0,1:T(4,128)S(1)}, u32[]{:S(2)}) copy-start(f32[128,4]{0,1:T(4,128)S(1)} %reshape.450) | copy-start | bytes 6148
  32.6 139.1 %copy-start.80 = (f32[256,64]{1,0:T(8,128)}, f32[256,64]{1,0:T(8,128)S(1)}, u32[]{:S(2)}) copy-start(f32[256,64]{1,0:T(8,128)S(1)} %get-tuple-element.190) | copy-start | bytes 196612
  32.6 164.4 %copy-start.78 = (f32[256,64]{1,0:T(8,128)}, f32[256,64]{1,0:T(8,128)S(1)}, u32[]{:S(2)}) copy-start(f32[256,64]{1,0:T(8,128)S(1)} %get-tuple-element.179) | copy-start | bytes 196612
  61.4 114.0 %all-to-all-start.4 = ((bf16[256,4,128]{2,0,1:T(8,128)(2,1)}), bf16[256,4,128]{2,0,1:T(8,128)(2,1)}, u32[]{:S(2)}, u32[]{:S(2)}) async-start(bf16[256,4,128]{2,0,1:T(8,128)(2,1)} %bitcast.371), calls=%async_computation.4 | async-start | bytes 524288 | tf_op jit(solution)/shard_map/all_to_all | solution.py:230
  155.3 12.5 copy-start.36
  175.4 8.8 all-to-all-start
  184.9 8.6 all-to-all-start.2
  193.5 8.6 all-to-all-start.1
  197.9 18.5 copy-start.91
  202.1 8.6 all-to-all-start.6
  210.7 8.6 all-to-all-start.5
  216.8 23.2 %copy-start.52 = (bf16[512,2,128]{0,2,1:T(8,128)(2,1)}, bf16[512,2,128]{0,2,1:T(8,128)(2,1)S(1)}, u32[]{:S(2)}) copy-start(bf16[512,2,128]{0,2,1:T(8,128)(2,1)S(1)} %all_to_all.179) | copy-start | bytes 786436
  216.8 21.3 %copy-start.58 = (bf16[256,2,2,128]{3,0,1,2:T(8,128)(2,1)}, bf16[256,2,2,128]{3,0,1,2:T(8,128)(2,1)S(1)}, u32[]{:S(2)}) copy-start(bf16[256,2,2,128]{3,0,1,2:T(8,128)(2,1)S(1)} %copy.167) | copy-start | bytes 786436
  216.9 21.3 %copy-start.60 = (bf16[256,2,2,128]{3,0,1,2:T(8,128)(2,1)}, bf16[256,2,2,128]{3,0,1,2:T(8,128)(2,1)S(1)}, u32[]{:S(2)}) copy-start(bf16[256,2,2,128]{3,0,1,2:T(8,128)(2,1)S(1)} %copy.163) | copy-start | bytes 786436
  223.8 19.8 %all-to-all-start.7 = ((bf16[512,2,128]{2,1,0:T(2,128)(2,1)}), bf16[512,2,128]{2,1,0:T(2,128)(2,1)S(1)}, u32[]{:S(2)}, u32[]{:S(2)}) async-start(bf16[512,2,128]{2,1,0:T(2,128)(2,1)} %copy.181), calls=%async_computation.7 | async-start | bytes 524288 | tf_op jit(solution)/shard_map/all_to_all | solution.py:247
  243.7 8.6 all-to-all-start.3
  247.1 93.9 %all-reduce.21.cloned.1.call-start = ((), (), s32[]{:S(2)}) async-start(), calls=%async_computation.43 | async-start | bytes 8388608 | tf_op jit(solution)/shard_map/psum | solution.py:250
  258.4 233.9 %all-gather.20.cloned.1.call-start = ((), (), s32[]{:S(2)}) async-start(), calls=%async_computation.29 | async-start | bytes 10485760 | tf_op jit(solution)/shard_map/all_gather | solution.py:107
  259.0 382.9 %all-gather.22.cloned.1.call-start = ((), (), s32[]{:S(2)}) async-start(), calls=%async_computation.30 | async-start | bytes 10485760 | tf_op jit(solution)/shard_map/all_gather | solution.py:108
  259.7 531.7 %all-gather.24.cloned.1.call-start = ((), (), s32[]{:S(2)}) async-start(), calls=%async_computation.31 | async-start | bytes 10485760 | tf_op jit(solution)/shard_map/all_gather | solution.py:110
  260.5 626.4 %all-reduce.19.cloned.1.call-start = ((), (), s32[]{:S(2)}) async-start(), calls=%async_computation.42 | async-start | bytes 8388608 | tf_op jit(solution)/shard_map/psum | solution.py:260
  348.5 293.4 %copy-start.17 = (bf16[256,2048]{1,0:T(8,128)(2,1)}, bf16[256,2048]{1,0:T(8,128)(2,1)S(1)}, u32[]{:S(2)}) copy-start(bf16[256,2048]{1,0:T(8,128)(2,1)S(1)} %get-tuple-element.129) | copy-start | bytes 3145732
  650.2 141.2 %copy-start.83 = (bf16[256,2048]{1,0:T(8,128)(2,1)S(1)}, bf16[256,2048]{1,0:T(8,128)(2,1)}, u32[]{:S(2)}) copy-start(bf16[256,2048]{1,0:T(8,128)(2,1)} %get-tuple-element.204) | copy-start | bytes 3145732
  802.8 210.5 %all-reduce.17.cloned.1.call-start = ((), (), s32[]{:S(2)}) async-start(), calls=%async_computation.41 | async-start | bytes 8388608 | tf_op jit(solution)/shard_map/psum | solution.py:282
  895.5 11.4 copy-start.46
  904.2 19.4 copy-start.87
  927.4 86.0 %copy-start.124 = (f32[256]{0:T(256)S(1)}, f32[256]{0:T(256)}, u32[]{:S(2)}) copy-start(f32[256]{0:T(256)} %copy-done.123) | copy-start | bytes 3076
  927.4 86.0 %copy-start.126 = (f32[256]{0:T(256)S(1)}, f32[256]{0:T(256)}, u32[]{:S(2)}) copy-start(f32[256]{0:T(256)} %copy-done.125) | copy-start | bytes 3076
  927.4 86.0 %copy-start.128 = (f32[256]{0:T(256)S(1)}, f32[256]{0:T(256)}, u32[]{:S(2)}) copy-start(f32[256]{0:T(256)} %copy-done.127) | copy-start | bytes 3076
  927.4 86.0 %copy-start.131 = (f32[256]{0:T(256)S(1)}, f32[256]{0:T(256)}, u32[]{:S(2)}) copy-start(f32[256]{0:T(256)} %copy-done.130) | copy-start | bytes 3076
  927.4 279.5 %reduce-scatter.20.cloned.1.call-start = ((), (), s32[]{:S(2)}) async-start(), calls=%async_computation.35 | async-start | bytes 2621440 | tf_op jit(solution)/shard_map/reduce_scatter | solution.py:412
  1031.0 8.7 all-to-all-start.8
  1034.5 13.9 copy-start.104
  1039.8 8.6 all-to-all-start.12
  1049.8 12.4 copy-start.53
  1049.8 8.9 all-to-all-start.15
  1058.7 8.6 all-to-all-start.11
  1062.2 144.8 %reduce-scatter.18.cloned.1.call-start = ((), (), s32[]{:S(2)}) async-start(), calls=%async_computation.34 | async-start | bytes 2621440 | tf_op jit(solution)/shard_map/reduce_scatter | solution.py:403
  1076.9 8.6 all-to-all-start.10
  1082.6 15.1 copy-start.55
  1085.6 12.1 copy-start.89
  1085.6 8.6 all-to-all-start.9
  1094.2 8.6 all-to-all-start.13
  1098.1 13.3 copy-start.81
  1102.8 8.6 all-to-all-start.14
  1106.2 100.7 %reduce-scatter.16.cloned.1.call-start = ((), (), s32[]{:S(2)}) async-start(), calls=%async_computation.33 | async-start | bytes 2621440 | tf_op jit(solution)/shard_map/reduce_scatter | solution.py:400
  1127.3 89.5 %reduce-scatter.14.cloned.1.call-start = ((), (), s32[]{:S(2)}) async-start(), calls=%async_computation.32 | async-start | bytes 2621440 | tf_op jit(solution)/shard_map/reduce_scatter | solution.py:397
  1133.0 229.9 %reduce-scatter.24.cloned.1.call-start = ((), (), s32[]{:S(2)}) async-start(), calls=%async_computation.37 | async-start | bytes 10485760 | tf_op jit(solution)/shard_map/reduce_scatter | solution.py:409
  1154.4 356.0 %reduce-scatter.22.cloned.1.call-start = ((), (), s32[]{:S(2)}) async-start(), calls=%async_computation.36 | async-start | bytes 10485760 | tf_op jit(solution)/shard_map/reduce_scatter | solution.py:406
  1175.5 482.6 %reduce-scatter.26.cloned.1.call-start = ((), (), s32[]{:S(2)}) async-start(), calls=%async_computation.38 | async-start | bytes 10485760 | tf_op jit(solution)/shard_map/reduce_scatter | solution.py:415
  1196.8 483.7 %reduce-scatter.28.cloned.1.call-start = ((), (), s32[]{:S(2)}) async-start(), calls=%async_computation.39 | async-start | bytes 40960
  1197.6 502.2 %reduce-scatter.30.cloned.1.call-start = ((), (), s32[]{:S(2)}) async-start(), calls=%async_computation.40 | async-start | bytes 40960
  1198.4 554.1 %all-reduce.23.cloned.1.call-start = ((), (), s32[]{:S(2)}) async-start(), calls=%async_computation.44 | async-start | bytes 4194304 | tf_op jit(solution)/shard_map/psum | solution.py:352
  1206.9 750.0 %all-reduce.25.cloned.1.call-start = ((), (), s32[]{:S(2)}) async-start(), calls=%async_computation.45 | async-start | bytes 16777216 | tf_op jit(solution)/shard_map/psum | solution.py:444
  1658.1 13.4 copy-start.44
  1671.5 81.1 %copy-start.3 = (bf16[2,1,256,2048]{3,2,1,0:T(8,128)(2,1)S(1)}, bf16[2,1,256,2048]{3,2,1,0:T(8,128)(2,1)}, u32[]{:S(2)}) copy-start(bf16[2,1,256,2048]{3,2,1,0:T(8,128)(2,1)} %param.15) | copy-start | bytes 6291460
  (132 other events, 506.9 us)
Sparse Core Ops, SparseCore 0:
  9.6 48.6 all-gather.11
  59.9 44.6 all-gather.15
  106.2 44.6 all-gather.13
  152.3 44.6 all-gather.17
  258.5 82.4 all-reduce.20
  342.5 149.7 all-gather.19
  494.0 147.8 all-gather.21
  643.5 147.8 all-gather.23
  802.9 83.8 all-reduce.18
  927.5 85.7 all-reduce.16
  1027.7 43.9 reduce-scatter.19
  1074.5 43.2 reduce-scatter.17
  1127.4 43.3 reduce-scatter.15
  1173.5 43.1 reduce-scatter.13
  1219.1 143.7 reduce-scatter.23
  1365.3 145.1 reduce-scatter.21
  1512.8 145.1 reduce-scatter.25
  1660.8 19.6 reduce-scatter.27
  1682.7 17.0 reduce-scatter.29
  1702.8 49.6 all-reduce.22
  1755.6 201.2 all-reduce.24
where the time goes:
time: 1980 us
  waiting for transfers between devices  1520 us (77%)
  matrix products  179 us (9%)
  blocking collectives  73.9 us (4%)
  other arithmetic  73.8 us (4%)
  starting transfers between devices  68.6 us (3%)
  local copies, waits for them, and re-layouts  46.1 us (2%)
    psum x1, waiting for transfers between devices, local(): lax.psum(part_query.astype(jnp.bfloat16), 'ctx').astype(jnp.float32)  198 us
    reduce_scatter x1, waiting for transfers between devices, local(): lax.psum_scatter(grad_gate.astype(jnp.bfloat16), 'fsdp', scatter_dimensio...  148 us
    reduce_scatter x1, waiting for transfers between devices, local(): lax.psum_scatter(grad_down.astype(jnp.bfloat16), 'fsdp', scatter_dimensio...  148 us
    reduce_scatter x1, waiting for transfers between devices, local(): lax.psum_scatter(grad_up.astype(jnp.bfloat16), 'fsdp', scatter_dimension=...  146 us
    all_gather x1, waiting for transfers between devices, fetch_forward(): lax.all_gather(w_gate, 'fsdp', axis=0, tiled=True)  144 us
    all_gather x1, waiting for transfers between devices, fetch_forward(): lax.all_gather(w_up, 'fsdp', axis=0, tiled=True)  138 us
    all_gather x1, waiting for transfers between devices, fetch_forward(): lax.all_gather(w_down, 'fsdp', axis=1, tiled=True)  137 us
    psum x1, waiting for transfers between devices, local(): lax.psum(product_back(gate_low, gate_full) + product_back(up_low, up_full...  85.9 us
  transfers between devices with their start and end apart: 37, of which 32 were waited for; matrix products, arithmetic and copies ran while one was open for 10% of the time, Pallas kernels for 0%

commit v1 on v0

v1 whole, which is shorter than its diff:
```python
import math

import jax
import jax.numpy as jnp
from jax import lax
from jax.sharding import PartitionSpec as P

D = 2048
HD = 128
EPSILON = 1e-06
ROTARY_BASE = 500000.0
MASKED = -1e30
GAIN_ROWS = 16
LOW = jnp.bfloat16
WIDE = jnp.float32


def product(left_side, right_side):
    return jnp.dot(left_side, right_side, preferred_element_type=WIDE)


def product_back(left_side, right_side):
    return lax.dot_general(
        left_side, right_side, (((1,), (1,)), ((), ())), preferred_element_type=WIDE
    )


def product_left(left_side, right_side):
    return lax.dot_general(
        left_side, right_side, (((0,), (0,)), ((), ())), preferred_element_type=WIDE
    )


def doc_positions(segment_row):
    earlier = (segment_row[None, :] < segment_row[:, None]).astype(jnp.int32)
    return jnp.arange(segment_row.shape[0], dtype=jnp.int32) - jnp.sum(earlier, axis=1)


def rotary_tables(positions):
    half_size = HD // 2
    frequency = ROTARY_BASE ** (-(jnp.arange(half_size, dtype=WIDE) * 2.0 / HD))
    angle_table = positions.astype(WIDE)[:, None] * frequency[None, :]
    return (jnp.cos(angle_table)[:, None, :], jnp.sin(angle_table)[:, None, :])


def rotate(values, cosine, sine_table):
    half_size = values.shape[-1] // 2
    first_half = values[..., :half_size]
    second_half = values[..., half_size:]
    return jnp.concatenate(
        [
            first_half * cosine - second_half * sine_table,
            second_half * cosine + first_half * sine_table,
        ],
        axis=-1,
    )


def attention_mask(segment_row):
    places = jnp.arange(segment_row.shape[0])
    return (segment_row[:, None] == segment_row[None, :]) & (places[None, :] <= places[:, None])


def head_scores(query_heads, key_heads, allowed):
    raw_scores = jnp.einsum(
        "qhd,khd->hqk", query_heads, key_heads, preferred_element_type=WIDE
    ) * (1.0 / math.sqrt(HD))
    return jnp.where(allowed[None], raw_scores, MASKED)


def flip(value, axis, bit, size):
    return lax.ppermute(value, axis, [(place, place ^ bit) for place in range(size)])


def after(value, *earlier):
    return lax.optimization_barrier((value,) + earlier)[0]


def solution(mesh):
    fsdp = mesh.shape["fsdp"]
    ctx = mesh.shape["ctx"]
    tp = mesh.shape["tp"]

    def shift(value, step):
        return lax.ppermute(
            value, "fsdp", [(place, (place - step) % fsdp) for place in range(fsdp)]
        )

    def swap(value):
        return flip(value, "ctx", 1, ctx)

    def tp_gather(block):
        second = flip(block, "tp", 2, tp)
        pair = jnp.concatenate([block, second], axis=0)
        return jnp.concatenate([pair, flip(pair, "tp", 1, tp)], axis=0)

    def tp_scatter(make, rows):
        half = rows[0].shape[0] // 2
        sent = make(*(part[half:] for part in rows)).astype(LOW)
        got = flip(sent, "tp", 1, tp)
        kept = make(*(part[:half] for part in rows)) + got.astype(WIDE)
        again = flip(kept[half // 2 :].astype(LOW), "tp", 2, tp)
        return kept[: half // 2] + again.astype(WIDE)

    def local(
        inputs,
        out_grad,
        segments,
        w_query,
        w_key,
        w_value,
        w_out,
        w_gate,
        w_up,
        w_down,
        query_gain,
        key_gain,
        attn_gain,
        mlp_gain,
    ):
        f = lax.axis_index("fsdp")
        c = lax.axis_index("ctx")
        t = lax.axis_index("tp")
        half_len = inputs.shape[2]
        length = half_len * ctx
        part_len = length // tp
        block = D // fsdp
        half_block = block // 2
        heads_here = query_gain.shape[0]
        width = heads_here * HD
        hidden_here = w_gate.shape[1] // fsdp
        scale_factor = 1.0 / math.sqrt(HD)
        first = c == 0

        def pair(own, other, axis):
            return jnp.where(
                first,
                jnp.concatenate([own, other], axis=axis),
                jnp.concatenate([other, own], axis=axis),
            )

        def near_rows(value):
            return jnp.concatenate(
                [
                    lax.dynamic_slice_in_dim(value, (t ^ bit) * part_len, part_len, 0)
                    for bit in (0, 2, 1, 3)
                ],
                axis=0,
            )

        def plain_rows(value, size):
            parts = []
            for place in range(tp):
                far = t ^ place
                spot = (far & 1) * 2 + (far >> 1)
                parts.append(lax.dynamic_slice_in_dim(value, spot * size, size, 0))
            return jnp.concatenate(parts, axis=0)

        def place(r):
            return lax.rem(f + (r % fsdp), fsdp)

        gain_pack = jnp.concatenate(
            [query_gain.reshape(-1), key_gain.reshape(-1), attn_gain, mlp_gain]
        )
        gain_rows = jnp.pad(gain_pack, (0, GAIN_ROWS * 2 * width - gain_pack.size)).reshape(
            GAIN_ROWS, 2 * width
        )

        def half_of(shard, side):
            return lax.dynamic_slice_in_dim(shard, side * half_block, half_block, 0)

        def ring(own, more):
            moving = half_of(own, c)
            if more is not None:
                moving = jnp.concatenate([moving, more], axis=0)
            whole = lax.dynamic_update_slice(
                jnp.zeros((D, own.shape[1]), LOW), own, (f * block, 0)
            )
            moved = [moving]
            for r in range(1, fsdp):
                moved.append(shift(moved[-1], 1))
                got = moved[-1][:half_block]
                begin = place(r) * block
                whole = lax.dynamic_update_slice(whole, got, (begin + c * half_block, 0))
                whole = lax.dynamic_update_slice(
                    whole, swap(got), (begin + (1 - c) * half_block, 0)
                )
            return whole, moved

        qk_full, qk_moved = ring(jnp.concatenate([w_query, w_key], axis=1), gain_rows)
        vo_full, vo_moved = ring(jnp.concatenate([w_value, w_out.T], axis=1), None)
        value_full, out_full = vo_full[:, :width], vo_full[:, width:]

        gain_near = jnp.stack([part[half_block:].reshape(-1) for part in qk_moved]).astype(WIDE)
        gain_all = lax.dynamic_slice_in_dim(
            jnp.concatenate([gain_near, gain_near], axis=0), lax.rem(fsdp - f, fsdp), fsdp, 0
        )
        qk_size = query_gain.size
        query_gain_row = (
            gain_all[:, :qk_size].reshape(fsdp, heads_here, -1).transpose(1, 0, 2).reshape(-1)
        )
        key_gain_row = (
            gain_all[:, qk_size : 2 * qk_size]
            .reshape(fsdp, heads_here, -1)
            .transpose(1, 0, 2)
            .reshape(-1)
        )
        attn_gains = gain_all[:, 2 * qk_size : 2 * qk_size + block].reshape(1, -1)
        mlp_gains = gain_all[:, 2 * qk_size + block : 2 * (qk_size + block)].reshape(1, -1)

        sub_len = half_len // tp
        tokens_kept = lax.dynamic_index_in_dim(inputs[:, 0], c, 0, keepdims=False)
        tokens_sent = lax.dynamic_slice(
            inputs, (1 - c, 0, t * sub_len, 0), (1, 1, sub_len, D)
        )[0, 0]
        tokens_got = plain_rows(tp_gather(swap(tokens_sent)), sub_len)
        tokens = pair(tokens_kept, tokens_got, 0)
        segment_row = lax.dynamic_index_in_dim(segments[:, 0], c, 0, keepdims=False)

        half_hidden = hidden_here // 2

        def fetch_rows(shard):
            mine = half_of(shard, c).reshape(half_block, fsdp, hidden_here).transpose(1, 0, 2)
            mine = lax.all_to_all(mine, "fsdp", 0, 0, tiled=True)
            return pair(mine[:, None], swap(mine)[:, None], 1).reshape(D, hidden_here)

        def fetch_columns(shard):
            mine = shard.reshape(fsdp, 2, half_hidden, block)
            mine = lax.dynamic_index_in_dim(mine, c, 1, keepdims=False)
            mine = lax.all_to_all(mine, "fsdp", 0, 0, tiled=True)
            whole = pair(mine[:, None], swap(mine)[:, None], 1)
            return whole.reshape(fsdp, hidden_here, block).transpose(1, 0, 2).reshape(-1, D)

        gate_late, up_late, down_late = lax.optimization_barrier(
            (w_gate, w_up, w_down, qk_moved[-1])
        )[:3]
        wide_full = jnp.concatenate([fetch_rows(gate_late), fetch_rows(up_late)], axis=1)
        down_full = fetch_columns(down_late)

        allowed = attention_mask(segment_row)
        cosine, sine_table = rotary_tables(doc_positions(segment_row))
        raw = product(tokens, qk_full)
        query_raw = raw[:, :width]
        key_raw = raw[:, width:]
        value_heads = product(tokens, value_full).astype(LOW).reshape(length, heads_here, HD)
        squares = lax.psum(
            jnp.stack([jnp.sum(query_raw * query_raw, axis=1), jnp.sum(key_raw * key_raw, axis=1)]),
            "tp",
        )
        query_scale = lax.rsqrt(squares[0] / D + EPSILON)[:, None]
        key_scale = lax.rsqrt(squares[1] / D + EPSILON)[:, None]
        query_heads = rotate(
            (query_raw * query_scale * query_gain_row).reshape(length, heads_here, HD),
            cosine,
            sine_table,
        ).astype(LOW)
        key_heads = rotate(
            (key_raw * key_scale * key_gain_row).reshape(length, heads_here, HD),
            cosine,
            sine_table,
        ).astype(LOW)
        scores = head_scores(query_heads, key_heads, allowed)
        top_score = jnp.max(scores, axis=-1, keepdims=True)
        log_total = top_score + jnp.log(
            jnp.sum(jnp.exp(scores - top_score), axis=-1, keepdims=True)
        )
        probs_low = jnp.exp(scores - log_total).astype(LOW)
        attended = (
            jnp.einsum("hqk,khd->qhd", probs_low, value_heads, preferred_element_type=WIDE)
            .astype(LOW)
            .reshape(length, width)
        )
        attended_near = near_rows(attended)
        branch = tp_scatter(lambda rows: product_back(rows, out_full), (attended_near,))

        tokens_part = lax.dynamic_slice_in_dim(tokens, t * part_len, part_len, 0).astype(WIDE)
        branch_scale = lax.rsqrt(jnp.mean(branch * branch, axis=-1, keepdims=True) + EPSILON)
        hidden = tokens_part + branch * branch_scale * attn_gains
        hidden_low = hidden.astype(LOW)

        group_size = min(fsdp, 4)

        def all_chunks(part):
            moved = [part]
            for _ in range(1, fsdp):
                moved.append(shift(moved[-1], 1))
            groups = []
            for g in range(0, fsdp, group_size):
                group = jnp.zeros((group_size * length, D), LOW)
                for r in range(group_size):
                    second = flip(moved[g + r], "tp", 2, tp)
                    both = jnp.concatenate([moved[g + r], second], axis=0)
                    third = flip(both, "tp", 1, tp)
                    group = lax.dynamic_update_slice(group, both, (r * length, 0))
                    group = lax.dynamic_update_slice(
                        group, third, (r * length + length // 2, 0)
                    )
                groups.append(group)
            return groups, [
                group[r * length : (r + 1) * length] for group in groups for r in range(group_size)
            ]

        def all_tokens(left_groups, right_groups):
            total = product_left(left_groups[0], right_groups[0])
            for left_side, right_side in zip(left_groups[1:], right_groups[1:]):
                total = total + product_left(left_side, right_side)
            return total.astype(LOW)

        def grouped(chunks):
            return [
                jnp.concatenate(chunks[g : g + group_size], axis=0)
                for g in range(0, fsdp, group_size)
            ]

        def to_owner(parts):
            total = parts[0]
            for r in range(1, fsdp):
                total = total + shift(parts[r].astype(LOW), -r).astype(WIDE)
            return total

        hidden_all, hidden_chunks = all_chunks(hidden_low)
        wide_chunks, active_chunks, down_parts = [], [], []
        for chunk in hidden_chunks:
            wide = product(chunk, wide_full)
            gate_value, up_value = wide[:, :hidden_here], wide[:, hidden_here:]
            active = (gate_value * jax.nn.sigmoid(gate_value) * up_value).astype(LOW)
            down_parts.append(tp_scatter(lambda rows: product(rows, down_full), (active,)))
            wide_chunks.append(wide)
            active_chunks.append(active)
        down = to_owner(down_parts)

        down_scale = lax.rsqrt(jnp.mean(down * down, axis=-1, keepdims=True) + EPSILON)
        output_part = (hidden + down * down_scale * mlp_gains).astype(LOW)

        inner = lax.rem(t, tp // 2) * part_len
        grad_kept = lax.dynamic_slice(
            out_grad, (c, 0, inner, 0), (1, 1, part_len, D)
        )[0, 0]
        grad_sent = lax.dynamic_slice(
            out_grad, (1 - c, 0, inner, 0), (1, 1, part_len, D)
        )[0, 0]
        mine_here = t // (tp // 2) == c
        cotangent = jnp.where(
            mine_here, grad_kept, swap(after(grad_sent, qk_moved[-1]))
        ).astype(WIDE)

        scaled = cotangent * mlp_gains
        down_mean = jnp.mean(scaled * down, axis=-1, keepdims=True)
        down_low = (down_scale * (scaled - down * (down_scale * down_scale * down_mean))).astype(
            LOW
        )
        mlp_gain_grad = jnp.sum(cotangent * down * down_scale, axis=0)

        grad_all, grad_chunks = all_chunks(down_low)
        wide_lows, hidden_parts = [], []
        for chunk, wide in zip(grad_chunks, wide_chunks):
            gate_value, up_value = wide[:, :hidden_here], wide[:, hidden_here:]
            act_grad = product_back(chunk, down_full)
            sig = jax.nn.sigmoid(gate_value)
            gate_low = (act_grad * up_value * sig * (1.0 + gate_value * (1.0 - sig))).astype(LOW)
            up_low = (act_grad * gate_value * sig).astype(LOW)
            wide_low = jnp.concatenate([gate_low, up_low], axis=1)
            hidden_parts.append(
                tp_scatter(lambda rows: product_back(rows, wide_full), (wide_low,))
            )
            wide_lows.append(wide_low)
        hidden_grad = cotangent + to_owner(hidden_parts)

        def half_sum(split, earlier):
            sent = lax.dynamic_index_in_dim(split, 1 - c, 1, keepdims=False)
            kept = lax.dynamic_index_in_dim(split, c, 1, keepdims=False)
            got = swap(sent if earlier is None else after(sent, earlier))
            return (kept.astype(WIDE) + got.astype(WIDE)).astype(LOW)

        down_grads = all_tokens(grouped(active_chunks), grad_all)
        down_split = down_grads.reshape(2, half_hidden, fsdp, block).transpose(2, 0, 1, 3)
        down_sum = half_sum(down_split, None)
        wide_grads = all_tokens(hidden_all, grouped(wide_lows))
        wide_split = wide_grads.reshape(fsdp, 2, half_block, 2 * hidden_here)
        gate_sum = half_sum(wide_split[..., :hidden_here], down_sum)
        up_sum = half_sum(wide_split[..., hidden_here:], gate_sum)

        def both_sides(summed):
            mine = lax.all_to_all(after(summed, hidden_grad), "fsdp", 0, 0, tiled=True)
            return lax.all_gather(mine, "ctx", axis=0)

        grad_down = both_sides(down_sum).transpose(1, 0, 2, 3).reshape(-1, block).astype(WIDE)
        grad_gate = both_sides(gate_sum).transpose(0, 2, 1, 3).reshape(block, -1).astype(WIDE)
        grad_up = both_sides(up_sum).transpose(0, 2, 1, 3).reshape(block, -1).astype(WIDE)

        lifted = hidden_grad * attn_gains
        branch_mean = jnp.mean(lifted * branch, axis=-1, keepdims=True)
        branch_low = (
            branch_scale * (lifted - branch * (branch_scale * branch_scale * branch_mean))
        ).astype(LOW)
        attn_gain_grad = jnp.sum(hidden_grad * branch * branch_scale, axis=0)
        branch_near = tp_gather(branch_low)
        heads_grad = plain_rows(
            product(branch_near, out_full).astype(LOW), part_len
        ).reshape(length, heads_here, HD)
        attn_probs = jnp.exp(head_scores(query_heads, key_heads, allowed) - log_total)
        value_grad = (
            jnp.einsum(
                "hqk,qhd->khd", attn_probs.astype(LOW), heads_grad, preferred_element_type=WIDE
            )
            .astype(LOW)
            .reshape(length, width)
        )
        probs_grad = jnp.einsum(
            "qhd,khd->hqk", heads_grad, value_heads, preferred_element_type=WIDE
        )
        score_grad = (
            attn_probs * (probs_grad - jnp.sum(attn_probs * probs_grad, axis=-1, keepdims=True))
        ).astype(LOW)
        query_grad = (
            jnp.einsum("hqk,khd->qhd", score_grad, key_heads, preferred_element_type=WIDE)
            * scale_factor
        )
        key_grad = (
            jnp.einsum("hqk,qhd->khd", score_grad, query_heads, preferred_element_type=WIDE)
            * scale_factor
        )
        query_norm_grad = rotate(query_grad, cosine, -sine_table).reshape(length, width)
        key_norm_grad = rotate(key_grad, cosine, -sine_table).reshape(length, width)
        query_term = query_norm_grad * query_gain_row
        key_term = key_norm_grad * key_gain_row
        dots = lax.psum(
            jnp.stack(
                [jnp.sum(query_term * query_raw, axis=1), jnp.sum(key_term * key_raw, axis=1)]
            ),
            "tp",
        )
        query_cube = query_scale * query_scale * query_scale
        key_cube = key_scale * key_scale * key_scale
        query_raw_grad = (
            query_scale * query_term - query_raw * (query_cube * dots[0][:, None] / D)
        ).astype(LOW)
        key_raw_grad = (
            key_scale * key_term - key_raw * (key_cube * dots[1][:, None] / D)
        ).astype(LOW)
        query_gain_grad = jnp.sum(query_norm_grad * query_raw * query_scale, axis=0)
        key_gain_grad = jnp.sum(key_norm_grad * key_raw * key_scale, axis=0)
        qk_grad = jnp.concatenate([query_raw_grad, key_raw_grad], axis=1)

        def gathered(partial, dim):
            mine = lax.psum_scatter(partial, "fsdp", scatter_dimension=dim, tiled=True)
            return lax.psum(mine, "ctx").astype(WIDE)

        grad_out = gathered(product_left(attended_near, branch_near).astype(LOW), 1)
        grad_value = gathered(product_left(tokens, value_grad).astype(LOW), 0)

        def row_shard(grads):
            summed = half_sum(grads.astype(LOW).reshape(fsdp, 2, half_block, width), None)
            parts = lax.all_to_all(summed, "fsdp", 0, 0, tiled=True)
            mine = jnp.sum(parts.astype(WIDE), axis=0).astype(LOW)
            mine = lax.optimization_barrier(mine)
            return pair(mine, swap(mine), 0).astype(WIDE)

        grad_query = row_shard(product_left(tokens, query_raw_grad))
        grad_key = row_shard(product_left(tokens, key_raw_grad))

        input_part = hidden_grad + tp_scatter(
            lambda rows, more: product_back(rows, qk_full) + product_back(more, value_full),
            (near_rows(qk_grad), near_rows(value_grad)),
        )

        def spread(part):
            part = lax.optimization_barrier(part.astype(LOW))
            pairs = []
            for low_place in range(tp // 2):
                here, there = tp // 2 + low_place, tp + low_place
                pairs += [(here, there), (there, here)]
            got = lax.ppermute(part, ("ctx", "tp"), pairs)
            near = jnp.where(mine_here, part, got)
            far = flip(near, "tp", 2, tp)
            mine = jnp.where(mine_here, near, far)
            other = jnp.where(mine_here, far, near)
            both = jnp.where(
                first, jnp.stack([mine, other]), jnp.stack([other, mine])
            )
            beside = flip(both, "tp", 1, tp)
            return jnp.where(
                t % 2 == 0,
                jnp.concatenate([both, beside], axis=1),
                jnp.concatenate([beside, both], axis=1),
            )[:, None]

        layer_out = spread(after(output_part, hidden_grad))
        layer_in_grad = spread(input_part).astype(WIDE)

        rows_grad = jnp.stack([attn_gain_grad, mlp_gain_grad])
        for bit in (1, 2):
            rows_grad = rows_grad + flip(rows_grad, "tp", bit, tp)
        packed = jnp.concatenate(
            [
                rows_grad.reshape(2, fsdp, block).transpose(1, 0, 2).reshape(fsdp, 2 * block),
                jnp.stack([query_gain_grad, key_gain_grad])
                .reshape(2 * heads_here, fsdp, HD // fsdp)
                .transpose(1, 0, 2)
                .reshape(fsdp, -1),
            ],
            axis=1,
        )
        packed = packed + swap(packed)
        own_gains = lax.dynamic_index_in_dim(packed, f, 0, keepdims=False)
        for r in range(1, fsdp):
            own_gains = own_gains + shift(
                lax.dynamic_index_in_dim(packed, place(r), 0, keepdims=False), -r
            )
        sum_heads = own_gains[2 * block :].reshape(2, heads_here, HD // fsdp)
        return (
            layer_out,
            layer_in_grad,
            grad_query,
            grad_key,
            grad_value,
            grad_out,
            grad_gate,
            grad_up,
            grad_down,
            sum_heads[0],
            sum_heads[1],
            own_gains[:block],
            own_gains[block : 2 * block],
        )

    rows = P("fsdp", "tp")
    columns = P("tp", "fsdp")
    whole_tokens = P(None, "fsdp", "ctx", None)
    return jax.shard_map(
        local,
        mesh=mesh,
        in_specs=(
            whole_tokens,
            whole_tokens,
            P(None, "fsdp", None),
            rows,
            rows,
            rows,
            columns,
            rows,
            rows,
            columns,
            columns,
            columns,
            P("fsdp"),
            P("fsdp"),
        ),
        out_specs=(
            whole_tokens,
            whole_tokens,
            rows,
            rows,
            rows,
            columns,
            rows,
            rows,
            columns,
            columns,
            columns,
            P("fsdp"),
            P("fsdp"),
        ),
        check_vma=False,
    )
```

time: 1980 us -> 913 us (0.46)
  waiting for transfers between devices: 1520 us -> 306 us
  local copies, waits for them, and re-layouts: 46.1 us -> 174 us
  starting transfers between devices: 68.6 us -> 176 us
  blocking collectives: 73.9 us -> 13.6 us
  matrix products: 179 us -> 120 us
  other arithmetic: 73.8 us -> 96.4 us
    all_gather x7 -> x3, waiting for transfers between devices: 524 us -> 0.02 us  [both_sides(): return lax.all_gather(mine, 'ctx', axis=0)]
    reduce_scatter x7 -> x2, waiting for transfers between devices: 451 us -> 0.01 us  [gathered(): mine = lax.psum_scatter(partial, 'fsdp', scatter_dimension=dim, tiled=True)]
    psum x5 -> x1, waiting for transfers between devices: 469 us -> 18.4 us  [gathered(): return lax.psum(mine, 'ctx').astype(WIDE)]
    ppermute x0 -> x88, waiting for transfers between devices: none -> 227 us  [the longest x65 162 us: flip(): lax.ppermute(value, axis, [(place, place ^ bit) for place in range(size)])]
    ppermute x0 -> x88, starting transfers between devices: none -> 143 us  [the longest x65 87 us: flip(): lax.ppermute(value, axis, [(place, place ^ bit) for place in range(size)])]
    all_gather x4 -> x0, blocking collectives: 44.1 us -> none  [the longest x1 12.6 us: fetch_forward(): lax.all_gather(query_gain, 'fsdp', axis=1, tiled=True)]
    dot_general x14 -> x6, matrix products: 72 us -> 28.8 us  [product_left(): lax.dot_general(left_side, right_side, (((0,), (0,)), ((), ())), preferre...]
    dynamic_update_slice x0 -> x29, local copies, waits for them, and re-layouts: none -> 34.5 us  [the longest x8 10.2 us: all_chunks(): group = lax.dynamic_update_slice(group, both, (r * length, 0))]
  transfers between devices with their start and end apart: 37 -> 102, of which waited for: 32 -> 34; matrix products, arithmetic and copies ran while one was open for 10% -> 37% of each run, Pallas kernels for 0% -> 0%
where the time goes in v1:
time: 913 us; the launch traced here: 905 us
  waiting for transfers between devices  306 us (34%)
  starting transfers between devices  176 us (19%)
  local copies, waits for them, and re-layouts  174 us (19%)
  matrix products  120 us (13%)
  other arithmetic  96.4 us (11%)
  between operations  18 us (2%)
  blocking collectives  13.6 us (1%)
    ppermute x65, waiting for transfers between devices, flip(): lax.ppermute(value, axis, [(place, place ^ bit) for place in range(size)])  162 us
    ppermute x65, starting transfers between devices, flip(): lax.ppermute(value, axis, [(place, place ^ bit) for place in range(size)])  87 us
    ppermute x21, waiting for transfers between devices, shift(): lax.ppermute(value, 'fsdp', [(place, (place - step) % fsdp) for place in...  65.7 us
    ppermute x21, starting transfers between devices, shift(): lax.ppermute(value, 'fsdp', [(place, (place - step) % fsdp) for place in...  53.3 us
    dot_general x18, matrix products, product_back(): lax.dot_general(left_side, right_side, (((1,), (1,)), ((), ())), preferre...  49.7 us
    unnamed x294, local copies, waits for them, and re-layouts  39 us
    dot_general x15, matrix products, product(): return jnp.dot(left_side, right_side, preferred_element_type=WIDE)  29.6 us
    dot_general x6, matrix products, product_left(): lax.dot_general(left_side, right_side, (((0,), (0,)), ((), ())), preferre...  28.8 us
  transfers between devices with their start and end apart: 102, of which 34 were waited for; matrix products, arithmetic and copies ran while one was open for 37% of the time, Pallas kernels for 0%

profile of v1, /device:TPU:0, one launch (start us, length us, event | category | flops | bytes accessed | tf_op | source)
XLA Modules:
  0.0 904.7 jit_solution(6961073358568220267)
XLA Ops:
  11.3 5.0 collective-permute-start.3
  85.6 4.7 collective-permute-done.12
  100.2 3.9 copy.173
  106.4 4.2 all-to-all-start
  110.6 3.9 copy.175
  117.3 3.7 fusion.64
  123.0 5.2 fusion.230
  129.9 6.5 psum.28
  157.1 4.8 all-to-all-start.1
  171.4 17.0 %all-to-all-done.1 = bf16[4,256,512]{1,2,0:T(8,128)(2,1)S(1)} async-done(((bf16[4,256,512]{1,2,0:T(8,128)(2,1)}), bf16[4,256,512]{1,2,0:T(8,128)(2,1)S(1)}, u32[]{:S(2)}, u32[]{:S(2)}) %all-to-all-start.1) | async-done | bytes 1048608 | tf_op jit(solution)/shard_map/all_to_all | solution.py:224
  200.1 3.8 collective-permute-start.19
  203.9 14.6 %all-to-all-done.2 = bf16[4,256,512]{1,2,0:T(8,128)(2,1)S(1)} async-done(((bf16[4,256,512]{1,2,0:T(8,128)(2,1)}), bf16[4,256,512]{1,2,0:T(8,128)(2,1)S(1)}, u32[]{:S(2)}, u32[]{:S(2)}) %all-to-all-start.2) | async-done | bytes 1048608 | tf_op jit(solution)/shard_map/all_to_all | solution.py:230
  222.2 11.6 %collective-permute-start.22 = (bf16[128,2048]{1,0:T(8,128)(2,1)}, bf16[128,2048]{1,0:T(8,128)(2,1)}, u32[]{:S(2)}, u32[]{:S(2)}) collective-permute-start(bf16[128,2048]{1,0:T(8,128)(2,1)} %collective-permute-done.19), channel_id=1, source_target_pairs={{0,24},{8,0},{16,8},{24,16},{1,25},{9,1},{17,9},{25,17},{2,26},{10... | collective-permute-start | bytes 1572872 | tf_op jit(solution)/shard_map/ppermute | solution.py:85
  235.7 5.6 dynamic_update_slice.104
  242.6 5.1 maximum_select_fusion
  251.8 10.4 %collective-permute-done.30 = bf16[4,256,512]{1,2,0:T(8,128)(2,1)S(1)} collective-permute-done((bf16[4,256,512]{1,2,0:T(8,128)(2,1)S(1)}, bf16[4,256,512]{1,2,0:T(8,128)(2,1)S(1)}, u32[]{:S(2)}, u32[]{:S(2)}) %collective-permute-start.30) | collective-permute-done | bytes 1048608 | tf_op jit(solution)/shard_map/ppermute | solution.py:72
  262.6 4.2 copy.176
  266.8 4.1 copy.174
  273.2 11.6 %copy.179 = bf16[512,4,512]{0,2,1:T(8,128)(2,1)S(1)} copy(bf16[512,4,512]{2,0,1:T(8,128)(2,1)} %bitcast.240) | data formatting | bytes 4194304 | tf_op jit(solution)/shard_map/transpose | solution.py:232
  293.3 8.4 collective-permute-done.26
  309.2 4.1 fusion.31
  334.6 6.9 collective-permute-done.40
  345.9 6.8 collective-permute-done.37
  356.3 7.7 collective-permute-done.34
  369.1 5.7 collective-permute-done.32
  374.8 15.9 %collective-permute-done.38 = bf16[128,2048]{1,0:T(8,128)(2,1)} collective-permute-done((bf16[128,2048]{1,0:T(8,128)(2,1)}, bf16[128,2048]{1,0:T(8,128)(2,1)}, u32[]{:S(2)}, u32[]{:S(2)}) %collective-permute-start.38) | collective-permute-done | bytes 524320 | tf_op jit(solution)/shard_map/ppermute | solution.py:85
  398.5 9.9 %collective-permute-done.45 = bf16[128,2048]{1,0:T(8,128)(2,1)S(1)} collective-permute-done((bf16[128,2048]{1,0:T(8,128)(2,1)S(1)}, bf16[128,2048]{1,0:T(8,128)(2,1)S(1)}, u32[]{:S(2)}, u32[]{:S(2)}) %collective-permute-start.45) | collective-permute-done | bytes 524320 | tf_op jit(solution)/shard_map/ppermute | solution.py:85
  413.0 9.4 %collective-permute-done.48 = bf16[128,2048]{1,0:T(8,128)(2,1)S(1)} collective-permute-done((bf16[128,2048]{1,0:T(8,128)(2,1)S(1)}, bf16[128,2048]{1,0:T(8,128)(2,1)S(1)}, u32[]{:S(2)}, u32[]{:S(2)}) %collective-permute-start.48) | collective-permute-done | bytes 524320 | tf_op jit(solution)/shard_map/ppermute | solution.py:85
  428.5 6.7 collective-permute-done.51
  436.6 4.4 collective-permute-done.49
  441.1 8.5 collective-permute-done.52
  461.2 6.2 convolution_convert_fusion
  472.4 13.3 %fusion.16 = bf16[2048,1024]{1,0:T(8,128)(2,1)} fusion(bf16[2048,2048]{1,0:T(8,128)(2,1)S(1)} %bitcast.239, bf16[512,512]{1,0:T(8,128)(2,1)} %copy-done.128, bf16[512,512]{1,0:T(8,128)(2,1)} %copy-done.126, bf16[512,512]{1,0:T(8,128)(2,1)} %copy-done.124, bf16[512,512]{1,0:T(8,128)(2,1)} %copy-done.122, bf16[512,512]{1,0:T(8,128)(2,1)} %get-tuple-element.114, ...), kind=kOutput, calls=%fused_computation.25 | convolution fusion | flops 8625586176 | bytes 16777216 | tf_op jit(solution)/shard_map/dot_general | solution.py:29
  495.8 3.8 fusion.223
  517.6 8.2 collective-permute-done.79
  532.1 10.5 %collective-permute-done.57 = bf16[128,2048]{1,0:T(8,128)(2,1)S(1)} collective-permute-done((bf16[128,2048]{1,0:T(8,128)(2,1)S(1)}, bf16[128,2048]{1,0:T(8,128)(2,1)S(1)}, u32[]{:S(2)}, u32[]{:S(2)}) %collective-permute-start.57) | collective-permute-done | bytes 524320 | tf_op jit(solution)/shard_map/ppermute | solution.py:72
  542.8 8.6 collective-permute-done.80
  553.1 21.3 %collective-permute-done.61 = bf16[128,2048]{1,0:T(8,128)(2,1)S(1)} collective-permute-done((bf16[128,2048]{1,0:T(8,128)(2,1)S(1)}, bf16[128,2048]{1,0:T(8,128)(2,1)S(1)}, u32[]{:S(2)}, u32[]{:S(2)}) %collective-permute-start.61) | collective-permute-done | bytes 524320 | tf_op jit(solution)/shard_map/ppermute | solution.py:85
  575.1 4.2 all-to-all-start.5
  579.6 26.2 %all-to-all-done.5 = bf16[4,256,512]{2,1,0:T(8,128)(2,1)} async-done(((bf16[4,256,512]{2,1,0:T(8,128)(2,1)}), bf16[4,256,512]{2,1,0:T(8,128)(2,1)}, u32[]{:S(2)}, u32[]{:S(2)}) %all-to-all-start.5) | async-done | bytes 1048608 | tf_op jit(solution)/shard_map/all_to_all | solution.py:384
  621.9 18.5 %collective-permute-start.66 = (bf16[128,2048]{1,0:T(8,128)(2,1)}, bf16[128,2048]{1,0:T(8,128)(2,1)}, u32[]{:S(2)}, u32[]{:S(2)}) collective-permute-start(bf16[128,2048]{1,0:T(8,128)(2,1)} %broadcast_select_fusion.2), channel_id=1, source_target_pairs={{0,2},{1,3},{2,0},{3,1},{4,6},{5,7},{6,4},{7,5},{8,10},{9,11},{10,... | collective-permute-start | bytes 1572872 | tf_op jit(solution)/shard_map/ppermute | solution.py:72
  642.7 27.3 %collective-permute-done.81 = bf16[4,256,512]{2,1,0:T(8,128)(2,1)} collective-permute-done((bf16[4,256,512]{2,1,0:T(8,128)(2,1)}, bf16[4,256,512]{2,1,0:T(8,128)(2,1)}, u32[]{:S(2)}, u32[]{:S(2)}) %collective-permute-start.81) | collective-permute-done | bytes 1048608 | tf_op jit(solution)/shard_map/ppermute | solution.py:72
  672.5 4.2 all-to-all-start.6
  685.9 3.9 convolution_convert_fusion.14
  694.3 3.9 multiply_reduce_fusion
  705.7 7.1 psum.29
  721.5 4.2 convolution_convert_fusion.1
  725.7 4.8 fusion.127
  730.5 4.1 fusion.21
  744.8 3.6 fusion.123
  749.7 13.7 %collective-permute-done.84 = f32[4,1280]{1,0:T(4,128)S(1)} collective-permute-done((f32[4,1280]{1,0:T(4,128)S(1)}, f32[4,1280]{1,0:T(4,128)S(1)}, u32[]{:S(2)}, u32[]{:S(2)}) %collective-permute-start.84) | collective-permute-done | bytes 20512 | tf_op jit(solution)/shard_map/ppermute | solution.py:72
  763.5 3.8 collective-permute-start.87
  777.2 3.9 all-to-all-start.3
  781.1 3.9 collective-permute-done.71
  789.2 11.2 %collective-permute-done.77 = bf16[4,256,512]{2,1,0:T(8,128)(2,1)} collective-permute-done((bf16[4,256,512]{2,1,0:T(8,128)(2,1)}, bf16[4,256,512]{2,1,0:T(8,128)(2,1)}, u32[]{:S(2)}, u32[]{:S(2)}) %collective-permute-start.77) | collective-permute-done | bytes 1048608 | tf_op jit(solution)/shard_map/ppermute | solution.py:72
  804.2 18.7 %collective-permute-start.73 = (bf16[128,2048]{1,0:T(8,128)(2,1)}, bf16[128,2048]{1,0:T(8,128)(2,1)}, u32[]{:S(2)}, u32[]{:S(2)}) collective-permute-start(bf16[128,2048]{1,0:T(8,128)(2,1)} %broadcast_select_fusion.1), channel_id=1, source_target_pairs={{0,2},{1,3},{2,0},{3,1},{4,6},{5,7},{6,4},{7,5},{8,10},{9,11},{10,... | collective-permute-start | bytes 1572872 | tf_op jit(solution)/shard_map/ppermute | solution.py:72
  822.9 4.7 all-to-all-start.4
  827.8 3.8 fusion.39
  831.6 4.2 convert_bitcast_fusion.2
  844.1 4.0 copy.244
  854.2 6.1 collective-permute-done.78
  866.3 4.0 copy.245
  870.3 4.4 fusion.41
  874.7 18.4 %all-reduce.6.cloned.1.call-done = (bf16[512,512]{1,0:T(8,128)(2,1)}, bf16[512,512]{1,0:T(8,128)(2,1)}) async-done(((bf16[512,512]{1,0:T(8,128)(2,1)}, bf16[512,512]{1,0:T(8,128)(2,1)}), (bf16[512,512]{1,0:T(8,128)(2,1)}, bf16[512,512]{1,0:T(8,128)(2,1)})) %all-reduce.6.cloned.1.call-update) | async-done | bytes 1048592 | tf_op jit(solution)/shard_map/psum | solution.py:447
  (687 shorter events, 373.5 us)
Async XLA Ops:
  11.3 30.3 %collective-permute-start.3 = (bf16[256,1024]{0,1:T(8,128)(2,1)}, bf16[256,1024]{0,1:T(8,128)(2,1)}, u32[]{:S(2)}, u32[]{:S(2)}) collective-permute-start(bf16[256,1024]{0,1:T(8,128)(2,1)} %fusion.118), channel_id=1, source_target_pairs={{0,24},{8,0},{16,8},{24,16},{1,25},{9,1},{17,9},{25,17},{2,26},{10... | collective-permute-start | bytes 1572872 | tf_op jit(solution)/shard_map/ppermute | solution.py:85
  24.3 21.1 %collective-permute-start.9 = (bf16[272,1024]{1,0:T(8,128)(2,1)}, bf16[272,1024]{1,0:T(8,128)(2,1)}, u32[]{:S(2)}, u32[]{:S(2)}) collective-permute-start(bf16[272,1024]{1,0:T(8,128)(2,1)} %pad_maximum_fusion.8), channel_id=1, source_target_pairs={{0,24},{8,0},{16,8},{24,16},{1,25},{9,1},{17,9},{25,17},{2,26},{10... | collective-permute-start | bytes 1671176 | tf_op jit(solution)/shard_map/ppermute | solution.py:85
  57.3 24.5 %collective-permute-start.6 = (bf16[256,1024]{0,1:T(8,128)(2,1)}, bf16[256,1024]{0,1:T(8,128)(2,1)}, u32[]{:S(2)}, u32[]{:S(2)}) collective-permute-start(bf16[256,1024]{0,1:T(8,128)(2,1)} %collective-permute-done.5), channel_id=1, source_target_pairs={{0,4},{4,0},{1,5},{5,1},{2,6},{6,2},{3,7},{7,3},{8,12},{12,8},{9,1... | collective-permute-start | bytes 1572872 | tf_op jit(solution)/shard_map/ppermute | solution.py:72
  58.7 21.7 %collective-permute-start.7 = (bf16[256,1024]{0,1:T(8,128)(2,1)}, bf16[256,1024]{0,1:T(8,128)(2,1)}, u32[]{:S(2)}, u32[]{:S(2)}) collective-permute-start(bf16[256,1024]{0,1:T(8,128)(2,1)} %collective-permute-done.5), channel_id=1, source_target_pairs={{0,24},{8,0},{16,8},{24,16},{1,25},{9,1},{17,9},{25,17},{2,26},{10... | collective-permute-start | bytes 1572872 | tf_op jit(solution)/shard_map/ppermute | solution.py:85
  71.8 20.6 %collective-permute-start.13 = (bf16[272,1024]{1,0:T(8,128)(2,1)}, bf16[272,1024]{1,0:T(8,128)(2,1)}, u32[]{:S(2)}, u32[]{:S(2)}) collective-permute-start(bf16[272,1024]{1,0:T(8,128)(2,1)} %collective-permute-done.11), channel_id=1, source_target_pairs={{0,24},{8,0},{16,8},{24,16},{1,25},{9,1},{17,9},{25,17},{2,26},{10... | collective-permute-start | bytes 1671176 | tf_op jit(solution)/shard_map/ppermute | solution.py:85
  80.4 35.0 %collective-permute-start.8 = (bf16[256,1024]{0,1:T(8,128)(2,1)}, bf16[256,1024]{0,1:T(8,128)(2,1)}, u32[]{:S(2)}, u32[]{:S(2)}) collective-permute-start(bf16[256,1024]{0,1:T(8,128)(2,1)} %collective-permute-done.7), channel_id=1, source_target_pairs={{0,4},{4,0},{1,5},{5,1},{2,6},{6,2},{3,7},{7,3},{8,12},{12,8},{9,1... | collective-permute-start | bytes 1572872 | tf_op jit(solution)/shard_map/ppermute | solution.py:72
  93.7 27.2 %collective-permute-start.14 = (bf16[256,1024]{1,0:T(8,128)(2,1)S(1)}, bf16[256,1024]{1,0:T(8,128)(2,1)}, u32[]{:S(2)}, u32[]{:S(2)}) collective-permute-start(bf16[256,1024]{1,0:T(8,128)(2,1)S(1)} %slice.400), channel_id=1, source_target_pairs={{0,4},{4,0},{1,5},{5,1},{2,6},{6,2},{3,7},{7,3},{8,12},{12,8},{9,1... | collective-permute-start | bytes 1572872 | tf_op jit(solution)/shard_map/ppermute | solution.py:72
  106.4 50.8 %all-to-all-start = ((bf16[4,256,512]{1,2,0:T(8,128)(2,1)}), bf16[4,256,512]{1,2,0:T(8,128)(2,1)}, u32[]{:S(2)}, u32[]{:S(2)}) async-start(bf16[4,256,512]{1,2,0:T(8,128)(2,1)} %bitcast.15), calls=%async_computation | async-start | bytes 2097152 | tf_op jit(solution)/shard_map/all_to_all | solution.py:224
  157.1 31.2 %all-to-all-start.1 = ((bf16[4,256,512]{1,2,0:T(8,128)(2,1)}), bf16[4,256,512]{1,2,0:T(8,128)(2,1)S(1)}, u32[]{:S(2)}, u32[]{:S(2)}) async-start(bf16[4,256,512]{1,2,0:T(8,128)(2,1)} %bitcast.243), calls=%async_computation.1 | async-start | bytes 2097152 | tf_op jit(solution)/shard_map/all_to_all | solution.py:224
  166.7 27.9 %collective-permute-start.16 = (bf16[128,2048]{1,0:T(8,128)(2,1)}, bf16[128,2048]{1,0:T(8,128)(2,1)}, u32[]{:S(2)}, u32[]{:S(2)}) collective-permute-start(bf16[128,2048]{1,0:T(8,128)(2,1)} %slice.689), channel_id=1, source_target_pairs={{0,2},{1,3},{2,0},{3,1},{4,6},{5,7},{6,4},{7,5},{8,10},{9,11},{10,... | collective-permute-start | bytes 1572872 | tf_op jit(solution)/shard_map/ppermute | solution.py:72
  188.3 30.2 %all-to-all-start.2 = ((bf16[4,256,512]{1,2,0:T(8,128)(2,1)}), bf16[4,256,512]{1,2,0:T(8,128)(2,1)S(1)}, u32[]{:S(2)}, u32[]{:S(2)}) async-start(bf16[4,256,512]{1,2,0:T(8,128)(2,1)} %bitcast.25), calls=%async_computation.2 | async-start | bytes 2097152 | tf_op jit(solution)/shard_map/all_to_all | solution.py:230
  192.6 48.7 %collective-permute-start.28 = (bf16[4,256,512]{1,2,0:T(8,128)(2,1)}, bf16[4,256,512]{1,2,0:T(8,128)(2,1)}, u32[]{:S(2)}, u32[]{:S(2)}) collective-permute-start(bf16[4,256,512]{1,2,0:T(8,128)(2,1)} %all-to-all-done), channel_id=1, source_target_pairs={{0,4},{4,0},{1,5},{5,1},{2,6},{6,2},{3,7},{7,3},{8,12},{12,8},{9,1... | collective-permute-start | bytes 3145736 | tf_op jit(solution)/shard_map/ppermute | solution.py:72
  194.0 48.7 %collective-permute-start.29 = (bf16[4,256,512]{1,2,0:T(8,128)(2,1)S(1)}, bf16[4,256,512]{1,2,0:T(8,128)(2,1)}, u32[]{:S(2)}, u32[]{:S(2)}) collective-permute-start(bf16[4,256,512]{1,2,0:T(8,128)(2,1)S(1)} %all-to-all-done.1), channel_id=1, source_target_pairs={{0,4},{4,0},{1,5},{5,1},{2,6},{6,2},{3,7},{7,3},{8,12},{12,8},{9,1... | collective-permute-start | bytes 3145736 | tf_op jit(solution)/shard_map/ppermute | solution.py:72
  198.7 21.1 %collective-permute-start.17 = (bf16[128,2048]{1,0:T(8,128)(2,1)}, bf16[128,2048]{1,0:T(8,128)(2,1)}, u32[]{:S(2)}, u32[]{:S(2)}) collective-permute-start(bf16[128,2048]{1,0:T(8,128)(2,1)} %fusion.97), channel_id=1, source_target_pairs={{0,2},{1,3},{2,0},{3,1},{4,6},{5,7},{6,4},{7,5},{8,10},{9,11},{10,... | collective-permute-start | bytes 1572872 | tf_op jit(solution)/shard_map/ppermute | solution.py:72
  200.1 22.1 %collective-permute-start.19 = (bf16[128,2048]{1,0:T(8,128)(2,1)}, bf16[128,2048]{1,0:T(8,128)(2,1)}, u32[]{:S(2)}, u32[]{:S(2)}) collective-permute-start(bf16[128,2048]{1,0:T(8,128)(2,1)} %fusion.97), channel_id=1, source_target_pairs={{0,24},{8,0},{16,8},{24,16},{1,25},{9,1},{17,9},{25,17},{2,26},{10... | collective-permute-start | bytes 1572872 | tf_op jit(solution)/shard_map/ppermute | solution.py:85
  218.5 43.7 %collective-permute-start.30 = (bf16[4,256,512]{1,2,0:T(8,128)(2,1)S(1)}, bf16[4,256,512]{1,2,0:T(8,128)(2,1)S(1)}, u32[]{:S(2)}, u32[]{:S(2)}) collective-permute-start(bf16[4,256,512]{1,2,0:T(8,128)(2,1)S(1)} %all-to-all-done.2), channel_id=1, source_target_pairs={{0,4},{4,0},{1,5},{5,1},{2,6},{6,2},{3,7},{7,3},{8,12},{12,8},{9,1... | collective-permute-start | bytes 3145736 | tf_op jit(solution)/shard_map/ppermute | solution.py:72
  222.1 68.8 %collective-permute-start.18 = (bf16[256,2048]{1,0:T(8,128)(2,1)}, bf16[256,2048]{1,0:T(8,128)(2,1)}, u32[]{:S(2)}, u32[]{:S(2)}) collective-permute-start(bf16[256,2048]{1,0:T(8,128)(2,1)} %pad_maximum_fusion.3), channel_id=1, source_target_pairs={{0,1},{1,0},{2,3},{3,2},{4,5},{5,4},{6,7},{7,6},{8,9},{9,8},{10,11... | collective-permute-start | bytes 3145736 | tf_op jit(solution)/shard_map/ppermute | solution.py:72
  222.2 25.6 %collective-permute-start.22 = (bf16[128,2048]{1,0:T(8,128)(2,1)}, bf16[128,2048]{1,0:T(8,128)(2,1)}, u32[]{:S(2)}, u32[]{:S(2)}) collective-permute-start(bf16[128,2048]{1,0:T(8,128)(2,1)} %collective-permute-done.19), channel_id=1, source_target_pairs={{0,24},{8,0},{16,8},{24,16},{1,25},{9,1},{17,9},{25,17},{2,26},{10... | collective-permute-start | bytes 1572872 | tf_op jit(solution)/shard_map/ppermute | solution.py:85
  241.3 43.5 %collective-permute-start.20 = (bf16[128,2048]{1,0:T(8,128)(2,1)}, bf16[128,2048]{1,0:T(8,128)(2,1)}, u32[]{:S(2)}, u32[]{:S(2)}) collective-permute-start(bf16[128,2048]{1,0:T(8,128)(2,1)} %collective-permute-done.19), channel_id=1, source_target_pairs={{0,2},{1,3},{2,0},{3,1},{4,6},{5,7},{6,4},{7,5},{8,10},{9,11},{10,... | collective-permute-start | bytes 1572872 | tf_op jit(solution)/shard_map/ppermute | solution.py:72
  247.8 40.7 %collective-permute-start.23 = (bf16[128,2048]{1,0:T(8,128)(2,1)}, bf16[128,2048]{1,0:T(8,128)(2,1)}, u32[]{:S(2)}, u32[]{:S(2)}) collective-permute-start(bf16[128,2048]{1,0:T(8,128)(2,1)} %collective-permute-done.22), channel_id=1, source_target_pairs={{0,2},{1,3},{2,0},{3,1},{4,6},{5,7},{6,4},{7,5},{8,10},{9,11},{10,... | collective-permute-start | bytes 1572872 | tf_op jit(solution)/shard_map/ppermute | solution.py:72
  248.5 38.6 %collective-permute-start.25 = (bf16[128,2048]{1,0:T(8,128)(2,1)}, bf16[128,2048]{1,0:T(8,128)(2,1)}, u32[]{:S(2)}, u32[]{:S(2)}) collective-permute-start(bf16[128,2048]{1,0:T(8,128)(2,1)} %collective-permute-done.22), channel_id=1, source_target_pairs={{0,24},{8,0},{16,8},{24,16},{1,25},{9,1},{17,9},{25,17},{2,26},{10... | collective-permute-start | bytes 1572872 | tf_op jit(solution)/shard_map/ppermute | solution.py:85
  328.9 23.8 %collective-permute-start.37 = (bf16[128,2048]{1,0:T(8,128)(2,1)S(1)}, bf16[128,2048]{1,0:T(8,128)(2,1)S(1)}, u32[]{:S(2)}, u32[]{:S(2)}) collective-permute-start(bf16[128,2048]{1,0:T(8,128)(2,1)S(1)} %slice.686), channel_id=1, source_target_pairs={{0,2},{1,3},{2,0},{3,1},{4,6},{5,7},{6,4},{7,5},{8,10},{9,11},{10,... | collective-permute-start | bytes 1572872 | tf_op jit(solution)/shard_map/ppermute | solution.py:72
  330.8 33.2 %collective-permute-start.34 = (bf16[128,2048]{1,0:T(8,128)(2,1)S(1)}, bf16[128,2048]{1,0:T(8,128)(2,1)S(1)}, u32[]{:S(2)}, u32[]{:S(2)}) collective-permute-start(bf16[128,2048]{1,0:T(8,128)(2,1)S(1)} %slice.687), channel_id=1, source_target_pairs={{0,2},{1,3},{2,0},{3,1},{4,6},{5,7},{6,4},{7,5},{8,10},{9,11},{10,... | collective-permute-start | bytes 1572872 | tf_op jit(solution)/shard_map/ppermute | solution.py:72
  333.9 40.9 %collective-permute-start.32 = (bf16[128,2048]{1,0:T(8,128)(2,1)}, bf16[128,2048]{1,0:T(8,128)(2,1)S(1)}, u32[]{:S(2)}, u32[]{:S(2)}) collective-permute-start(bf16[128,2048]{1,0:T(8,128)(2,1)} %slice.688), channel_id=1, source_target_pairs={{0,2},{1,3},{2,0},{3,1},{4,6},{5,7},{6,4},{7,5},{8,10},{9,11},{10,... | collective-permute-start | bytes 1572872 | tf_op jit(solution)/shard_map/ppermute | solution.py:72
  342.4 32.4 %collective-permute-start.41 = (bf16[128,2048]{1,0:T(8,128)(2,1)}, bf16[128,2048]{1,0:T(8,128)(2,1)S(1)}, u32[]{:S(2)}, u32[]{:S(2)}) collective-permute-start(bf16[128,2048]{1,0:T(8,128)(2,1)} %fusion.90), channel_id=1, source_target_pairs={{0,24},{8,0},{16,8},{24,16},{1,25},{9,1},{17,9},{25,17},{2,26},{10... | collective-permute-start | bytes 1572872 | tf_op jit(solution)/shard_map/ppermute | solution.py:85
  353.6 37.0 %collective-permute-start.38 = (bf16[128,2048]{1,0:T(8,128)(2,1)}, bf16[128,2048]{1,0:T(8,128)(2,1)}, u32[]{:S(2)}, u32[]{:S(2)}) collective-permute-start(bf16[128,2048]{1,0:T(8,128)(2,1)} %fusion.91), channel_id=1, source_target_pairs={{0,16},{8,24},{16,0},{24,8},{1,17},{9,25},{17,1},{25,9},{2,18},{10... | collective-permute-start | bytes 1572872 | tf_op jit(solution)/shard_map/ppermute | solution.py:85
  364.9 25.8 %collective-permute-start.35 = (bf16[128,2048]{1,0:T(8,128)(2,1)}, bf16[128,2048]{1,0:T(8,128)(2,1)}, u32[]{:S(2)}, u32[]{:S(2)}) collective-permute-start(bf16[128,2048]{1,0:T(8,128)(2,1)} %fusion.92), channel_id=1, source_target_pairs={{0,8},{8,16},{16,24},{24,0},{1,9},{9,17},{17,25},{25,1},{2,10},{10... | collective-permute-start | bytes 1572872 | tf_op jit(solution)/shard_map/ppermute | solution.py:85
  367.7 25.4 %collective-permute-start.42 = (bf16[128,2048]{1,0:T(8,128)(2,1)S(1)}, bf16[128,2048]{1,0:T(8,128)(2,1)S(1)}, u32[]{:S(2)}, u32[]{:S(2)}) collective-permute-start(bf16[128,2048]{1,0:T(8,128)(2,1)S(1)} %dynamic-slice_bitcast_fusion.4), channel_id=1, source_target_pairs={{0,4},{4,0},{1,5},{5,1},{2,6},{6,2},{3,7},{7,3},{8,12},{12,8},{9,1... | collective-permute-start | bytes 1572872 | tf_op jit(solution)/shard_map/ppermute | solution.py:72
  411.5 24.9 %collective-permute-start.44 = (bf16[256,2048]{1,0:T(8,128)(2,1)S(1)}, bf16[256,2048]{1,0:T(8,128)(2,1)S(1)}, u32[]{:S(2)}, u32[]{:S(2)}) collective-permute-start(bf16[256,2048]{1,0:T(8,128)(2,1)S(1)} %pad_maximum_fusion.4), channel_id=1, source_target_pairs={{0,1},{1,0},{2,3},{3,2},{4,5},{5,4},{6,7},{7,6},{8,9},{9,8},{10,11... | collective-permute-start | bytes 3145736 | tf_op jit(solution)/shard_map/ppermute | solution.py:72
  428.3 21.5 %collective-permute-start.47 = (bf16[256,2048]{1,0:T(8,128)(2,1)S(1)}, bf16[256,2048]{1,0:T(8,128)(2,1)S(1)}, u32[]{:S(2)}, u32[]{:S(2)}) collective-permute-start(bf16[256,2048]{1,0:T(8,128)(2,1)S(1)} %constant_dynamic-update-slice_fusion.11), channel_id=1, source_target_pairs={{0,1},{1,0},{2,3},{3,2},{4,5},{5,4},{6,7},{7,6},{8,9},{9,8},{10,11... | collective-permute-start | bytes 3145736 | tf_op jit(solution)/shard_map/ppermute | solution.py:72
  469.7 32.4 %collective-permute-start.62 = (bf16[256,2048]{1,0:T(8,128)(2,1)}, bf16[256,2048]{1,0:T(8,128)(2,1)}, u32[]{:S(2)}, u32[]{:S(2)}) collective-permute-start(bf16[256,2048]{1,0:T(8,128)(2,1)} %convolution_convert_fusion.10), channel_id=1, source_target_pairs={{0,1},{1,0},{2,3},{3,2},{4,5},{5,4},{6,7},{7,6},{8,9},{9,8},{10,11... | collective-permute-start | bytes 3145736 | tf_op jit(solution)/shard_map/ppermute | solution.py:72
  489.4 20.8 %collective-permute-start.56 = (bf16[256,2048]{1,0:T(8,128)(2,1)}, bf16[256,2048]{1,0:T(8,128)(2,1)}, u32[]{:S(2)}, u32[]{:S(2)}) collective-permute-start(bf16[256,2048]{1,0:T(8,128)(2,1)} %convolution_convert_fusion.12), channel_id=1, source_target_pairs={{0,1},{1,0},{2,3},{3,2},{4,5},{5,4},{6,7},{7,6},{8,9},{9,8},{10,11... | collective-permute-start | bytes 3145736 | tf_op jit(solution)/shard_map/ppermute | solution.py:72
  491.9 22.3 %collective-permute-start.54 = (bf16[256,2048]{1,0:T(8,128)(2,1)}, bf16[256,2048]{1,0:T(8,128)(2,1)}, u32[]{:S(2)}, u32[]{:S(2)}) collective-permute-start(bf16[256,2048]{1,0:T(8,128)(2,1)} %convolution_convert_fusion.13), channel_id=1, source_target_pairs={{0,1},{1,0},{2,3},{3,2},{4,5},{5,4},{6,7},{7,6},{8,9},{9,8},{10,11... | collective-permute-start | bytes 3145736 | tf_op jit(solution)/shard_map/ppermute | solution.py:72
  500.6 25.3 %collective-permute-start.79 = (bf16[4,256,512]{2,1,0:T(8,128)(2,1)S(1)}, bf16[4,256,512]{2,1,0:T(8,128)(2,1)S(1)}, u32[]{:S(2)}, u32[]{:S(2)}) collective-permute-start(bf16[4,256,512]{2,1,0:T(8,128)(2,1)S(1)} %bitcast.284), channel_id=1, source_target_pairs={{0,4},{4,0},{1,5},{5,1},{2,6},{6,2},{3,7},{7,3},{8,12},{12,8},{9,1... | collective-permute-start | bytes 3145736 | tf_op jit(solution)/shard_map/ppermute | solution.py:72
  505.3 23.1 %collective-permute-start.63 = (bf16[128,2048]{1,0:T(8,128)(2,1)S(1)}, bf16[128,2048]{1,0:T(8,128)(2,1)S(1)}, u32[]{:S(2)}, u32[]{:S(2)}) collective-permute-start(bf16[128,2048]{1,0:T(8,128)(2,1)S(1)} %slice.681), channel_id=1, source_target_pairs={{0,2},{1,3},{2,0},{3,1},{4,6},{5,7},{6,4},{7,5},{8,10},{9,11},{10,... | collective-permute-start | bytes 1572872 | tf_op jit(solution)/shard_map/ppermute | solution.py:72
  509.4 22.0 %collective-permute-start.60 = (bf16[128,2048]{1,0:T(8,128)(2,1)S(1)}, bf16[128,2048]{1,0:T(8,128)(2,1)S(1)}, u32[]{:S(2)}, u32[]{:S(2)}) collective-permute-start(bf16[128,2048]{1,0:T(8,128)(2,1)S(1)} %slice.682), channel_id=1, source_target_pairs={{0,2},{1,3},{2,0},{3,1},{4,6},{5,7},{6,4},{7,5},{8,10},{9,11},{10,... | collective-permute-start | bytes 1572872 | tf_op jit(solution)/shard_map/ppermute | solution.py:72
  512.8 29.8 %collective-permute-start.57 = (bf16[128,2048]{1,0:T(8,128)(2,1)S(1)}, bf16[128,2048]{1,0:T(8,128)(2,1)S(1)}, u32[]{:S(2)}, u32[]{:S(2)}) collective-permute-start(bf16[128,2048]{1,0:T(8,128)(2,1)S(1)} %slice.683), channel_id=1, source_target_pairs={{0,2},{1,3},{2,0},{3,1},{4,6},{5,7},{6,4},{7,5},{8,10},{9,11},{10,... | collective-permute-start | bytes 1572872 | tf_op jit(solution)/shard_map/ppermute | solution.py:72
  516.9 36.2 %collective-permute-start.55 = (bf16[128,2048]{1,0:T(8,128)(2,1)S(1)}, bf16[128,2048]{1,0:T(8,128)(2,1)S(1)}, u32[]{:S(2)}, u32[]{:S(2)}) collective-permute-start(bf16[128,2048]{1,0:T(8,128)(2,1)S(1)} %slice.684), channel_id=1, source_target_pairs={{0,2},{1,3},{2,0},{3,1},{4,6},{5,7},{6,4},{7,5},{8,10},{9,11},{10,... | collective-permute-start | bytes 1572872 | tf_op jit(solution)/shard_map/ppermute | solution.py:72
  527.1 24.4 %collective-permute-start.80 = (bf16[4,256,512]{2,1,0:T(8,128)(2,1)S(1)}, bf16[4,256,512]{2,1,0:T(8,128)(2,1)S(1)}, u32[]{:S(2)}, u32[]{:S(2)}) collective-permute-start(bf16[4,256,512]{2,1,0:T(8,128)(2,1)S(1)} %dynamic-slice_bitcast_fusion.1), channel_id=1, source_target_pairs={{0,4},{4,0},{1,5},{5,1},{2,6},{6,2},{3,7},{7,3},{8,12},{12,8},{9,1... | collective-permute-start | bytes 3145736 | tf_op jit(solution)/shard_map/ppermute | solution.py:72
  528.6 24.5 %collective-permute-start.64 = (bf16[128,2048]{1,0:T(8,128)(2,1)S(1)}, bf16[128,2048]{1,0:T(8,128)(2,1)S(1)}, u32[]{:S(2)}, u32[]{:S(2)}) collective-permute-start(bf16[128,2048]{1,0:T(8,128)(2,1)S(1)} %fusion.84), channel_id=1, source_target_pairs={{0,24},{8,0},{16,8},{24,16},{1,25},{9,1},{17,9},{25,17},{2,26},{10... | collective-permute-start | bytes 1572872 | tf_op jit(solution)/shard_map/ppermute | solution.py:85
  531.5 42.8 %collective-permute-start.61 = (bf16[128,2048]{1,0:T(8,128)(2,1)S(1)}, bf16[128,2048]{1,0:T(8,128)(2,1)S(1)}, u32[]{:S(2)}, u32[]{:S(2)}) collective-permute-start(bf16[128,2048]{1,0:T(8,128)(2,1)S(1)} %fusion.85), channel_id=1, source_target_pairs={{0,16},{8,24},{16,0},{24,8},{1,17},{9,25},{17,1},{25,9},{2,18},{10... | collective-permute-start | bytes 1572872 | tf_op jit(solution)/shard_map/ppermute | solution.py:85
  542.8 31.5 %collective-permute-start.58 = (bf16[128,2048]{1,0:T(8,128)(2,1)S(1)}, bf16[128,2048]{1,0:T(8,128)(2,1)S(1)}, u32[]{:S(2)}, u32[]{:S(2)}) collective-permute-start(bf16[128,2048]{1,0:T(8,128)(2,1)S(1)} %fusion.86), channel_id=1, source_target_pairs={{0,8},{8,16},{16,24},{24,0},{1,9},{9,17},{17,25},{25,1},{2,10},{10... | collective-permute-start | bytes 1572872 | tf_op jit(solution)/shard_map/ppermute | solution.py:85
  575.1 30.7 %all-to-all-start.5 = ((bf16[4,256,512]{2,1,0:T(8,128)(2,1)}), bf16[4,256,512]{2,1,0:T(8,128)(2,1)}, u32[]{:S(2)}, u32[]{:S(2)}) async-start(bf16[4,256,512]{2,1,0:T(8,128)(2,1)} %fusion.51), calls=%async_computation.7 | async-start | bytes 2097152 | tf_op jit(solution)/shard_map/all_to_all | solution.py:384
  579.4 252.2 %all-gather.7.cloned.1.call-start = ((), (), s32[]{:S(2)}) async-start(), calls=%async_computation.12 | async-start | bytes 3145728 | tf_op jit(solution)/shard_map/all_gather | solution.py:385
  579.5 34.0 %collective-permute-start.82 = (f32[2,2048]{1,0:T(2,128)S(1)}, f32[2,2048]{1,0:T(2,128)S(1)}, u32[]{:S(2)}, u32[]{:S(2)}) collective-permute-start(f32[2,2048]{1,0:T(2,128)S(1)} %pad_maximum_fusion.26), channel_id=1, source_target_pairs={{0,1},{1,0},{2,3},{3,2},{4,5},{5,4},{6,7},{7,6},{8,9},{9,8},{10,11... | collective-permute-start | bytes 49160 | tf_op jit(solution)/shard_map/ppermute | solution.py:72
  610.0 62.6 %all-to-all-start.7 = ((bf16[4,256,512]{2,1,0:T(8,128)(2,1)}), bf16[4,256,512]{2,1,0:T(8,128)(2,1)S(1)}, u32[]{:S(2)}, u32[]{:S(2)}) async-start(bf16[4,256,512]{2,1,0:T(8,128)(2,1)} %fusion.50), calls=%async_computation.9 | async-start | bytes 2097152 | tf_op jit(solution)/shard_map/all_to_all | solution.py:384
  617.3 23.2 %collective-permute-start.68 = (bf16[128,2048]{1,0:T(8,128)(2,1)}, bf16[128,2048]{1,0:T(8,128)(2,1)}, u32[]{:S(2)}, u32[]{:S(2)}) collective-permute-start(bf16[128,2048]{1,0:T(8,128)(2,1)} %get-tuple-element.135), channel_id=1, source_target_pairs={{0,2},{1,3},{2,0},{3,1},{4,6},{5,7},{6,4},{7,5},{8,10},{9,11},{10,... | collective-permute-start | bytes 1572872 | tf_op jit(solution)/shard_map/ppermute | solution.py:72
  617.3 52.7 %collective-permute-start.81 = (bf16[4,256,512]{2,1,0:T(8,128)(2,1)}, bf16[4,256,512]{2,1,0:T(8,128)(2,1)}, u32[]{:S(2)}, u32[]{:S(2)}) collective-permute-start(bf16[4,256,512]{2,1,0:T(8,128)(2,1)} %dynamic-slice_bitcast_fusion), channel_id=1, source_target_pairs={{0,4},{4,0},{1,5},{5,1},{2,6},{6,2},{3,7},{7,3},{8,12},{12,8},{9,1... | collective-permute-start | bytes 3145736 | tf_op jit(solution)/shard_map/ppermute | solution.py:72
  621.9 55.9 %collective-permute-start.66 = (bf16[128,2048]{1,0:T(8,128)(2,1)}, bf16[128,2048]{1,0:T(8,128)(2,1)}, u32[]{:S(2)}, u32[]{:S(2)}) collective-permute-start(bf16[128,2048]{1,0:T(8,128)(2,1)} %broadcast_select_fusion.2), channel_id=1, source_target_pairs={{0,2},{1,3},{2,0},{3,1},{4,6},{5,7},{6,4},{7,5},{8,10},{9,11},{10,... | collective-permute-start | bytes 1572872 | tf_op jit(solution)/shard_map/ppermute | solution.py:72
  642.7 38.7 %collective-permute-start.69 = (bf16[256,2048]{1,0:T(8,128)(2,1)}, bf16[256,2048]{1,0:T(8,128)(2,1)}, u32[]{:S(2)}, u32[]{:S(2)}) collective-permute-start(bf16[256,2048]{1,0:T(8,128)(2,1)} %pad_maximum_fusion.5), channel_id=1, source_target_pairs={{0,1},{1,0},{2,3},{3,2},{4,5},{5,4},{6,7},{7,6},{8,9},{9,8},{10,11... | collective-permute-start | bytes 3145736 | tf_op jit(solution)/shard_map/ppermute | solution.py:72
  672.5 104.6 %all-to-all-start.6 = ((bf16[4,256,512]{2,1,0:T(8,128)(2,1)}), bf16[4,256,512]{2,1,0:T(8,128)(2,1)}, u32[]{:S(2)}, u32[]{:S(2)}) async-start(bf16[4,256,512]{2,1,0:T(8,128)(2,1)} %fusion.49), calls=%async_computation.8 | async-start | bytes 2097152 | tf_op jit(solution)/shard_map/all_to_all | solution.py:384
  676.8 161.7 %all-gather.11.cloned.1.call-start = ((), (), s32[]{:S(2)}) async-start(), calls=%async_computation.14 | async-start | bytes 3145728 | tf_op jit(solution)/shard_map/all_gather | solution.py:385
  677.5 175.2 %reduce-scatter.3.cloned.1.call-start = ((), (), s32[]{:S(2)}) async-start(), calls=%async_computation.10 | async-start | bytes 2621440 | tf_op jit(solution)/shard_map/reduce_scatter | solution.py:446
  693.3 159.5 %reduce-scatter.5.cloned.1.call-start = ((), (), s32[]{:S(2)}) async-start(), calls=%async_computation.11 | async-start | bytes 2621440 | tf_op jit(solution)/shard_map/reduce_scatter | solution.py:446
  734.6 33.8 %collective-permute-start.70 = (bf16[256,2048]{1,0:T(8,128)(2,1)}, bf16[256,2048]{1,0:T(8,128)(2,1)}, u32[]{:S(2)}, u32[]{:S(2)}) collective-permute-start(bf16[256,2048]{1,0:T(8,128)(2,1)} %fusion.21), channel_id=1, source_target_pairs={{0,1},{1,0},{2,3},{3,2},{4,5},{5,4},{6,7},{7,6},{8,9},{9,8},{10,11... | collective-permute-start | bytes 3145736 | tf_op jit(solution)/shard_map/ppermute | solution.py:72
  737.3 37.3 %collective-permute-start.75 = (bf16[4,256,512]{2,1,0:T(8,128)(2,1)S(1)}, bf16[4,256,512]{2,1,0:T(8,128)(2,1)}, u32[]{:S(2)}, u32[]{:S(2)}) collective-permute-start(bf16[4,256,512]{2,1,0:T(8,128)(2,1)S(1)} %dynamic-slice_bitcast_fusion.3), channel_id=1, source_target_pairs={{0,4},{4,0},{1,5},{5,1},{2,6},{6,2},{3,7},{7,3},{8,12},{12,8},{9,1... | collective-permute-start | bytes 3145736 | tf_op jit(solution)/shard_map/ppermute | solution.py:72
  774.0 53.7 %collective-permute-start.67 = (bf16[2,128,2048]{2,1,0:T(8,128)(2,1)}, bf16[2,128,2048]{2,1,0:T(8,128)(2,1)}, u32[]{:S(2)}, u32[]{:S(2)}) collective-permute-start(bf16[2,128,2048]{2,1,0:T(8,128)(2,1)} %maximum_select_fusion.5), channel_id=1, source_target_pairs={{0,1},{1,0},{2,3},{3,2},{4,5},{5,4},{6,7},{7,6},{8,9},{9,8},{10,11... | collective-permute-start | bytes 3145736 | tf_op jit(solution)/shard_map/ppermute | solution.py:72
  774.1 26.3 %collective-permute-start.77 = (bf16[4,256,512]{2,1,0:T(8,128)(2,1)}, bf16[4,256,512]{2,1,0:T(8,128)(2,1)}, u32[]{:S(2)}, u32[]{:S(2)}) collective-permute-start(bf16[4,256,512]{2,1,0:T(8,128)(2,1)} %dynamic-slice_bitcast_fusion.2), channel_id=1, source_target_pairs={{0,4},{4,0},{1,5},{5,1},{2,6},{6,2},{3,7},{7,3},{8,12},{12,8},{9,1... | collective-permute-start | bytes 3145736 | tf_op jit(solution)/shard_map/ppermute | solution.py:72
  777.2 45.7 %all-to-all-start.3 = ((bf16[4,256,512]{2,1,0:T(8,128)(2,1)}), bf16[4,256,512]{2,1,0:T(8,128)(2,1)S(1)}, u32[]{:S(2)}, u32[]{:S(2)}) async-start(bf16[4,256,512]{2,1,0:T(8,128)(2,1)} %fusion.53), calls=%async_computation.3 | async-start | bytes 2097152 | tf_op jit(solution)/shard_map/all_to_all | solution.py:454
  781.1 80.4 %all-gather.9.cloned.1.call-start = ((), (), s32[]{:S(2)}) async-start(), calls=%async_computation.13 | async-start | bytes 3145728 | tf_op jit(solution)/shard_map/all_gather | solution.py:385
  804.2 31.6 %collective-permute-start.73 = (bf16[128,2048]{1,0:T(8,128)(2,1)}, bf16[128,2048]{1,0:T(8,128)(2,1)}, u32[]{:S(2)}, u32[]{:S(2)}) collective-permute-start(bf16[128,2048]{1,0:T(8,128)(2,1)} %broadcast_select_fusion.1), channel_id=1, source_target_pairs={{0,2},{1,3},{2,0},{3,1},{4,6},{5,7},{6,4},{7,5},{8,10},{9,11},{10,... | collective-permute-start | bytes 1572872 | tf_op jit(solution)/shard_map/ppermute | solution.py:72
  822.9 29.0 %all-to-all-start.4 = ((bf16[4,256,512]{2,1,0:T(8,128)(2,1)}), bf16[4,256,512]{2,1,0:T(8,128)(2,1)S(1)}, u32[]{:S(2)}, u32[]{:S(2)}) async-start(bf16[4,256,512]{2,1,0:T(8,128)(2,1)} %fusion.52), calls=%async_computation.4 | async-start | bytes 2097152 | tf_op jit(solution)/shard_map/all_to_all | solution.py:454
  827.6 65.5 %all-reduce.6.cloned.1.call-start = ((), (), s32[]{:S(2)}) async-start(), calls=%async_computation.15 | async-start | bytes 2097152 | tf_op jit(solution)/shard_map/psum | solution.py:447
  838.2 32.1 %collective-permute-start.74 = (bf16[2,128,2048]{2,1,0:T(8,128)(2,1)}, bf16[2,128,2048]{2,1,0:T(8,128)(2,1)}, u32[]{:S(2)}, u32[]{:S(2)}) collective-permute-start(bf16[2,128,2048]{2,1,0:T(8,128)(2,1)} %maximum_select_fusion.6), channel_id=1, source_target_pairs={{0,1},{1,0},{2,3},{3,2},{4,5},{5,4},{6,7},{7,6},{8,9},{9,8},{10,11... | collective-permute-start | bytes 3145736 | tf_op jit(solution)/shard_map/ppermute | solution.py:72
  (170 other events, 1689.2 us)
Sparse Core Ops, SparseCore 0:
  606.0 53.0 all-gather.6
  679.2 32.8 all-gather.10
  789.3 44.4 all-gather.8
  852.9 40.1 all-reduce.5
Sparse Core Ops, SparseCore 1:
  693.4 43.9 reduce-scatter.2
  739.6 42.6 reduce-scatter.4

commit v2 on v1

v2 whole, which is shorter than its diff:
```python
import math

import jax
import jax.numpy as jnp
from jax import lax
from jax.experimental import pallas as pl
from jax.experimental.layout import Layout, with_layout_constraint
from jax.experimental.pallas import tpu as pltpu
from jax.sharding import PartitionSpec as P

D = 2048
HD = 128
EPSILON = 1e-06
ROTARY_BASE = 500000.0
MASKED = -1e30
LOW = jnp.bfloat16
WIDE = jnp.float32


def product(left_side, right_side):
    return jnp.dot(left_side, right_side, preferred_element_type=WIDE)


def product_back(left_side, right_side):
    return lax.dot_general(
        left_side, right_side, (((1,), (1,)), ((), ())), preferred_element_type=WIDE
    )


def product_left(left_side, right_side):
    return lax.dot_general(
        left_side, right_side, (((0,), (0,)), ((), ())), preferred_element_type=WIDE
    )


def doc_positions(segment_row):
    earlier = (segment_row[None, :] < segment_row[:, None]).astype(jnp.int32)
    return jnp.arange(segment_row.shape[0], dtype=jnp.int32) - jnp.sum(earlier, axis=1)


def rotary_tables(positions):
    half_size = HD // 2
    frequency = ROTARY_BASE ** (-(jnp.arange(half_size, dtype=WIDE) * 2.0 / HD))
    angle_table = positions.astype(WIDE)[:, None] * frequency[None, :]
    return (jnp.cos(angle_table)[:, None, :], jnp.sin(angle_table)[:, None, :])


def rotate(values, cosine, sine_table):
    half_size = values.shape[-1] // 2
    first_half = values[..., :half_size]
    second_half = values[..., half_size:]
    return jnp.concatenate(
        [
            first_half * cosine - second_half * sine_table,
            second_half * cosine + first_half * sine_table,
        ],
        axis=-1,
    )


def attention_mask(segment_row):
    places = jnp.arange(segment_row.shape[0])
    return (segment_row[:, None] == segment_row[None, :]) & (places[None, :] <= places[:, None])


def head_scores(query_heads, key_heads, allowed):
    raw_scores = jnp.einsum(
        "qhd,khd->hqk", query_heads, key_heads, preferred_element_type=WIDE
    ) * (1.0 / math.sqrt(HD))
    return jnp.where(allowed[None], raw_scores, MASKED)


def grad_blocks(lefts, rights, fsdp, split_left):
    rows, columns = lefts[0].shape[1], rights[0].shape[1]
    if split_left:
        rows = rows // fsdp
    else:
        columns = columns // fsdp
    half = rows // 2

    def kernel(*refs):
        left_refs, right_refs = refs[: len(lefts)], refs[len(lefts) : -1]
        out_ref = refs[-1]
        pieces = max(len(lefts), len(rights))

        def part(group, number):
            per = pieces // len(group)
            ref = group[number // per]
            size = ref.shape[0] // per
            start = (number % per) * size
            return ref[start : start + size, :]

        total = 0.0
        for number in range(pieces):
            total = total + lax.dot_general(
                part(left_refs, number),
                part(right_refs, number),
                (((0,), (0,)), ((), ())),
                preferred_element_type=WIDE,
            )
        out_ref[0, 0] = total[:half].astype(LOW)
        out_ref[1, 0] = total[half:].astype(LOW)

    def moving(size, width):
        return pl.BlockSpec((size, width), lambda g: (0, g))

    def fixed(size, width):
        return pl.BlockSpec((size, width), lambda g: (0, 0))

    left_spec, right_spec = (moving, fixed) if split_left else (fixed, moving)
    return pl.pallas_call(
        kernel,
        grid=(fsdp,),
        in_specs=[left_spec(left.shape[0], rows) for left in lefts]
        + [right_spec(right.shape[0], columns) for right in rights],
        out_specs=pl.BlockSpec((2, 1, half, columns), lambda g: (0, g, 0, 0)),
        out_shape=jax.ShapeDtypeStruct((2, fsdp, half, columns), LOW),
        compiler_params=pltpu.CompilerParams(vmem_limit_bytes=50 * 1024 * 1024),
        cost_estimate=pl.CostEstimate(flops=1, bytes_accessed=1, transcendentals=0),
    )(*lefts, *rights)


def pack_sends(side, w_gate, w_up, w_down, fsdp):
    rows, hidden = w_gate.shape[0] // 2, w_gate.shape[1] // fsdp
    down_rows, columns = hidden // 2, w_down.shape[1]

    def kernel(side_ref, gate_ref, up_ref, down_ref, gate_out, up_out, down_out):
        gate_out[0] = gate_ref[...]
        up_out[0] = up_ref[...]
        down_out[0] = down_ref[...]

    wide_in = pl.BlockSpec((rows, hidden), lambda g, chosen: (chosen[0], g))
    wide_out = pl.BlockSpec((1, rows, hidden), lambda g, chosen: (g, 0, 0))
    return pl.pallas_call(
        kernel,
        grid_spec=pltpu.PrefetchScalarGridSpec(
            num_scalar_prefetch=1,
            grid=(fsdp,),
            in_specs=[
                wide_in,
                wide_in,
                pl.BlockSpec((down_rows, columns), lambda g, chosen: (2 * g + chosen[0], 0)),
            ],
            out_specs=[
                wide_out,
                wide_out,
                pl.BlockSpec((1, down_rows, columns), lambda g, chosen: (g, 0, 0)),
            ],
        ),
        out_shape=[
            jax.ShapeDtypeStruct((fsdp, rows, hidden), w_gate.dtype),
            jax.ShapeDtypeStruct((fsdp, rows, hidden), w_gate.dtype),
            jax.ShapeDtypeStruct((fsdp, down_rows, columns), w_gate.dtype),
        ],
    )(side, w_gate, w_up, w_down)


def place_wide(side, gate_own, gate_other, up_own, up_other):
    fsdp, rows, hidden = gate_own.shape

    def kernel(side_ref, gate_a, gate_b, up_a, up_b, out_ref):
        for value in range(2):

            @pl.when(side_ref[0] == value)
            def _():
                mine = slice(value * rows, (value + 1) * rows)
                others = slice((1 - value) * rows, (2 - value) * rows)
                out_ref[mine, :hidden] = gate_a[0]
                out_ref[others, :hidden] = gate_b[0]
                out_ref[mine, hidden:] = up_a[0]
                out_ref[others, hidden:] = up_b[0]

    piece = pl.BlockSpec((1, rows, hidden), lambda g: (g, 0, 0))
    return pl.pallas_call(
        kernel,
        grid=(fsdp,),
        in_specs=[pl.BlockSpec(memory_space=pltpu.SMEM)] + [piece] * 4,
        out_specs=pl.BlockSpec((2 * rows, 2 * hidden), lambda g: (g, 0)),
        out_shape=jax.ShapeDtypeStruct((fsdp * 2 * rows, 2 * hidden), gate_own.dtype),
    )(side, gate_own, gate_other, up_own, up_other)


def place_down(side, own, other):
    fsdp, rows, columns = own.shape

    def kernel(side_ref, own_ref, other_ref, out_ref):
        for value in range(2):

            @pl.when(side_ref[0] == value)
            def _():
                out_ref[value * rows : (value + 1) * rows, :] = own_ref[0]
                out_ref[(1 - value) * rows : (2 - value) * rows, :] = other_ref[0]

    piece = pl.BlockSpec((1, rows, columns), lambda g: (g, 0, 0))
    return pl.pallas_call(
        kernel,
        grid=(fsdp,),
        in_specs=[pl.BlockSpec(memory_space=pltpu.SMEM), piece, piece],
        out_specs=pl.BlockSpec((2 * rows, columns), lambda g: (0, g)),
        out_shape=jax.ShapeDtypeStruct((2 * rows, fsdp * columns), own.dtype),
    )(side, own, other)


def widen_rows(side, own, other, parts):
    fsdp, rows, columns = own.shape
    hidden = columns // parts

    def kernel(side_ref, own_ref, other_ref, *out_refs):
        for value in range(2):

            @pl.when(side_ref[0] == value)
            def _():
                for number, out_ref in enumerate(out_refs):
                    take = slice(number * hidden, (number + 1) * hidden)
                    out_ref[value] = own_ref[0, :, take].astype(WIDE)
                    out_ref[1 - value] = other_ref[0, :, take].astype(WIDE)

    piece = pl.BlockSpec((1, rows, columns), lambda g: (g, 0, 0))
    outs = pl.pallas_call(
        kernel,
        grid=(fsdp,),
        in_specs=[pl.BlockSpec(memory_space=pltpu.SMEM), piece, piece],
        out_specs=[pl.BlockSpec((2, rows, hidden), lambda g: (0, 0, g))] * parts,
        out_shape=[jax.ShapeDtypeStruct((2, rows, fsdp * hidden), WIDE)] * parts,
    )(side, own, other)
    return [out.reshape(2 * rows, fsdp * hidden) for out in outs]


def widen_columns(side, own, other):
    fsdp, rows, columns = own.shape

    def kernel(side_ref, own_ref, other_ref, out_ref):
        for value in range(2):

            @pl.when(side_ref[0] == value)
            def _():
                out_ref[value * rows : (value + 1) * rows] = own_ref[0].astype(WIDE)
                out_ref[(1 - value) * rows : (2 - value) * rows] = other_ref[0].astype(WIDE)

    piece = pl.BlockSpec((1, rows, columns), lambda g: (g, 0, 0))
    return pl.pallas_call(
        kernel,
        grid=(fsdp,),
        in_specs=[pl.BlockSpec(memory_space=pltpu.SMEM), piece, piece],
        out_specs=pl.BlockSpec((2 * rows, columns), lambda g: (g, 0)),
        out_shape=jax.ShapeDtypeStruct((fsdp * 2 * rows, columns), WIDE),
    )(side, own, other)


def flip(value, axis, bit, size):
    return lax.ppermute(value, axis, [(place, place ^ bit) for place in range(size)])


def after(value, *earlier):
    return lax.optimization_barrier((value,) + earlier)[0]


def solution(mesh):
    fsdp = mesh.shape["fsdp"]
    ctx = mesh.shape["ctx"]
    tp = mesh.shape["tp"]

    def shift(value, step):
        return lax.ppermute(
            value, "fsdp", [(place, (place - step) % fsdp) for place in range(fsdp)]
        )

    def swap(value):
        return flip(value, "ctx", 1, ctx)

    def tp_gather(block):
        second = flip(block, "tp", 2, tp)
        pair = jnp.concatenate([block, second], axis=0)
        return jnp.concatenate([pair, flip(pair, "tp", 1, tp)], axis=0)

    def tp_scatter(make, rows):
        half = rows[0].shape[0] // 2
        sent = make(*(part[half:] for part in rows)).astype(LOW)
        got = flip(sent, "tp", 1, tp)
        kept = make(*(part[:half] for part in rows)) + got.astype(WIDE)
        sent_again = kept[half // 2 :].astype(LOW)
        return kept[: half // 2], flip(sent_again, "tp", 2, tp), sent, sent_again

    def local(
        inputs,
        out_grad,
        segments,
        w_query,
        w_key,
        w_value,
        w_out,
        w_gate,
        w_up,
        w_down,
        query_gain,
        key_gain,
        attn_gain,
        mlp_gain,
    ):
        f = lax.axis_index("fsdp")
        c = lax.axis_index("ctx")
        t = lax.axis_index("tp")
        half_len = inputs.shape[2]
        length = half_len * ctx
        part_len = length // tp
        block = D // fsdp
        half_block = block // 2
        heads_here = query_gain.shape[0]
        width = heads_here * HD
        hidden_here = w_gate.shape[1] // fsdp
        scale_factor = 1.0 / math.sqrt(HD)
        first = c == 0

        def pair(own, other, axis):
            return jnp.where(
                first,
                jnp.concatenate([own, other], axis=axis),
                jnp.concatenate([other, own], axis=axis),
            )

        def near_rows(value):
            return jnp.concatenate(
                [
                    lax.dynamic_slice_in_dim(value, (t ^ bit) * part_len, part_len, 0)
                    for bit in (0, 2, 1, 3)
                ],
                axis=0,
            )

        def plain_rows(value, size):
            parts = []
            for place in range(tp):
                far = t ^ place
                spot = (far & 1) * 2 + (far >> 1)
                parts.append(lax.dynamic_slice_in_dim(value, spot * size, size, 0))
            return jnp.concatenate(parts, axis=0)

        def place(r):
            return lax.rem(f + (r % fsdp), fsdp)

        gain_pack = jnp.concatenate(
            [query_gain.reshape(-1), key_gain.reshape(-1), attn_gain, mlp_gain]
        )[None]
        gain_near = jnp.concatenate(
            [gain_pack] + [shift(gain_pack, r) for r in range(1, fsdp)], axis=0
        )

        def half_of(shard, side):
            return lax.dynamic_slice_in_dim(shard, side * half_block, half_block, 0)

        def ring(own, earlier):
            moved = [half_of(own, c)]
            for r in range(1, fsdp):
                moved.append(shift(moved[-1] if r == 1 else after(moved[-1], *earlier), 1))
            whole = lax.dynamic_update_slice(
                jnp.zeros((D, own.shape[1]), LOW), after(own, moved[1]), (f * block, 0)
            )
            for r in range(1, fsdp):
                begin = place(r) * block
                whole = lax.dynamic_update_slice(whole, moved[r], (begin + c * half_block, 0))
                whole = lax.dynamic_update_slice(
                    whole, swap(moved[r]), (begin + (1 - c) * half_block, 0)
                )
            return with_layout_constraint(whole, Layout(major_to_minor=(0, 1))), moved

        qk_full, qk_moved = ring(jnp.concatenate([w_query, w_key], axis=1), (gain_near,))
        vo_full, vo_moved = ring(jnp.concatenate([w_value, w_out.T], axis=1), ())
        value_full, out_full = vo_full[:, :width], vo_full[:, width:]

        gain_all = lax.dynamic_slice_in_dim(
            jnp.concatenate([gain_near, gain_near], axis=0).astype(WIDE), lax.rem(fsdp - f, fsdp), fsdp, 0
        )
        qk_size = query_gain.size
        query_gain_row = (
            gain_all[:, :qk_size].reshape(fsdp, heads_here, -1).transpose(1, 0, 2).reshape(-1)
        )
        key_gain_row = (
            gain_all[:, qk_size : 2 * qk_size]
            .reshape(fsdp, heads_here, -1)
            .transpose(1, 0, 2)
            .reshape(-1)
        )
        attn_gains = gain_all[:, 2 * qk_size : 2 * qk_size + block].reshape(1, -1)
        mlp_gains = gain_all[:, 2 * qk_size + block : 2 * (qk_size + block)].reshape(1, -1)

        sub_len = half_len // tp
        tokens_kept = lax.dynamic_index_in_dim(inputs[:, 0], c, 0, keepdims=False)
        tokens_sent = lax.dynamic_slice(
            after(inputs, qk_moved[1]), (1 - c, 0, t * sub_len, 0), (1, 1, sub_len, D)
        )[0, 0]
        tokens_got = plain_rows(tp_gather(swap(tokens_sent)), sub_len)
        tokens = pair(tokens_kept, tokens_got, 0)
        segment_row = lax.dynamic_index_in_dim(segments[:, 0], c, 0, keepdims=False)

        half_hidden = hidden_here // 2

        def exchange(value):
            return lax.all_to_all(value, "fsdp", 0, 0, tiled=True)

        side = c[None]
        gate_sent, up_sent, down_sent = pack_sends(
            side, after(w_gate, qk_moved[1]), w_up, w_down, fsdp
        )
        gate_mine = exchange(after(gate_sent, qk_moved[-1]))
        up_mine = exchange(after(up_sent, gate_mine))
        down_mine = exchange(after(down_sent, up_mine))

        allowed = attention_mask(segment_row)
        cosine, sine_table = rotary_tables(doc_positions(segment_row))
        raw = product(tokens, qk_full)
        query_raw = raw[:, :width]
        key_raw = raw[:, width:]
        value_heads = product(tokens, value_full).astype(LOW).reshape(length, heads_here, HD)
        squares = lax.psum(
            jnp.stack([jnp.sum(query_raw * query_raw, axis=1), jnp.sum(key_raw * key_raw, axis=1)]),
            "tp",
        )
        squares, gate_mine = lax.optimization_barrier((squares, gate_mine))
        gate_other = swap(gate_mine)
        query_scale = lax.rsqrt(squares[0] / D + EPSILON)[:, None]
        key_scale = lax.rsqrt(squares[1] / D + EPSILON)[:, None]
        query_heads = rotate(
            (query_raw * query_scale * query_gain_row).reshape(length, heads_here, HD),
            cosine,
            sine_table,
        ).astype(LOW)
        key_heads = rotate(
            (key_raw * key_scale * key_gain_row).reshape(length, heads_here, HD),
            cosine,
            sine_table,
        ).astype(LOW)
        scores = head_scores(query_heads, key_heads, allowed)
        top_score = jnp.max(scores, axis=-1, keepdims=True)
        log_total = top_score + jnp.log(
            jnp.sum(jnp.exp(scores - top_score), axis=-1, keepdims=True)
        )
        probs_low = jnp.exp(scores - log_total).astype(LOW)
        probs_low, up_mine, gate_other = lax.optimization_barrier((probs_low, up_mine, gate_other))
        attended = (
            jnp.einsum("hqk,khd->qhd", probs_low, value_heads, preferred_element_type=WIDE)
            .astype(LOW)
            .reshape(length, width)
        )
        up_other = swap(up_mine)
        down_other = swap(down_mine)
        wide_full = place_wide(side, gate_mine, gate_other, up_mine, up_other)
        down_full = place_down(side, down_mine, down_other)
        attended_near = near_rows(attended)
        kept, again = tp_scatter(lambda rows: product_back(rows, out_full), (attended_near,))[:2]
        branch = kept + again.astype(WIDE)

        tokens_part = lax.dynamic_slice_in_dim(tokens, t * part_len, part_len, 0).astype(WIDE)
        branch_scale = lax.rsqrt(jnp.mean(branch * branch, axis=-1, keepdims=True) + EPSILON)
        hidden = tokens_part + branch * branch_scale * attn_gains
        hidden_low = hidden.astype(LOW)

        group_size = min(fsdp, 4)

        def to_owner(parts, gates=None):
            got = []
            for r in range(fsdp):
                kept, again = parts[r]
                if gates is not None and gates[r] is not None:
                    again = after(again, gates[r])
                part = kept + again.astype(WIDE)
                got.append(shift(part.astype(LOW), -r).astype(WIDE) if r else part)
            return sum(got[1:], got[0])

        def in_chunks(part, work):
            moved = [part]
            for _ in range(1, fsdp):
                moved.append(shift(moved[-1], 1))
            groups = []
            earlier = None
            for g in range(0, fsdp, group_size):
                group = jnp.zeros((group_size * length, D), LOW)
                for r in range(group_size):
                    second = flip(moved[g + r], "tp", 2, tp)
                    both = jnp.concatenate([moved[g + r], second], axis=0)
                    third = flip(both, "tp", 1, tp)
                    if earlier is not None:
                        third = after(third, earlier)
                    group = lax.dynamic_update_slice(group, both, (r * length, 0))
                    group = lax.dynamic_update_slice(
                        group, third, (r * length + length // 2, 0)
                    )
                    earlier = work(group[r * length : (r + 1) * length], g + r)
                groups.append(group)
            return groups

        wide_chunks, active_chunks, down_parts = [], [], []

        def forward(chunk, number):
            wide = product(chunk, wide_full)
            gate_value, up_value = wide[:, :hidden_here], wide[:, hidden_here:]
            active = (gate_value * jax.nn.sigmoid(gate_value) * up_value).astype(LOW)
            kept, again, sent, _ = tp_scatter(lambda rows: product(rows, down_full), (active,))
            down_parts.append((kept, again))
            wide_chunks.append(wide)
            active_chunks.append(active)
            return sent

        hidden_all = in_chunks(hidden_low, forward)
        down = to_owner(down_parts)

        down_scale = lax.rsqrt(jnp.mean(down * down, axis=-1, keepdims=True) + EPSILON)
        output_part = (hidden + down * down_scale * mlp_gains).astype(LOW)

        inner = lax.rem(t, tp // 2) * part_len
        grad_kept = lax.dynamic_slice(
            out_grad, (c, 0, inner, 0), (1, 1, part_len, D)
        )[0, 0]
        grad_sent = lax.dynamic_slice(
            out_grad, (1 - c, 0, inner, 0), (1, 1, part_len, D)
        )[0, 0]
        mine_here = t // (tp // 2) == c
        cotangent = jnp.where(
            mine_here, grad_kept, swap(after(grad_sent, qk_moved[-1]))
        ).astype(WIDE)

        scaled = cotangent * mlp_gains
        down_mean = jnp.mean(scaled * down, axis=-1, keepdims=True)
        down_low = (down_scale * (scaled - down * (down_scale * down_scale * down_mean))).astype(
            LOW
        )
        mlp_gain_grad = jnp.sum(cotangent * down * down_scale, axis=0)

        wide_lows, hidden_parts, last_sent = [], [], []

        def backward(chunk, number):
            wide = wide_chunks[number]
            gate_value, up_value = wide[:, :hidden_here], wide[:, hidden_here:]
            act_grad = product_back(chunk, down_full)
            sig = jax.nn.sigmoid(gate_value)
            gate_low = (act_grad * up_value * sig * (1.0 + gate_value * (1.0 - sig))).astype(LOW)
            up_low = (act_grad * gate_value * sig).astype(LOW)
            wide_low = jnp.concatenate([gate_low, up_low], axis=1)
            kept, again, sent, sent_again = tp_scatter(
                lambda rows: product_back(rows, wide_full), (wide_low,)
            )
            hidden_parts.append((kept, again))
            last_sent.append(sent_again)
            wide_lows.append(wide_low)
            return sent

        grad_all = in_chunks(down_low, backward)

        def spread(part):
            pairs = []
            for low_place in range(tp // 2):
                here, there = tp // 2 + low_place, tp + low_place
                pairs += [(here, there), (there, here)]
            got = lax.ppermute(part, ("ctx", "tp"), pairs)
            near = jnp.where(mine_here, part, got)
            far = flip(near, "tp", 2, tp)
            mine = jnp.where(mine_here, near, far)
            other = jnp.where(mine_here, far, near)
            both = jnp.where(
                first, jnp.stack([mine, other], 1), jnp.stack([other, mine], 1)
            )
            beside = flip(both, "tp", 1, tp)
            return jnp.where(
                t % 2 == 0,
                jnp.concatenate([both, beside], axis=2),
                jnp.concatenate([beside, both], axis=2),
            )

        def halves(split):
            return (
                lax.dynamic_index_in_dim(split, c, 1, keepdims=False),
                lax.dynamic_index_in_dim(split, 1 - c, 1, keepdims=False),
            )

        def half_sum(kept, sent):
            return (kept.astype(WIDE) + swap(sent).astype(WIDE)).astype(LOW)

        late = lax.optimization_barrier((*grad_all, *hidden_all, *last_sent))
        late_grad = late[: len(grad_all)]
        late_hidden = late[len(grad_all) : len(grad_all) + len(hidden_all)]
        down_split = grad_blocks(active_chunks, late_grad, fsdp, False)
        down_sum = lax.psum_scatter(down_split, "ctx", scatter_dimension=0)
        late_hidden = list(lax.optimization_barrier((*late_hidden, down_split)))[:-1]
        wide_split = grad_blocks(late_hidden, wide_lows, fsdp, True)
        wide_sum = lax.psum_scatter(wide_split, "ctx", scatter_dimension=0)
        hidden_grad = cotangent + after(to_owner(hidden_parts), wide_split)

        lifted = hidden_grad * attn_gains
        branch_mean = jnp.mean(lifted * branch, axis=-1, keepdims=True)
        branch_low = (
            branch_scale * (lifted - branch * (branch_scale * branch_scale * branch_mean))
        ).astype(LOW)
        attn_gain_grad = jnp.sum(hidden_grad * branch * branch_scale, axis=0)
        branch_low, down_sum = lax.optimization_barrier((branch_low, down_sum))
        down_back = exchange(down_sum)
        branch_near = tp_gather(branch_low)
        heads_grad = plain_rows(
            product(branch_near, out_full).astype(LOW), part_len
        ).reshape(length, heads_here, HD)
        attn_probs = jnp.exp(head_scores(query_heads, key_heads, allowed) - log_total)
        value_grad = (
            jnp.einsum(
                "hqk,qhd->khd", attn_probs.astype(LOW), heads_grad, preferred_element_type=WIDE
            )
            .astype(LOW)
            .reshape(length, width)
        )
        value_part = product_left(tokens, value_grad).astype(LOW)
        out_part = product_left(attended_near, branch_near).astype(LOW)
        heads_grad, out_part, value_part = lax.optimization_barrier(
            (heads_grad, out_part, value_part)
        )
        probs_grad = jnp.einsum(
            "qhd,khd->hqk", heads_grad, value_heads, preferred_element_type=WIDE
        )
        score_grad = (
            attn_probs * (probs_grad - jnp.sum(attn_probs * probs_grad, axis=-1, keepdims=True))
        ).astype(LOW)
        score_grad, down_back, wide_sum = lax.optimization_barrier(
            (score_grad, down_back, wide_sum)
        )
        down_other = swap(down_back)
        wide_back = exchange(wide_sum)
        query_grad = (
            jnp.einsum("hqk,khd->qhd", score_grad, key_heads, preferred_element_type=WIDE)
            * scale_factor
        )
        key_grad = (
            jnp.einsum("hqk,qhd->khd", score_grad, query_heads, preferred_element_type=WIDE)
            * scale_factor
        )
        query_norm_grad = rotate(query_grad, cosine, -sine_table).reshape(length, width)
        key_norm_grad = rotate(key_grad, cosine, -sine_table).reshape(length, width)
        query_term = query_norm_grad * query_gain_row
        key_term = key_norm_grad * key_gain_row
        sums = jnp.concatenate(
            [
                jnp.sum(query_term * query_raw, axis=1),
                jnp.sum(key_term * key_raw, axis=1),
                attn_gain_grad,
                mlp_gain_grad,
            ]
        )
        sums = lax.psum(sums, "tp")
        dots = sums[: 2 * length].reshape(2, length)
        rows_grad = sums[2 * length :].reshape(2, D)
        query_cube = query_scale * query_scale * query_scale
        key_cube = key_scale * key_scale * key_scale
        query_raw_grad = (
            query_scale * query_term - query_raw * (query_cube * dots[0][:, None] / D)
        ).astype(LOW)
        key_raw_grad = (
            key_scale * key_term - key_raw * (key_cube * dots[1][:, None] / D)
        ).astype(LOW)
        query_gain_grad = jnp.sum(query_norm_grad * query_raw * query_scale, axis=0)
        key_gain_grad = jnp.sum(key_norm_grad * key_raw * key_scale, axis=0)
        qk_grad = jnp.concatenate([query_raw_grad, key_raw_grad], axis=1)

        def scattered(partial, dim):
            return lax.psum_scatter(partial, "fsdp", scatter_dimension=dim, tiled=True)

        out_mine, value_mine = scattered(out_part, 1), scattered(value_part, 0)
        gain_part = jnp.concatenate(
            [
                rows_grad.reshape(2, fsdp, block).transpose(1, 0, 2).reshape(fsdp, 2 * block),
                jnp.stack([query_gain_grad, key_gain_grad])
                .reshape(2 * heads_here, fsdp, HD // fsdp)
                .transpose(1, 0, 2)
                .reshape(fsdp, -1),
            ],
            axis=1,
        )
        gain_rows = -(-gain_part.shape[1] // (16 * width)) * 16
        gain_part = jnp.pad(gain_part, ((0, 0), (0, gain_rows * width - gain_part.shape[1])))
        gain_part = lax.optimization_barrier(
            gain_part.astype(LOW).reshape(fsdp, gain_rows, width)
        )

        def half_grads(grads, more):
            kept, sent = halves(grads.astype(LOW).reshape(fsdp, 2, half_block, width))
            if more is not None:
                kept = jnp.concatenate([kept, more], axis=1)
                sent = jnp.concatenate([sent, more], axis=1)
            return kept, sent

        def own_sum(summed):
            return jnp.sum(exchange(summed).astype(WIDE), axis=0)

        def row_shard(mine):
            mine = lax.optimization_barrier(mine.astype(LOW))
            return pair(mine, swap(mine), 0).astype(WIDE)

        query_kept, query_sent = half_grads(product_left(tokens, query_raw_grad), gain_part)
        key_kept, key_sent = half_grads(
            product_left(tokens, after(key_raw_grad, query_sent)), None
        )
        query_sum, out_mine, value_mine, wide_back = lax.optimization_barrier(
            (half_sum(query_kept, query_sent), out_mine, value_mine, wide_back)
        )
        wide_far = swap(wide_back)
        grad_out, grad_value = lax.psum((out_mine, value_mine), "ctx")
        grad_down = widen_columns(side, down_back, down_other)
        query_mine = own_sum(query_sum)
        key_sum, grad_down = lax.optimization_barrier(
            (half_sum(key_kept, key_sent), grad_down)
        )
        grad_gate, grad_up = widen_rows(side, wide_back, wide_far, 2)
        key_mine, grad_out, grad_value, grad_gate, grad_up = lax.optimization_barrier(
            (own_sum(key_sum), grad_out, grad_value, grad_gate, grad_up)
        )
        grad_query = row_shard(query_mine[:half_block])
        grad_key = row_shard(key_mine)
        own_gains = query_mine[half_block:].reshape(-1)
        qk_grad, value_grad = lax.optimization_barrier((qk_grad, value_grad, key_sent))[:2]
        grad_out, grad_value = grad_out.astype(WIDE), grad_value.astype(WIDE)

        kept, again = tp_scatter(
            lambda rows, more: product_back(rows, qk_full) + product_back(more, value_full),
            (near_rows(qk_grad), near_rows(value_grad)),
        )[:2]
        input_part = hidden_grad + (kept + again.astype(WIDE))

        both_parts = lax.optimization_barrier(jnp.stack([output_part, input_part.astype(LOW)]))
        both_parts = spread(both_parts)[:, :, None]
        layer_out, layer_in_grad = both_parts[0], both_parts[1].astype(WIDE)

        sum_heads = own_gains[2 * block : 2 * block + 2 * heads_here * (HD // fsdp)].reshape(2, heads_here, HD // fsdp)
        return (
            layer_out,
            layer_in_grad,
            grad_query,
            grad_key,
            grad_value,
            grad_out,
            grad_gate,
            grad_up,
            grad_down,
            sum_heads[0],
            sum_heads[1],
            own_gains[:block],
            own_gains[block : 2 * block],
        )

    rows = P("fsdp", "tp")
    columns = P("tp", "fsdp")
    whole_tokens = P(None, "fsdp", "ctx", None)
    return jax.shard_map(
        local,
        mesh=mesh,
        in_specs=(
            whole_tokens,
            whole_tokens,
            P(None, "fsdp", None),
            rows,
            rows,
            rows,
            columns,
            rows,
            rows,
            columns,
            columns,
            columns,
            P("fsdp"),
            P("fsdp"),
        ),
        out_specs=(
            whole_tokens,
            whole_tokens,
            rows,
            rows,
            rows,
            columns,
            rows,
            rows,
            columns,
            columns,
            columns,
            P("fsdp"),
            P("fsdp"),
        ),
        check_vma=False,
    )
```

time: 913 us -> 849 us (0.930)
  waiting for transfers between devices: 306 us -> 416 us
  local copies, waits for them, and re-layouts: 174 us -> 85.5 us
  starting transfers between devices: 176 us -> 108 us
  Pallas kernels: 0 us -> 44 us
  matrix products: 120 us -> 87.6 us
  other arithmetic: 96.4 us -> 64 us
    ppermute x65 -> x59, waiting for transfers between devices: 162 us -> 259 us  [flip(): lax.ppermute(value, axis, [(place, place ^ bit) for place in range(size)])]
    ppermute x65 -> x59, starting transfers between devices: 87 us -> 38.4 us  [flip(): lax.ppermute(value, axis, [(place, place ^ bit) for place in range(size)])]
    pallas_call x0 -> x7, Pallas kernels: none -> 44 us  [the longest x2 21.3 us: grad_blocks(): pl.pallas_call(kernel, grid=(fsdp,), in_specs=[left_spec(left.shape[0], r...]
    dot_general x18, matrix products: 49.7 us -> 30.4 us  [product_back(): lax.dot_general(left_side, right_side, (((1,), (1,)), ((), ())), preferre...]
    dot_general x6 -> x4, matrix products: 28.8 us -> 9.84 us  [product_left(): lax.dot_general(left_side, right_side, (((0,), (0,)), ((), ())), preferre...]
    convert_element_type x24 -> x17, other arithmetic: 36 us -> 18.4 us  [the longest x2 5.4 us: half_sum(): return (kept.astype(WIDE) + swap(sent).astype(WIDE)).astype(LOW)]
    all_to_all x8 -> x7, waiting for transfers between devices: 59.3 us -> 74.6 us  [exchange(): return lax.all_to_all(value, 'fsdp', 0, 0, tiled=True)]
    ppermute x21, starting transfers between devices: 53.3 us -> 38.5 us  [shift(): lax.ppermute(value, 'fsdp', [(place, (place - step) % fsdp) for place in...]
  transfers between devices with their start and end apart: 102 -> 93, of which waited for: 34 -> 41; matrix products, arithmetic and copies ran while one was open for 37% -> 24% of each run, Pallas kernels for 0% -> 4%
where the time goes in v2:
time: 849 us; the launch traced here: 839 us
  waiting for transfers between devices  416 us (49%)
  starting transfers between devices  108 us (13%)
  matrix products  87.6 us (10%)
  local copies, waits for them, and re-layouts  85.5 us (10%)
  other arithmetic  64 us (8%)
  Pallas kernels  44 us (5%)
  blocking collectives  16.9 us (2%)
  between operations  16.7 us (2%)
    ppermute x59, waiting for transfers between devices, flip(): lax.ppermute(value, axis, [(place, place ^ bit) for place in range(size)])  259 us
    ppermute x21, waiting for transfers between devices, shift(): lax.ppermute(value, 'fsdp', [(place, (place - step) % fsdp) for place in...  77.1 us
    all_to_all x7, waiting for transfers between devices, exchange(): return lax.all_to_all(value, 'fsdp', 0, 0, tiled=True)  74.6 us
    ppermute x21, starting transfers between devices, shift(): lax.ppermute(value, 'fsdp', [(place, (place - step) % fsdp) for place in...  38.5 us
    ppermute x59, starting transfers between devices, flip(): lax.ppermute(value, axis, [(place, place ^ bit) for place in range(size)])  38.4 us
    dot_general x15, matrix products, product(): return jnp.dot(left_side, right_side, preferred_element_type=WIDE)  30.8 us
    dot_general x18, matrix products, product_back(): lax.dot_general(left_side, right_side, (((1,), (1,)), ((), ())), preferre...  30.4 us
    all_to_all x7, starting transfers between devices, exchange(): return lax.all_to_all(value, 'fsdp', 0, 0, tiled=True)  29.2 us
  transfers between devices with their start and end apart: 93, of which 41 were waited for; matrix products, arithmetic and copies ran while one was open for 24% of the time, Pallas kernels for 4%

profile of v2, /device:TPU:0, one launch (start us, length us, event | category | flops | bytes accessed | tf_op | source)
XLA Modules:
  0.0 839.0 jit_solution(1404058193869014153)
XLA Ops:
  25.2 8.7 %collective-permute-done.4 = bf16[256,1024]{1,0:T(8,128)(2,1)} collective-permute-done((bf16[256,1024]{1,0:T(8,128)(2,1)S(1)}, bf16[256,1024]{1,0:T(8,128)(2,1)}, u32[]{:S(2)}, u32[]{:S(2)}) %collective-permute-start.4) | collective-permute-done | bytes 524320 | tf_op jit(solution)/shard_map/ppermute | solution.py:264
  36.2 9.0 %collective-permute-done = bf16[256,1024]{1,0:T(8,128)(2,1)} collective-permute-done((bf16[256,1024]{1,0:T(8,128)(2,1)}, bf16[256,1024]{1,0:T(8,128)(2,1)}, u32[]{:S(2)}, u32[]{:S(2)}) %collective-permute-start) | collective-permute-done | bytes 524320 | tf_op jit(solution)/shard_map/ppermute | solution.py:264
  61.5 4.1 shard_map.237
  88.1 4.3 all-to-all-start
  104.4 7.1 collective-permute-done.17
  112.4 4.5 fusion.169
  117.2 5.7 psum.28
  124.7 4.3 fusion.42
  129.1 4.5 all-to-all-start.1
  142.3 19.7 %collective-permute-done.18.gate_b = bf16[4,256,512]{2,1,0:T(8,128)(2,1)} collective-permute-done((bf16[4,256,512]{2,1,0:T(8,128)(2,1)}, bf16[4,256,512]{2,1,0:T(8,128)(2,1)}, u32[]{:S(2)}, u32[]{:S(2)}) %collective-permute-start.18) | collective-permute-done | bytes 1048608 | tf_op jit(solution)/shard_map/ppermute | solution.py:251
  170.4 4.8 all-to-all-start.2
  175.7 7.2 collective-permute-done.20
  187.9 13.4 %all-to-all-done.2.own_ref = bf16[4,256,512]{2,1,0:T(8,128)(2,1)} async-done(((bf16[4,256,512]{2,1,0:T(8,128)(2,1)}), bf16[4,256,512]{2,1,0:T(8,128)(2,1)}, u32[]{:S(2)}, u32[]{:S(2)}) %all-to-all-start.2) | async-done | bytes 1048608 | tf_op jit(solution)/shard_map/all_to_all | solution.py:398
  204.1 9.9 %collective-permute-done.27 = bf16[128,2048]{1,0:T(8,128)(2,1)S(1)} collective-permute-done((bf16[128,2048]{1,0:T(8,128)(2,1)S(1)}, bf16[128,2048]{1,0:T(8,128)(2,1)S(1)}, u32[]{:S(2)}, u32[]{:S(2)}) %collective-permute-start.27) | collective-permute-done | bytes 524320 | tf_op jit(solution)/shard_map/ppermute | solution.py:264
  217.3 4.7 shard_map.238
  222.0 4.4 dynamic_update_slice.104
  227.3 7.2 collective-permute-done.24.other_ref
  234.5 3.8 shard_map.239
  239.6 4.0 collective-permute-start.39
  247.0 5.3 fusion.23
  263.0 8.4 %collective-permute-done.40 = bf16[128,2048]{1,0:T(8,128)(2,1)S(1)} collective-permute-done((bf16[128,2048]{1,0:T(8,128)(2,1)S(1)}, bf16[128,2048]{1,0:T(8,128)(2,1)S(1)}, u32[]{:S(2)}, u32[]{:S(2)}) %collective-permute-start.40) | collective-permute-done | bytes 524320 | tf_op jit(solution)/shard_map/ppermute | solution.py:251
  289.4 19.5 %collective-permute-done.31 = bf16[128,2048]{1,0:T(8,128)(2,1)S(1)} collective-permute-done((bf16[128,2048]{1,0:T(8,128)(2,1)S(1)}, bf16[128,2048]{1,0:T(8,128)(2,1)S(1)}, u32[]{:S(2)}, u32[]{:S(2)}) %collective-permute-start.31) | collective-permute-done | bytes 524320 | tf_op jit(solution)/shard_map/ppermute | solution.py:251
  309.9 10.3 %collective-permute-done.37 = bf16[128,2048]{1,0:T(8,128)(2,1)S(1)} collective-permute-done((bf16[128,2048]{1,0:T(8,128)(2,1)S(1)}, bf16[128,2048]{1,0:T(8,128)(2,1)S(1)}, u32[]{:S(2)}, u32[]{:S(2)}) %collective-permute-start.37) | collective-permute-done | bytes 524320 | tf_op jit(solution)/shard_map/ppermute | solution.py:251
  321.1 9.9 %collective-permute-done.43 = bf16[128,2048]{1,0:T(8,128)(2,1)S(1)} collective-permute-done((bf16[128,2048]{1,0:T(8,128)(2,1)S(1)}, bf16[128,2048]{1,0:T(8,128)(2,1)S(1)}, u32[]{:S(2)}, u32[]{:S(2)}) %collective-permute-start.43) | collective-permute-done | bytes 524320 | tf_op jit(solution)/shard_map/ppermute | solution.py:251
  335.5 12.3 %collective-permute-done.38 = bf16[128,2048]{1,0:T(8,128)(2,1)} collective-permute-done((bf16[128,2048]{1,0:T(8,128)(2,1)}, bf16[128,2048]{1,0:T(8,128)(2,1)}, u32[]{:S(2)}, u32[]{:S(2)}) %collective-permute-start.38) | collective-permute-done | bytes 524320 | tf_op jit(solution)/shard_map/ppermute | solution.py:264
  347.8 9.2 %collective-permute-done.44 = bf16[128,2048]{1,0:T(8,128)(2,1)} collective-permute-done((bf16[128,2048]{1,0:T(8,128)(2,1)}, bf16[128,2048]{1,0:T(8,128)(2,1)}, u32[]{:S(2)}, u32[]{:S(2)}) %collective-permute-start.44) | collective-permute-done | bytes 524320 | tf_op jit(solution)/shard_map/ppermute | solution.py:264
  365.9 9.3 %collective-permute-done.46 = bf16[128,2048]{1,0:T(8,128)(2,1)S(1)} collective-permute-done((bf16[128,2048]{1,0:T(8,128)(2,1)S(1)}, bf16[128,2048]{1,0:T(8,128)(2,1)S(1)}, u32[]{:S(2)}, u32[]{:S(2)}) %collective-permute-start.46) | collective-permute-done | bytes 524320 | tf_op jit(solution)/shard_map/ppermute | solution.py:251
  378.5 3.3 collective-permute-start.56
  382.9 8.1 collective-permute-done.51
  393.2 4.3 collective-permute-start.62
  401.2 5.7 collective-permute-done.62
  408.0 11.9 %collective-permute-done.63 = bf16[128,2048]{1,0:T(8,128)(2,1)S(1)} collective-permute-done((bf16[128,2048]{1,0:T(8,128)(2,1)S(1)}, bf16[128,2048]{1,0:T(8,128)(2,1)S(1)}, u32[]{:S(2)}, u32[]{:S(2)}) %collective-permute-start.63) | collective-permute-done | bytes 524320 | tf_op jit(solution)/shard_map/ppermute | solution.py:251
  445.6 8.2 shard_map.240
  457.7 13.1 %shard_map.241 = bf16[2,4,256,1024]{3,2,1,0:T(8,128)(2,1)} custom-call(bf16[2048,2048]{1,0:T(8,128)(2,1)} %copy-done.8, bf16[512,1024]{1,0:T(8,128)(2,1)S(1)} %pad_maximum_fusion.2.refs_1_, bf16[512,1024]{1,0:T(8,128)(2,1)S(1)} %pad_maximum_fusion.3.refs_2_, bf16[512,1024]{1,0:T(8,128)(2,1)S(1)} %pad_maximum_fusion.4.refs_3_, ...), custom_call_target="tpu_custom_call" | custom-call | flops 1 | bytes 1 | tf_op jit(solution)/shard_map/pallas_call | solution.py:111
  474.9 10.9 %collective-permute-done.54 = bf16[128,2048]{1,0:T(8,128)(2,1)S(1)} collective-permute-done((bf16[128,2048]{1,0:T(8,128)(2,1)}, bf16[128,2048]{1,0:T(8,128)(2,1)S(1)}, u32[]{:S(2)}, u32[]{:S(2)}) %collective-permute-start.54) | collective-permute-done | bytes 524320 | tf_op jit(solution)/shard_map/ppermute | solution.py:251
  489.2 7.9 collective-permute-done.60
  497.7 21.0 %collective-permute-done.66 = bf16[128,2048]{1,0:T(8,128)(2,1)S(1)} collective-permute-done((bf16[128,2048]{1,0:T(8,128)(2,1)}, bf16[128,2048]{1,0:T(8,128)(2,1)S(1)}, u32[]{:S(2)}, u32[]{:S(2)}) %collective-permute-start.66) | collective-permute-done | bytes 524320 | tf_op jit(solution)/shard_map/ppermute | solution.py:251
  519.9 4.1 collective-permute-done.61
  524.0 11.1 %collective-permute-done.67 = bf16[128,2048]{1,0:T(8,128)(2,1)S(1)} collective-permute-done((bf16[128,2048]{1,0:T(8,128)(2,1)S(1)}, bf16[128,2048]{1,0:T(8,128)(2,1)S(1)}, u32[]{:S(2)}, u32[]{:S(2)}) %collective-permute-start.67) | collective-permute-done | bytes 524320 | tf_op jit(solution)/shard_map/ppermute | solution.py:264
  540.2 13.3 %collective-permute-done.68 = bf16[128,2048]{1,0:T(8,128)(2,1)S(1)} collective-permute-done((bf16[128,2048]{1,0:T(8,128)(2,1)S(1)}, bf16[128,2048]{1,0:T(8,128)(2,1)S(1)}, u32[]{:S(2)}, u32[]{:S(2)}) %collective-permute-start.68) | collective-permute-done | bytes 524320 | tf_op jit(solution)/shard_map/ppermute | solution.py:251
  554.5 4.3 all-to-all-start.3
  559.2 3.6 fusion.45
  564.0 4.5 convolution_convert_fusion.3
  576.8 8.1 multiply_convert_fusion
  584.9 12.0 %all-to-all-done.3.own_ref = bf16[4,256,512]{2,1,0:T(8,128)(2,1)} async-done(((bf16[4,256,512]{2,1,0:T(8,128)(2,1)}), bf16[4,256,512]{2,1,0:T(8,128)(2,1)}, u32[]{:S(2)}, u32[]{:S(2)}) %all-to-all-start.3) | async-done | bytes 1048608 | tf_op jit(solution)/shard_map/all_to_all | solution.py:398
  603.1 11.3 %psum.29 = f32[5120]{0:T(1024)S(1)} all-reduce(f32[5120]{0:T(1024)S(1)} %pad_maximum_fusion.16), channel_id=1, replica_groups=mesh['fsdp'=4,'ctx'=2,'tp'=4] {'tp'}, use_global_device_ids=true, to_apply=%region_17.18 | all-reduce | flops 5120 | bytes 40960 | tf_op jit(solution)/shard_map/psum | solution.py:643
  614.7 3.2 subtract_convert_fusion.1
  626.4 4.4 fusion.6
  630.8 3.6 all-to-all-start.4
  637.2 3.9 fusion.5
  643.6 11.9 %collective-permute-done.71 = bf16[128,2048]{1,0:T(8,128)(2,1)S(1)} collective-permute-done((bf16[128,2048]{1,0:T(8,128)(2,1)S(1)}, bf16[128,2048]{1,0:T(8,128)(2,1)S(1)}, u32[]{:S(2)}, u32[]{:S(2)}) %collective-permute-start.71) | collective-permute-done | bytes 524320 | tf_op jit(solution)/shard_map/ppermute | solution.py:251
  660.6 29.7 %collective-permute-done.78.other_ref = bf16[4,256,512]{2,1,0:T(8,128)(2,1)} collective-permute-done((bf16[4,256,512]{2,1,0:T(8,128)(2,1)}, bf16[4,256,512]{2,1,0:T(8,128)(2,1)}, u32[]{:S(2)}, u32[]{:S(2)}) %collective-permute-start.78) | collective-permute-done | bytes 1048608 | tf_op jit(solution)/shard_map/ppermute | solution.py:251
  690.4 4.2 shard_map.242
  697.4 19.1 %all-to-all-done.4.own_ref = bf16[4,256,1024]{2,1,0:T(8,128)(2,1)S(1)} async-done(((bf16[4,256,1024]{2,1,0:T(8,128)(2,1)}), bf16[4,256,1024]{2,1,0:T(8,128)(2,1)S(1)}, u32[]{:S(2)}, u32[]{:S(2)}) %all-to-all-start.4) | async-done | bytes 2097184 | tf_op jit(solution)/shard_map/all_to_all | solution.py:398
  716.4 4.3 all-to-all-start.6
  724.2 11.8 %collective-permute-done.75 = bf16[4,272,512]{2,1,0:T(8,128)(2,1)} collective-permute-done((bf16[4,272,512]{2,1,0:T(8,128)(2,1)}, bf16[4,272,512]{2,1,0:T(8,128)(2,1)}, u32[]{:S(2)}, u32[]{:S(2)}) %collective-permute-start.75) | collective-permute-done | bytes 1114144 | tf_op jit(solution)/shard_map/ppermute | solution.py:251
  738.6 8.4 %all-to-all-done.6 = bf16[4,256,512]{2,1,0:T(8,128)(2,1)} async-done(((bf16[4,256,512]{2,1,0:T(8,128)(2,1)}), bf16[4,256,512]{2,1,0:T(8,128)(2,1)}, u32[]{:S(2)}, u32[]{:S(2)}) %all-to-all-start.6) | async-done | bytes 1048608 | tf_op jit(solution)/shard_map/all_to_all | solution.py:398
  747.0 3.5 all-to-all-start.5
  755.6 21.7 %all-to-all-done.5 = bf16[4,272,512]{2,1,0:T(8,128)(2,1)S(1)} async-done(((bf16[4,272,512]{2,1,0:T(8,128)(2,1)}), bf16[4,272,512]{2,1,0:T(8,128)(2,1)S(1)}, u32[]{:S(2)}, u32[]{:S(2)}) %all-to-all-start.5) | async-done | bytes 1114144 | tf_op jit(solution)/shard_map/all_to_all | solution.py:398
  778.9 23.6 %collective-permute-done.79.other_ref = bf16[4,256,1024]{2,1,0:T(8,128)(2,1)} collective-permute-done((bf16[4,256,1024]{2,1,0:T(8,128)(2,1)S(1)}, bf16[4,256,1024]{2,1,0:T(8,128)(2,1)}, u32[]{:S(2)}, u32[]{:S(2)}) %collective-permute-start.79) | collective-permute-done | bytes 2097184 | tf_op jit(solution)/shard_map/ppermute | solution.py:251
  802.5 5.9 shard_map.243
  808.4 5.6 all-reduce.6.cloned.1.call-done
  823.4 5.2 maximum_select_fusion
  828.7 3.4 fusion.8
  (582 shorter events, 266.8 us)
Async XLA Ops:
  20.4 24.8 %collective-permute-start = (bf16[256,1024]{1,0:T(8,128)(2,1)}, bf16[256,1024]{1,0:T(8,128)(2,1)}, u32[]{:S(2)}, u32[]{:S(2)}) collective-permute-start(bf16[256,1024]{1,0:T(8,128)(2,1)} %constant_dynamic-slice_fusion.18), channel_id=1, source_target_pairs={{0,24},{8,0},{16,8},{24,16},{1,25},{9,1},{17,9},{25,17},{2,26},{10... | collective-permute-start | bytes 1572872 | tf_op jit(solution)/shard_map/ppermute | solution.py:264
  33.9 31.7 %collective-permute-start.6 = (bf16[256,1024]{1,0:T(8,128)(2,1)}, bf16[256,1024]{1,0:T(8,128)(2,1)}, u32[]{:S(2)}, u32[]{:S(2)}) collective-permute-start(bf16[256,1024]{1,0:T(8,128)(2,1)} %collective-permute-done.4), channel_id=1, source_target_pairs={{0,24},{8,0},{16,8},{24,16},{1,25},{9,1},{17,9},{25,17},{2,26},{10... | collective-permute-start | bytes 1572872 | tf_op jit(solution)/shard_map/ppermute | solution.py:264
  47.7 19.9 %collective-permute-start.14 = (bf16[256,1024]{1,0:T(8,128)(2,1)}, bf16[256,1024]{1,0:T(8,128)(2,1)}, u32[]{:S(2)}, u32[]{:S(2)}) collective-permute-start(bf16[256,1024]{1,0:T(8,128)(2,1)} %collective-permute-done), channel_id=1, source_target_pairs={{0,24},{8,0},{16,8},{24,16},{1,25},{9,1},{17,9},{25,17},{2,26},{10... | collective-permute-start | bytes 1572872 | tf_op jit(solution)/shard_map/ppermute | solution.py:264
  50.6 19.3 %collective-permute-start.5 = (bf16[256,1024]{1,0:T(8,128)(2,1)}, bf16[256,1024]{1,0:T(8,128)(2,1)}, u32[]{:S(2)}, u32[]{:S(2)}) collective-permute-start(bf16[256,1024]{1,0:T(8,128)(2,1)} %collective-permute-done.4), channel_id=1, source_target_pairs={{0,4},{4,0},{1,5},{5,1},{2,6},{6,2},{3,7},{7,3},{8,12},{12,8},{9,1... | collective-permute-start | bytes 1572872 | tf_op jit(solution)/shard_map/ppermute | solution.py:251
  51.2 26.7 %collective-permute-start.10 = (bf16[256,1024]{1,0:T(8,128)(2,1)}, bf16[256,1024]{1,0:T(8,128)(2,1)}, u32[]{:S(2)}, u32[]{:S(2)}) collective-permute-start(bf16[256,1024]{1,0:T(8,128)(2,1)} %collective-permute-done), channel_id=1, source_target_pairs={{0,4},{4,0},{1,5},{5,1},{2,6},{6,2},{3,7},{7,3},{8,12},{12,8},{9,1... | collective-permute-start | bytes 1572872 | tf_op jit(solution)/shard_map/ppermute | solution.py:251
  65.7 28.3 %collective-permute-start.8 = (bf16[256,1024]{1,0:T(8,128)(2,1)}, bf16[256,1024]{1,0:T(8,128)(2,1)}, u32[]{:S(2)}, u32[]{:S(2)}) collective-permute-start(bf16[256,1024]{1,0:T(8,128)(2,1)} %collective-permute-done.6), channel_id=1, source_target_pairs={{0,24},{8,0},{16,8},{24,16},{1,25},{9,1},{17,9},{25,17},{2,26},{10... | collective-permute-start | bytes 1572872 | tf_op jit(solution)/shard_map/ppermute | solution.py:264
  65.8 16.8 %collective-permute-start.3 = (bf16[128,2048]{1,0:T(8,128)(2,1)S(1)}, bf16[128,2048]{1,0:T(8,128)(2,1)S(1)}, u32[]{:S(2)}, u32[]{:S(2)}) collective-permute-start(bf16[128,2048]{1,0:T(8,128)(2,1)S(1)} %pad_maximum_fusion.12), channel_id=1, source_target_pairs={{0,1},{1,0},{2,3},{3,2},{4,5},{5,4},{6,7},{7,6},{8,9},{9,8},{10,11... | collective-permute-start | bytes 1572872 | tf_op jit(solution)/shard_map/ppermute | solution.py:251
  67.7 20.4 %collective-permute-start.16 = (bf16[256,1024]{1,0:T(8,128)(2,1)}, bf16[256,1024]{1,0:T(8,128)(2,1)}, u32[]{:S(2)}, u32[]{:S(2)}) collective-permute-start(bf16[256,1024]{1,0:T(8,128)(2,1)} %collective-permute-done.14), channel_id=1, source_target_pairs={{0,24},{8,0},{16,8},{24,16},{1,25},{9,1},{17,9},{25,17},{2,26},{10... | collective-permute-start | bytes 1572872 | tf_op jit(solution)/shard_map/ppermute | solution.py:264
  69.9 24.6 %collective-permute-start.7 = (bf16[256,1024]{1,0:T(8,128)(2,1)}, bf16[256,1024]{1,0:T(8,128)(2,1)}, u32[]{:S(2)}, u32[]{:S(2)}) collective-permute-start(bf16[256,1024]{1,0:T(8,128)(2,1)} %collective-permute-done.6), channel_id=1, source_target_pairs={{0,4},{4,0},{1,5},{5,1},{2,6},{6,2},{3,7},{7,3},{8,12},{12,8},{9,1... | collective-permute-start | bytes 1572872 | tf_op jit(solution)/shard_map/ppermute | solution.py:251
  77.9 22.5 %collective-permute-start.15 = (bf16[256,1024]{1,0:T(8,128)(2,1)}, bf16[256,1024]{1,0:T(8,128)(2,1)}, u32[]{:S(2)}, u32[]{:S(2)}) collective-permute-start(bf16[256,1024]{1,0:T(8,128)(2,1)} %collective-permute-done.14), channel_id=1, source_target_pairs={{0,4},{4,0},{1,5},{5,1},{2,6},{6,2},{3,7},{7,3},{8,12},{12,8},{9,1... | collective-permute-start | bytes 1572872 | tf_op jit(solution)/shard_map/ppermute | solution.py:251
  88.1 41.0 %all-to-all-start = ((bf16[4,256,512]{2,1,0:T(8,128)(2,1)}), bf16[4,256,512]{2,1,0:T(8,128)(2,1)}, u32[]{:S(2)}, u32[]{:S(2)}) async-start(bf16[4,256,512]{2,1,0:T(8,128)(2,1)} %get-tuple-element.72), calls=%async_computation | async-start | bytes 2097152 | tf_op jit(solution)/shard_map/all_to_all | solution.py:398
  92.4 19.2 %collective-permute-start.17 = (bf16[256,1024]{1,0:T(8,128)(2,1)}, bf16[256,1024]{1,0:T(8,128)(2,1)S(1)}, u32[]{:S(2)}, u32[]{:S(2)}) collective-permute-start(bf16[256,1024]{1,0:T(8,128)(2,1)} %collective-permute-done.16), channel_id=1, source_target_pairs={{0,4},{4,0},{1,5},{5,1},{2,6},{6,2},{3,7},{7,3},{8,12},{12,8},{9,1... | collective-permute-start | bytes 1572872 | tf_op jit(solution)/shard_map/ppermute | solution.py:251
  93.9 28.9 %collective-permute-start.9 = (bf16[256,1024]{1,0:T(8,128)(2,1)}, bf16[256,1024]{1,0:T(8,128)(2,1)}, u32[]{:S(2)}, u32[]{:S(2)}) collective-permute-start(bf16[256,1024]{1,0:T(8,128)(2,1)} %collective-permute-done.8), channel_id=1, source_target_pairs={{0,4},{4,0},{1,5},{5,1},{2,6},{6,2},{3,7},{7,3},{8,12},{12,8},{9,1... | collective-permute-start | bytes 1572872 | tf_op jit(solution)/shard_map/ppermute | solution.py:251
  129.1 33.0 %all-to-all-start.1 = ((bf16[4,256,512]{2,1,0:T(8,128)(2,1)}), bf16[4,256,512]{2,1,0:T(8,128)(2,1)}, u32[]{:S(2)}, u32[]{:S(2)}) async-start(bf16[4,256,512]{2,1,0:T(8,128)(2,1)} %get-tuple-element.75), calls=%async_computation.1 | async-start | bytes 2097152 | tf_op jit(solution)/shard_map/all_to_all | solution.py:398
  136.7 25.3 %collective-permute-start.18 = (bf16[4,256,512]{2,1,0:T(8,128)(2,1)}, bf16[4,256,512]{2,1,0:T(8,128)(2,1)}, u32[]{:S(2)}, u32[]{:S(2)}) collective-permute-start(bf16[4,256,512]{2,1,0:T(8,128)(2,1)} %all-to-all-done.gate_a), channel_id=1, source_target_pairs={{0,4},{4,0},{1,5},{5,1},{2,6},{6,2},{3,7},{7,3},{8,12},{12,8},{9,1... | collective-permute-start | bytes 3145736 | tf_op jit(solution)/shard_map/ppermute | solution.py:251
  170.4 31.0 %all-to-all-start.2 = ((bf16[4,256,512]{2,1,0:T(8,128)(2,1)}), bf16[4,256,512]{2,1,0:T(8,128)(2,1)}, u32[]{:S(2)}, u32[]{:S(2)}) async-start(bf16[4,256,512]{2,1,0:T(8,128)(2,1)} %get-tuple-element.81), calls=%async_computation.2 | async-start | bytes 2097152 | tf_op jit(solution)/shard_map/all_to_all | solution.py:398
  175.1 364.4 %reduce-scatter.5.cloned.1.call-start = ((), (), s32[]{:S(2)}) async-start(), calls=%async_computation.11 | async-start | bytes 3145728 | tf_op jit(solution)/shard_map/reduce_scatter | solution.py:581
  186.0 16.7 %collective-permute-start.21 = (bf16[128,2048]{1,0:T(8,128)(2,1)S(1)}, bf16[128,2048]{1,0:T(8,128)(2,1)}, u32[]{:S(2)}, u32[]{:S(2)}) collective-permute-start(bf16[128,2048]{1,0:T(8,128)(2,1)S(1)} %fusion.74), channel_id=1, source_target_pairs={{0,2},{1,3},{2,0},{3,1},{4,6},{5,7},{6,4},{7,5},{8,10},{9,11},{10,... | collective-permute-start | bytes 1572872 | tf_op jit(solution)/shard_map/ppermute | solution.py:251
  187.6 29.7 %collective-permute-start.23 = (bf16[4,256,512]{2,1,0:T(8,128)(2,1)}, bf16[4,256,512]{2,1,0:T(8,128)(2,1)}, u32[]{:S(2)}, u32[]{:S(2)}) collective-permute-start(bf16[4,256,512]{2,1,0:T(8,128)(2,1)} %all-to-all-done.1.up_a), channel_id=1, source_target_pairs={{0,4},{4,0},{1,5},{5,1},{2,6},{6,2},{3,7},{7,3},{8,12},{12,8},{9,1... | collective-permute-start | bytes 3145736 | tf_op jit(solution)/shard_map/ppermute | solution.py:251
  201.4 33.2 %collective-permute-start.24 = (bf16[4,256,512]{2,1,0:T(8,128)(2,1)}, bf16[4,256,512]{2,1,0:T(8,128)(2,1)}, u32[]{:S(2)}, u32[]{:S(2)}) collective-permute-start(bf16[4,256,512]{2,1,0:T(8,128)(2,1)} %all-to-all-done.2.own_ref), channel_id=1, source_target_pairs={{0,4},{4,0},{1,5},{5,1},{2,6},{6,2},{3,7},{7,3},{8,12},{12,8},{9,1... | collective-permute-start | bytes 3145736 | tf_op jit(solution)/shard_map/ppermute | solution.py:251
  204.0 40.7 %collective-permute-start.22 = (bf16[256,2048]{1,0:T(8,128)(2,1)S(1)}, bf16[256,2048]{1,0:T(8,128)(2,1)}, u32[]{:S(2)}, u32[]{:S(2)}) collective-permute-start(bf16[256,2048]{1,0:T(8,128)(2,1)S(1)} %pad_maximum_fusion.7), channel_id=1, source_target_pairs={{0,1},{1,0},{2,3},{3,2},{4,5},{5,4},{6,7},{7,6},{8,9},{9,8},{10,11... | collective-permute-start | bytes 3145736 | tf_op jit(solution)/shard_map/ppermute | solution.py:251
  213.9 24.4 %collective-permute-start.28 = (bf16[128,2048]{1,0:T(8,128)(2,1)S(1)}, bf16[128,2048]{1,0:T(8,128)(2,1)S(1)}, u32[]{:S(2)}, u32[]{:S(2)}) collective-permute-start(bf16[128,2048]{1,0:T(8,128)(2,1)S(1)} %collective-permute-done.27), channel_id=1, source_target_pairs={{0,2},{1,3},{2,0},{3,1},{4,6},{5,7},{6,4},{7,5},{8,10},{9,11},{10,... | collective-permute-start | bytes 1572872 | tf_op jit(solution)/shard_map/ppermute | solution.py:251
  214.5 24.7 %collective-permute-start.33 = (bf16[128,2048]{1,0:T(8,128)(2,1)S(1)}, bf16[128,2048]{1,0:T(8,128)(2,1)}, u32[]{:S(2)}, u32[]{:S(2)}) collective-permute-start(bf16[128,2048]{1,0:T(8,128)(2,1)S(1)} %collective-permute-done.27), channel_id=1, source_target_pairs={{0,24},{8,0},{16,8},{24,16},{1,25},{9,1},{17,9},{25,17},{2,26},{10... | collective-permute-start | bytes 1572872 | tf_op jit(solution)/shard_map/ppermute | solution.py:264
  239.1 20.0 %collective-permute-start.29 = (bf16[256,2048]{1,0:T(8,128)(2,1)}, bf16[256,2048]{1,0:T(8,128)(2,1)S(1)}, u32[]{:S(2)}, u32[]{:S(2)}) collective-permute-start(bf16[256,2048]{1,0:T(8,128)(2,1)} %constant_dynamic-update-slice_fusion.5), channel_id=1, source_target_pairs={{0,1},{1,0},{2,3},{3,2},{4,5},{5,4},{6,7},{7,6},{8,9},{9,8},{10,11... | collective-permute-start | bytes 3145736 | tf_op jit(solution)/shard_map/ppermute | solution.py:251
  239.1 17.8 %collective-permute-start.34 = (bf16[128,2048]{1,0:T(8,128)(2,1)}, bf16[128,2048]{1,0:T(8,128)(2,1)S(1)}, u32[]{:S(2)}, u32[]{:S(2)}) collective-permute-start(bf16[128,2048]{1,0:T(8,128)(2,1)} %collective-permute-done.33), channel_id=1, source_target_pairs={{0,2},{1,3},{2,0},{3,1},{4,6},{5,7},{6,4},{7,5},{8,10},{9,11},{10,... | collective-permute-start | bytes 1572872 | tf_op jit(solution)/shard_map/ppermute | solution.py:251
  239.6 17.9 %collective-permute-start.39 = (bf16[128,2048]{1,0:T(8,128)(2,1)}, bf16[128,2048]{1,0:T(8,128)(2,1)S(1)}, u32[]{:S(2)}, u32[]{:S(2)}) collective-permute-start(bf16[128,2048]{1,0:T(8,128)(2,1)} %collective-permute-done.33), channel_id=1, source_target_pairs={{0,24},{8,0},{16,8},{24,16},{1,25},{9,1},{17,9},{25,17},{2,26},{10... | collective-permute-start | bytes 1572872 | tf_op jit(solution)/shard_map/ppermute | solution.py:264
  255.4 25.5 %collective-permute-start.25 = (bf16[256,2048]{1,0:T(8,128)(2,1)S(1)}, bf16[256,2048]{1,0:T(8,128)(2,1)S(1)}, u32[]{:S(2)}, u32[]{:S(2)}) collective-permute-start(bf16[256,2048]{1,0:T(8,128)(2,1)S(1)} %convolution_convert_fusion.7), channel_id=1, source_target_pairs={{0,1},{1,0},{2,3},{3,2},{4,5},{5,4},{6,7},{7,6},{8,9},{9,8},{10,11... | collective-permute-start | bytes 3145736 | tf_op jit(solution)/shard_map/ppermute | solution.py:251
  263.0 21.4 %collective-permute-start.30 = (bf16[256,2048]{1,0:T(8,128)(2,1)S(1)}, bf16[256,2048]{1,0:T(8,128)(2,1)S(1)}, u32[]{:S(2)}, u32[]{:S(2)}) collective-permute-start(bf16[256,2048]{1,0:T(8,128)(2,1)S(1)} %convolution_convert_fusion.6), channel_id=1, source_target_pairs={{0,1},{1,0},{2,3},{3,2},{4,5},{5,4},{6,7},{7,6},{8,9},{9,8},{10,11... | collective-permute-start | bytes 3145736 | tf_op jit(solution)/shard_map/ppermute | solution.py:251
  282.8 52.7 %collective-permute-start.26 = (bf16[128,2048]{1,0:T(8,128)(2,1)}, bf16[128,2048]{1,0:T(8,128)(2,1)}, u32[]{:S(2)}, u32[]{:S(2)}) collective-permute-start(bf16[128,2048]{1,0:T(8,128)(2,1)} %slice.692), channel_id=1, source_target_pairs={{0,2},{1,3},{2,0},{3,1},{4,6},{5,7},{6,4},{7,5},{8,10},{9,11},{10,... | collective-permute-start | bytes 1572872 | tf_op jit(solution)/shard_map/ppermute | solution.py:251
  285.1 23.8 %collective-permute-start.31 = (bf16[128,2048]{1,0:T(8,128)(2,1)S(1)}, bf16[128,2048]{1,0:T(8,128)(2,1)S(1)}, u32[]{:S(2)}, u32[]{:S(2)}) collective-permute-start(bf16[128,2048]{1,0:T(8,128)(2,1)S(1)} %slice.691), channel_id=1, source_target_pairs={{0,2},{1,3},{2,0},{3,1},{4,6},{5,7},{6,4},{7,5},{8,10},{9,11},{10,... | collective-permute-start | bytes 1572872 | tf_op jit(solution)/shard_map/ppermute | solution.py:251
  286.5 33.7 %collective-permute-start.37 = (bf16[128,2048]{1,0:T(8,128)(2,1)S(1)}, bf16[128,2048]{1,0:T(8,128)(2,1)S(1)}, u32[]{:S(2)}, u32[]{:S(2)}) collective-permute-start(bf16[128,2048]{1,0:T(8,128)(2,1)S(1)} %slice.690), channel_id=1, source_target_pairs={{0,2},{1,3},{2,0},{3,1},{4,6},{5,7},{6,4},{7,5},{8,10},{9,11},{10,... | collective-permute-start | bytes 1572872 | tf_op jit(solution)/shard_map/ppermute | solution.py:251
  288.9 42.1 %collective-permute-start.43 = (bf16[128,2048]{1,0:T(8,128)(2,1)S(1)}, bf16[128,2048]{1,0:T(8,128)(2,1)S(1)}, u32[]{:S(2)}, u32[]{:S(2)}) collective-permute-start(bf16[128,2048]{1,0:T(8,128)(2,1)S(1)} %slice.689), channel_id=1, source_target_pairs={{0,2},{1,3},{2,0},{3,1},{4,6},{5,7},{6,4},{7,5},{8,10},{9,11},{10,... | collective-permute-start | bytes 1572872 | tf_op jit(solution)/shard_map/ppermute | solution.py:251
  309.9 25.6 %collective-permute-start.32 = (bf16[128,2048]{1,0:T(8,128)(2,1)}, bf16[128,2048]{1,0:T(8,128)(2,1)}, u32[]{:S(2)}, u32[]{:S(2)}) collective-permute-start(bf16[128,2048]{1,0:T(8,128)(2,1)} %fusion.69), channel_id=1, source_target_pairs={{0,8},{8,16},{16,24},{24,0},{1,9},{9,17},{17,25},{25,1},{2,10},{10... | collective-permute-start | bytes 1572872 | tf_op jit(solution)/shard_map/ppermute | solution.py:264
  321.1 26.6 %collective-permute-start.38 = (bf16[128,2048]{1,0:T(8,128)(2,1)}, bf16[128,2048]{1,0:T(8,128)(2,1)}, u32[]{:S(2)}, u32[]{:S(2)}) collective-permute-start(bf16[128,2048]{1,0:T(8,128)(2,1)} %fusion.68), channel_id=1, source_target_pairs={{0,16},{8,24},{16,0},{24,8},{1,17},{9,25},{17,1},{25,9},{2,18},{10... | collective-permute-start | bytes 1572872 | tf_op jit(solution)/shard_map/ppermute | solution.py:264
  331.9 25.0 %collective-permute-start.44 = (bf16[128,2048]{1,0:T(8,128)(2,1)}, bf16[128,2048]{1,0:T(8,128)(2,1)}, u32[]{:S(2)}, u32[]{:S(2)}) collective-permute-start(bf16[128,2048]{1,0:T(8,128)(2,1)} %fusion.67), channel_id=1, source_target_pairs={{0,24},{8,0},{16,8},{24,16},{1,25},{9,1},{17,9},{25,17},{2,26},{10... | collective-permute-start | bytes 1572872 | tf_op jit(solution)/shard_map/ppermute | solution.py:264
  335.1 24.2 %collective-permute-start.45 = (bf16[128,2048]{1,0:T(8,128)(2,1)S(1)}, bf16[128,2048]{1,0:T(8,128)(2,1)S(1)}, u32[]{:S(2)}, u32[]{:S(2)}) collective-permute-start(bf16[128,2048]{1,0:T(8,128)(2,1)S(1)} %dynamic-slice_bitcast_fusion.3), channel_id=1, source_target_pairs={{0,4},{4,0},{1,5},{5,1},{2,6},{6,2},{3,7},{7,3},{8,12},{12,8},{9,1... | collective-permute-start | bytes 1572872 | tf_op jit(solution)/shard_map/ppermute | solution.py:251
  375.3 22.2 %collective-permute-start.47 = (bf16[256,2048]{1,0:T(8,128)(2,1)S(1)}, bf16[256,2048]{1,0:T(8,128)(2,1)S(1)}, u32[]{:S(2)}, u32[]{:S(2)}) collective-permute-start(bf16[256,2048]{1,0:T(8,128)(2,1)S(1)} %pad_maximum_fusion.8), channel_id=1, source_target_pairs={{0,1},{1,0},{2,3},{3,2},{4,5},{5,4},{6,7},{7,6},{8,9},{9,8},{10,11... | collective-permute-start | bytes 3145736 | tf_op jit(solution)/shard_map/ppermute | solution.py:251
  391.0 17.0 %collective-permute-start.52 = (bf16[256,2048]{1,0:T(8,128)(2,1)S(1)}, bf16[256,2048]{1,0:T(8,128)(2,1)S(1)}, u32[]{:S(2)}, u32[]{:S(2)}) collective-permute-start(bf16[256,2048]{1,0:T(8,128)(2,1)S(1)} %constant_dynamic-update-slice_fusion.11), channel_id=1, source_target_pairs={{0,1},{1,0},{2,3},{3,2},{4,5},{5,4},{6,7},{7,6},{8,9},{9,8},{10,11... | collective-permute-start | bytes 3145736 | tf_op jit(solution)/shard_map/ppermute | solution.py:251
  392.5 15.2 %collective-permute-start.57 = (bf16[128,2048]{1,0:T(8,128)(2,1)S(1)}, bf16[128,2048]{1,0:T(8,128)(2,1)S(1)}, u32[]{:S(2)}, u32[]{:S(2)}) collective-permute-start(bf16[128,2048]{1,0:T(8,128)(2,1)S(1)} %collective-permute-done.56), channel_id=1, source_target_pairs={{0,2},{1,3},{2,0},{3,1},{4,6},{5,7},{6,4},{7,5},{8,10},{9,11},{10,... | collective-permute-start | bytes 1572872 | tf_op jit(solution)/shard_map/ppermute | solution.py:251
  401.2 33.1 %collective-permute-start.48 = (bf16[256,2048]{1,0:T(8,128)(2,1)S(1)}, bf16[256,2048]{1,0:T(8,128)(2,1)S(1)}, u32[]{:S(2)}, u32[]{:S(2)}) collective-permute-start(bf16[256,2048]{1,0:T(8,128)(2,1)S(1)} %convolution_convert_fusion.12), channel_id=1, source_target_pairs={{0,1},{1,0},{2,3},{3,2},{4,5},{5,4},{6,7},{7,6},{8,9},{9,8},{10,11... | collective-permute-start | bytes 3145736 | tf_op jit(solution)/shard_map/ppermute | solution.py:251
  407.7 15.9 %collective-permute-start.58 = (bf16[256,2048]{1,0:T(8,128)(2,1)S(1)}, bf16[256,2048]{1,0:T(8,128)(2,1)S(1)}, u32[]{:S(2)}, u32[]{:S(2)}) collective-permute-start(bf16[256,2048]{1,0:T(8,128)(2,1)S(1)} %constant_dynamic-update-slice_fusion.13), channel_id=1, source_target_pairs={{0,1},{1,0},{2,3},{3,2},{4,5},{5,4},{6,7},{7,6},{8,9},{9,8},{10,11... | collective-permute-start | bytes 3145736 | tf_op jit(solution)/shard_map/ppermute | solution.py:251
  453.8 143.1 %reduce-scatter.7.cloned.1.call-start = ((), (), s32[]{:S(2)}) async-start(), calls=%async_computation.12 | async-start | bytes 6291456 | tf_op jit(solution)/shard_map/reduce_scatter | solution.py:584
  470.8 15.1 %collective-permute-start.54 = (bf16[128,2048]{1,0:T(8,128)(2,1)}, bf16[128,2048]{1,0:T(8,128)(2,1)S(1)}, u32[]{:S(2)}, u32[]{:S(2)}) collective-permute-start(bf16[128,2048]{1,0:T(8,128)(2,1)} %slice.687), channel_id=1, source_target_pairs={{0,2},{1,3},{2,0},{3,1},{4,6},{5,7},{6,4},{7,5},{8,10},{9,11},{10,... | collective-permute-start | bytes 1572872 | tf_op jit(solution)/shard_map/ppermute | solution.py:251
  470.9 26.2 %collective-permute-start.60 = (bf16[128,2048]{1,0:T(8,128)(2,1)}, bf16[128,2048]{1,0:T(8,128)(2,1)S(1)}, u32[]{:S(2)}, u32[]{:S(2)}) collective-permute-start(bf16[128,2048]{1,0:T(8,128)(2,1)} %slice.686), channel_id=1, source_target_pairs={{0,2},{1,3},{2,0},{3,1},{4,6},{5,7},{6,4},{7,5},{8,10},{9,11},{10,... | collective-permute-start | bytes 1572872 | tf_op jit(solution)/shard_map/ppermute | solution.py:251
  472.9 47.0 %collective-permute-start.49 = (bf16[128,2048]{1,0:T(8,128)(2,1)}, bf16[128,2048]{1,0:T(8,128)(2,1)S(1)}, u32[]{:S(2)}, u32[]{:S(2)}) collective-permute-start(bf16[128,2048]{1,0:T(8,128)(2,1)} %slice.688), channel_id=1, source_target_pairs={{0,2},{1,3},{2,0},{3,1},{4,6},{5,7},{6,4},{7,5},{8,10},{9,11},{10,... | collective-permute-start | bytes 1572872 | tf_op jit(solution)/shard_map/ppermute | solution.py:251
  473.0 45.8 %collective-permute-start.66 = (bf16[128,2048]{1,0:T(8,128)(2,1)}, bf16[128,2048]{1,0:T(8,128)(2,1)S(1)}, u32[]{:S(2)}, u32[]{:S(2)}) collective-permute-start(bf16[128,2048]{1,0:T(8,128)(2,1)} %slice.685), channel_id=1, source_target_pairs={{0,2},{1,3},{2,0},{3,1},{4,6},{5,7},{6,4},{7,5},{8,10},{9,11},{10,... | collective-permute-start | bytes 1572872 | tf_op jit(solution)/shard_map/ppermute | solution.py:251
  487.2 32.6 %collective-permute-start.55 = (bf16[128,2048]{1,0:T(8,128)(2,1)S(1)}, bf16[128,2048]{1,0:T(8,128)(2,1)S(1)}, u32[]{:S(2)}, u32[]{:S(2)}) collective-permute-start(bf16[128,2048]{1,0:T(8,128)(2,1)S(1)} %fusion.63), channel_id=1, source_target_pairs={{0,8},{8,16},{16,24},{24,0},{1,9},{9,17},{17,25},{25,1},{2,10},{10... | collective-permute-start | bytes 1572872 | tf_op jit(solution)/shard_map/ppermute | solution.py:264
  497.2 26.7 %collective-permute-start.61 = (bf16[128,2048]{1,0:T(8,128)(2,1)S(1)}, bf16[128,2048]{1,0:T(8,128)(2,1)S(1)}, u32[]{:S(2)}, u32[]{:S(2)}) collective-permute-start(bf16[128,2048]{1,0:T(8,128)(2,1)S(1)} %fusion.62), channel_id=1, source_target_pairs={{0,16},{8,24},{16,0},{24,8},{1,17},{9,25},{17,1},{25,9},{2,18},{10... | collective-permute-start | bytes 1572872 | tf_op jit(solution)/shard_map/ppermute | solution.py:264
  518.9 16.2 %collective-permute-start.67 = (bf16[128,2048]{1,0:T(8,128)(2,1)S(1)}, bf16[128,2048]{1,0:T(8,128)(2,1)S(1)}, u32[]{:S(2)}, u32[]{:S(2)}) collective-permute-start(bf16[128,2048]{1,0:T(8,128)(2,1)S(1)} %fusion.61), channel_id=1, source_target_pairs={{0,24},{8,0},{16,8},{24,16},{1,25},{9,1},{17,9},{25,17},{2,26},{10... | collective-permute-start | bytes 1572872 | tf_op jit(solution)/shard_map/ppermute | solution.py:264
  554.5 42.4 %all-to-all-start.3 = ((bf16[4,256,512]{2,1,0:T(8,128)(2,1)}), bf16[4,256,512]{2,1,0:T(8,128)(2,1)}, u32[]{:S(2)}, u32[]{:S(2)}) async-start(bf16[4,256,512]{2,1,0:T(8,128)(2,1)} %bitcast.18), calls=%async_computation.4 | async-start | bytes 2097152 | tf_op jit(solution)/shard_map/all_to_all | solution.py:398
  558.8 179.8 %reduce-scatter.9.cloned.1.call-start = ((), (), s32[]{:S(2)}) async-start(), calls=%async_computation.13 | async-start | bytes 2621440 | tf_op jit(solution)/shard_map/reduce_scatter | solution.py:659
  572.9 165.7 %reduce-scatter.11.cloned.1.call-start = ((), (), s32[]{:S(2)}) async-start(), calls=%async_computation.14 | async-start | bytes 2621440 | tf_op jit(solution)/shard_map/reduce_scatter | solution.py:659
  630.8 85.6 %all-to-all-start.4 = ((bf16[4,256,1024]{2,1,0:T(8,128)(2,1)}), bf16[4,256,1024]{2,1,0:T(8,128)(2,1)S(1)}, u32[]{:S(2)}, u32[]{:S(2)}) async-start(bf16[4,256,1024]{2,1,0:T(8,128)(2,1)} %bitcast.164), calls=%async_computation.8 | async-start | bytes 4194304 | tf_op jit(solution)/shard_map/all_to_all | solution.py:398
  641.6 53.0 %collective-permute-start.77 = (bf16[4,256,512]{2,1,0:T(8,128)(2,1)}, bf16[4,256,512]{2,1,0:T(8,128)(2,1)}, u32[]{:S(2)}, u32[]{:S(2)}) collective-permute-start(bf16[4,256,512]{2,1,0:T(8,128)(2,1)} %dynamic-slice_bitcast_fusion.1), channel_id=1, source_target_pairs={{0,4},{4,0},{1,5},{5,1},{2,6},{6,2},{3,7},{7,3},{8,12},{12,8},{9,1... | collective-permute-start | bytes 3145736 | tf_op jit(solution)/shard_map/ppermute | solution.py:251
  641.6 48.8 %collective-permute-start.78 = (bf16[4,256,512]{2,1,0:T(8,128)(2,1)}, bf16[4,256,512]{2,1,0:T(8,128)(2,1)}, u32[]{:S(2)}, u32[]{:S(2)}) collective-permute-start(bf16[4,256,512]{2,1,0:T(8,128)(2,1)} %all-to-all-done.3.own_ref), channel_id=1, source_target_pairs={{0,4},{4,0},{1,5},{5,1},{2,6},{6,2},{3,7},{7,3},{8,12},{12,8},{9,1... | collective-permute-start | bytes 3145736 | tf_op jit(solution)/shard_map/ppermute | solution.py:251
  656.8 63.9 %collective-permute-start.72 = (bf16[2,128,2048]{2,1,0:T(8,128)(2,1)}, bf16[2,128,2048]{2,1,0:T(8,128)(2,1)}, u32[]{:S(2)}, u32[]{:S(2)}) collective-permute-start(bf16[2,128,2048]{2,1,0:T(8,128)(2,1)} %pad_maximum_fusion.11), channel_id=1, source_target_pairs={{2,4},{4,2},{3,5},{5,3},{10,12},{12,10},{11,13},{13,11},{18,20},{2... | collective-permute-start | bytes 3145736 | tf_op jit(solution)/shard_map/ppermute | solution.py:553
  658.5 77.4 %collective-permute-start.75 = (bf16[4,272,512]{2,1,0:T(8,128)(2,1)}, bf16[4,272,512]{2,1,0:T(8,128)(2,1)}, u32[]{:S(2)}, u32[]{:S(2)}) collective-permute-start(bf16[4,272,512]{2,1,0:T(8,128)(2,1)} %pad_maximum_fusion.1), channel_id=1, source_target_pairs={{0,4},{4,0},{1,5},{5,1},{2,6},{6,2},{3,7},{7,3},{8,12},{12,8},{9,1... | collective-permute-start | bytes 3342344 | tf_op jit(solution)/shard_map/ppermute | solution.py:251
  716.4 30.5 %all-to-all-start.6 = ((bf16[4,256,512]{2,1,0:T(8,128)(2,1)}), bf16[4,256,512]{2,1,0:T(8,128)(2,1)}, u32[]{:S(2)}, u32[]{:S(2)}) async-start(bf16[4,256,512]{2,1,0:T(8,128)(2,1)} %fusion.25), calls=%async_computation.10 | async-start | bytes 2097152 | tf_op jit(solution)/shard_map/all_to_all | solution.py:398
  723.0 27.8 %collective-permute-start.73 = (bf16[2,128,2048]{2,1,0:T(8,128)(2,1)}, bf16[2,128,2048]{2,1,0:T(8,128)(2,1)}, u32[]{:S(2)}, u32[]{:S(2)}) collective-permute-start(bf16[2,128,2048]{2,1,0:T(8,128)(2,1)} %broadcast_select_fusion.1), channel_id=1, source_target_pairs={{0,2},{1,3},{2,0},{3,1},{4,6},{5,7},{6,4},{7,5},{8,10},{9,11},{10,... | collective-permute-start | bytes 3145736 | tf_op jit(solution)/shard_map/ppermute | solution.py:251
  738.6 63.9 %collective-permute-start.79 = (bf16[4,256,1024]{2,1,0:T(8,128)(2,1)S(1)}, bf16[4,256,1024]{2,1,0:T(8,128)(2,1)}, u32[]{:S(2)}, u32[]{:S(2)}) collective-permute-start(bf16[4,256,1024]{2,1,0:T(8,128)(2,1)S(1)} %all-to-all-done.4.own_ref), channel_id=1, source_target_pairs={{0,4},{4,0},{1,5},{5,1},{2,6},{6,2},{3,7},{7,3},{8,12},{12,8},{9,1... | collective-permute-start | bytes 6291464 | tf_op jit(solution)/shard_map/ppermute | solution.py:251
  747.0 30.3 %all-to-all-start.5 = ((bf16[4,272,512]{2,1,0:T(8,128)(2,1)}), bf16[4,272,512]{2,1,0:T(8,128)(2,1)S(1)}, u32[]{:S(2)}, u32[]{:S(2)}) async-start(bf16[4,272,512]{2,1,0:T(8,128)(2,1)} %add_convert_fusion), calls=%async_computation.9 | async-start | bytes 2228224 | tf_op jit(solution)/shard_map/all_to_all | solution.py:398
  750.5 63.5 %all-reduce.6.cloned.1.call-start = ((), (), s32[]{:S(2)}) async-start(), calls=%async_computation.15 | async-start | bytes 2097152 | tf_op jit(solution)/shard_map/psum | solution.py:700
  754.1 69.3 %collective-permute-start.74 = (bf16[2,2,128,2048]{3,2,0,1:T(8,128)(2,1)}, bf16[2,2,128,2048]{3,2,0,1:T(8,128)(2,1)}, u32[]{:S(2)}, u32[]{:S(2)}) collective-permute-start(bf16[2,2,128,2048]{3,2,0,1:T(8,128)(2,1)} %maximum_select_fusion.1), channel_id=1, source_target_pairs={{0,1},{1,0},{2,3},{3,2},{4,5},{5,4},{6,7},{7,6},{8,9},{9,8},{10,11... | collective-permute-start | bytes 6291464 | tf_op jit(solution)/shard_map/ppermute | solution.py:251
  777.5 38.1 %collective-permute-start.76 = (bf16[256,512]{1,0:T(8,128)(2,1)S(1)}, bf16[256,512]{1,0:T(8,128)(2,1)S(1)}, u32[]{:S(2)}, u32[]{:S(2)}) collective-permute-start(bf16[256,512]{1,0:T(8,128)(2,1)S(1)} %slice.694), channel_id=1, source_target_pairs={{0,4},{4,0},{1,5},{5,1},{2,6},{6,2},{3,7},{7,3},{8,12},{12,8},{9,1... | collective-permute-start | bytes 786440 | tf_op jit(solution)/shard_map/ppermute | solution.py:251
  (137 other events, 1298.2 us)
Sparse Core Ops, SparseCore 0:
  454.0 30.3 reduce-scatter.4
  487.3 54.2 reduce-scatter.6
  573.0 46.9 reduce-scatter.8
  631.0 73.2 reduce-scatter.10
  754.3 59.6 all-reduce.5

commit v3 on v2

--- a/solution.py
+++ b/solution.py
@@ -471,20 +471,22 @@
             for _ in range(1, fsdp):
                 moved.append(shift(moved[-1], 1))
             groups = []
-            earlier = None
+            done = []
             for g in range(0, fsdp, group_size):
                 group = jnp.zeros((group_size * length, D), LOW)
                 for r in range(group_size):
                     second = flip(moved[g + r], "tp", 2, tp)
                     both = jnp.concatenate([moved[g + r], second], axis=0)
                     third = flip(both, "tp", 1, tp)
-                    if earlier is not None:
-                        third = after(third, earlier)
+                    if done:
+                        third = after(third, done[-1][0])
+                    if len(done) > 1:
+                        third = after(third, done[-2][1])
                     group = lax.dynamic_update_slice(group, both, (r * length, 0))
                     group = lax.dynamic_update_slice(
                         group, third, (r * length + length // 2, 0)
                     )
-                    earlier = work(group[r * length : (r + 1) * length], g + r)
+                    done.append(work(group[r * length : (r + 1) * length], g + r))
                 groups.append(group)
             return groups
 
@@ -498,7 +500,7 @@
             down_parts.append((kept, again))
             wide_chunks.append(wide)
             active_chunks.append(active)
-            return sent
+            return sent, again
 
         hidden_all = in_chunks(hidden_low, forward)
         down = to_owner(down_parts)
@@ -541,7 +543,7 @@
             hidden_parts.append((kept, again))
             last_sent.append(sent_again)
             wide_lows.append(wide_low)
-            return sent
+            return sent, again
 
         grad_all = in_chunks(down_low, backward)
 

time: 849 us -> 846 us (level)
    unnamed x239 -> x247, local copies, waits for them, and re-layouts: 27.7 us -> 26.7 us
  transfers between devices with their start and end apart: 93 -> 93, of which waited for: 41 -> 45; matrix products, arithmetic and copies ran while one was open for 24% -> 24% of each run, Pallas kernels for 4% -> 4%
where the time goes in v3:
time: 846 us; the launch traced here: 836 us
  waiting for transfers between devices  410 us (48%)
  starting transfers between devices  114 us (13%)
  matrix products  87.7 us (10%)
  local copies, waits for them, and re-layouts  81.8 us (10%)
  other arithmetic  65 us (8%)
  Pallas kernels  43.4 us (5%)
  blocking collectives  16.9 us (2%)
  between operations  16.8 us (2%)
    ppermute x59, waiting for transfers between devices, flip(): lax.ppermute(value, axis, [(place, place ^ bit) for place in range(size)])  251 us
    ppermute x21, waiting for transfers between devices, shift(): lax.ppermute(value, 'fsdp', [(place, (place - step) % fsdp) for place in...  82.8 us
    all_to_all x7, waiting for transfers between devices, exchange(): return lax.all_to_all(value, 'fsdp', 0, 0, tiled=True)  70.6 us
    ppermute x59, starting transfers between devices, flip(): lax.ppermute(value, axis, [(place, place ^ bit) for place in range(size)])  43.8 us
    ppermute x21, starting transfers between devices, shift(): lax.ppermute(value, 'fsdp', [(place, (place - step) % fsdp) for place in...  35.4 us
    all_to_all x7, starting transfers between devices, exchange(): return lax.all_to_all(value, 'fsdp', 0, 0, tiled=True)  32.9 us
    dot_general x15, matrix products, product(): return jnp.dot(left_side, right_side, preferred_element_type=WIDE)  30.7 us
    dot_general x18, matrix products, product_back(): lax.dot_general(left_side, right_side, (((1,), (1,)), ((), ())), preferre...  30.5 us
  transfers between devices with their start and end apart: 93, of which 45 were waited for; matrix products, arithmetic and copies ran while one was open for 24% of the time, Pallas kernels for 4%

profile of v3, /device:TPU:0, one launch (start us, length us, event | category | flops | bytes accessed | tf_op | source)
XLA Modules:
  0.0 836.3 jit_solution(14463746740734190343)
XLA Ops:
  25.2 8.7 %collective-permute-done.4 = bf16[256,1024]{1,0:T(8,128)(2,1)} collective-permute-done((bf16[256,1024]{1,0:T(8,128)(2,1)S(1)}, bf16[256,1024]{1,0:T(8,128)(2,1)}, u32[]{:S(2)}, u32[]{:S(2)}) %collective-permute-start.4) | collective-permute-done | bytes 524320 | tf_op jit(solution)/shard_map/ppermute | solution.py:264
  36.2 9.0 %collective-permute-done = bf16[256,1024]{1,0:T(8,128)(2,1)} collective-permute-done((bf16[256,1024]{1,0:T(8,128)(2,1)}, bf16[256,1024]{1,0:T(8,128)(2,1)}, u32[]{:S(2)}, u32[]{:S(2)}) %collective-permute-start) | collective-permute-done | bytes 524320 | tf_op jit(solution)/shard_map/ppermute | solution.py:264
  61.5 4.1 shard_map.237
  88.1 4.3 all-to-all-start
  104.4 7.1 collective-permute-done.17
  112.4 4.5 fusion.169
  117.2 5.7 psum.28
  124.7 4.3 fusion.42
  129.1 4.5 all-to-all-start.1
  142.3 19.7 %collective-permute-done.18.gate_b = bf16[4,256,512]{2,1,0:T(8,128)(2,1)} collective-permute-done((bf16[4,256,512]{2,1,0:T(8,128)(2,1)}, bf16[4,256,512]{2,1,0:T(8,128)(2,1)}, u32[]{:S(2)}, u32[]{:S(2)}) %collective-permute-start.18) | collective-permute-done | bytes 1048608 | tf_op jit(solution)/shard_map/ppermute | solution.py:251
  170.4 4.8 all-to-all-start.2
  175.8 7.1 collective-permute-done.20
  187.9 13.5 %all-to-all-done.2.own_ref = bf16[4,256,512]{2,1,0:T(8,128)(2,1)} async-done(((bf16[4,256,512]{2,1,0:T(8,128)(2,1)}), bf16[4,256,512]{2,1,0:T(8,128)(2,1)}, u32[]{:S(2)}, u32[]{:S(2)}) %all-to-all-start.2) | async-done | bytes 1048608 | tf_op jit(solution)/shard_map/all_to_all | solution.py:398
  204.1 9.9 %collective-permute-done.27 = bf16[128,2048]{1,0:T(8,128)(2,1)S(1)} collective-permute-done((bf16[128,2048]{1,0:T(8,128)(2,1)S(1)}, bf16[128,2048]{1,0:T(8,128)(2,1)S(1)}, u32[]{:S(2)}, u32[]{:S(2)}) %collective-permute-start.27) | collective-permute-done | bytes 524320 | tf_op jit(solution)/shard_map/ppermute | solution.py:264
  217.4 4.7 shard_map.238
  222.0 4.5 dynamic_update_slice.104
  227.3 7.2 collective-permute-done.24.other_ref
  234.5 3.8 shard_map.239
  239.6 4.0 collective-permute-start.39
  247.0 5.3 fusion.23
  264.5 7.8 collective-permute-done.40
  272.5 10.2 %collective-permute-done.26 = bf16[128,2048]{1,0:T(8,128)(2,1)S(1)} collective-permute-done((bf16[128,2048]{1,0:T(8,128)(2,1)S(1)}, bf16[128,2048]{1,0:T(8,128)(2,1)S(1)}, u32[]{:S(2)}, u32[]{:S(2)}) %collective-permute-start.26) | collective-permute-done | bytes 524320 | tf_op jit(solution)/shard_map/ppermute | solution.py:251
  288.9 10.3 %collective-permute-done.31 = bf16[128,2048]{1,0:T(8,128)(2,1)S(1)} collective-permute-done((bf16[128,2048]{1,0:T(8,128)(2,1)S(1)}, bf16[128,2048]{1,0:T(8,128)(2,1)S(1)}, u32[]{:S(2)}, u32[]{:S(2)}) %collective-permute-start.31) | collective-permute-done | bytes 524320 | tf_op jit(solution)/shard_map/ppermute | solution.py:251
  310.1 9.6 %collective-permute-done.37 = bf16[128,2048]{1,0:T(8,128)(2,1)S(1)} collective-permute-done((bf16[128,2048]{1,0:T(8,128)(2,1)S(1)}, bf16[128,2048]{1,0:T(8,128)(2,1)S(1)}, u32[]{:S(2)}, u32[]{:S(2)}) %collective-permute-start.37) | collective-permute-done | bytes 524320 | tf_op jit(solution)/shard_map/ppermute | solution.py:251
  320.6 9.9 %collective-permute-done.43 = bf16[128,2048]{1,0:T(8,128)(2,1)S(1)} collective-permute-done((bf16[128,2048]{1,0:T(8,128)(2,1)S(1)}, bf16[128,2048]{1,0:T(8,128)(2,1)S(1)}, u32[]{:S(2)}, u32[]{:S(2)}) %collective-permute-start.43) | collective-permute-done | bytes 524320 | tf_op jit(solution)/shard_map/ppermute | solution.py:251
  334.2 14.2 %collective-permute-done.38 = bf16[128,2048]{1,0:T(8,128)(2,1)} collective-permute-done((bf16[128,2048]{1,0:T(8,128)(2,1)}, bf16[128,2048]{1,0:T(8,128)(2,1)}, u32[]{:S(2)}, u32[]{:S(2)}) %collective-permute-start.38) | collective-permute-done | bytes 524320 | tf_op jit(solution)/shard_map/ppermute | solution.py:264
  348.5 8.0 collective-permute-done.44
  364.9 9.4 %collective-permute-done.46 = bf16[128,2048]{1,0:T(8,128)(2,1)S(1)} collective-permute-done((bf16[128,2048]{1,0:T(8,128)(2,1)S(1)}, bf16[128,2048]{1,0:T(8,128)(2,1)S(1)}, u32[]{:S(2)}, u32[]{:S(2)}) %collective-permute-start.46) | collective-permute-done | bytes 524320 | tf_op jit(solution)/shard_map/ppermute | solution.py:251
  381.1 9.5 %collective-permute-done.51 = bf16[128,2048]{1,0:T(8,128)(2,1)S(1)} collective-permute-done((bf16[128,2048]{1,0:T(8,128)(2,1)S(1)}, bf16[128,2048]{1,0:T(8,128)(2,1)S(1)}, u32[]{:S(2)}, u32[]{:S(2)}) %collective-permute-start.51) | collective-permute-done | bytes 524320 | tf_op jit(solution)/shard_map/ppermute | solution.py:251
  400.1 5.4 collective-permute-done.57
  413.7 8.1 collective-permute-done.63
  422.1 9.1 %collective-permute-done.49 = bf16[128,2048]{1,0:T(8,128)(2,1)S(1)} collective-permute-done((bf16[128,2048]{1,0:T(8,128)(2,1)S(1)}, bf16[128,2048]{1,0:T(8,128)(2,1)S(1)}, u32[]{:S(2)}, u32[]{:S(2)}) %collective-permute-start.49) | collective-permute-done | bytes 524320 | tf_op jit(solution)/shard_map/ppermute | solution.py:251
  438.0 7.1 collective-permute-done.54
  456.4 8.2 shard_map.240
  468.5 12.5 %shard_map.241 = bf16[2,4,256,1024]{3,2,1,0:T(8,128)(2,1)} custom-call(bf16[2048,2048]{1,0:T(8,128)(2,1)} %copy-done.8, bf16[512,1024]{1,0:T(8,128)(2,1)S(1)} %pad_maximum_fusion.2.refs_1_, bf16[512,1024]{1,0:T(8,128)(2,1)S(1)} %pad_maximum_fusion.3.refs_2_, bf16[512,1024]{1,0:T(8,128)(2,1)S(1)} %pad_maximum_fusion.4.refs_3_, ...), custom_call_target="tpu_custom_call" | custom-call | flops 1 | bytes 1 | tf_op jit(solution)/shard_map/pallas_call | solution.py:111
  484.3 4.1 collective-permute-start.55
  488.4 7.6 collective-permute-done.60
  500.2 6.7 collective-permute-done.66
  507.1 17.3 %collective-permute-done.61 = bf16[128,2048]{1,0:T(8,128)(2,1)S(1)} collective-permute-done((bf16[128,2048]{1,0:T(8,128)(2,1)S(1)}, bf16[128,2048]{1,0:T(8,128)(2,1)S(1)}, u32[]{:S(2)}, u32[]{:S(2)}) %collective-permute-start.61) | collective-permute-done | bytes 524320 | tf_op jit(solution)/shard_map/ppermute | solution.py:264
  524.4 6.6 collective-permute-done.67
  537.1 11.4 %collective-permute-done.68 = bf16[128,2048]{1,0:T(8,128)(2,1)S(1)} collective-permute-done((bf16[128,2048]{1,0:T(8,128)(2,1)S(1)}, bf16[128,2048]{1,0:T(8,128)(2,1)S(1)}, u32[]{:S(2)}, u32[]{:S(2)}) %collective-permute-start.68) | collective-permute-done | bytes 524320 | tf_op jit(solution)/shard_map/ppermute | solution.py:251
  549.6 8.0 all-to-all-start.3
  558.0 3.6 fusion.45
  562.7 4.5 convolution_convert_fusion.3
  575.5 8.1 multiply_convert_fusion
  583.6 9.8 %all-to-all-done.3.own_ref = bf16[4,256,512]{2,1,0:T(8,128)(2,1)} async-done(((bf16[4,256,512]{2,1,0:T(8,128)(2,1)}), bf16[4,256,512]{2,1,0:T(8,128)(2,1)}, u32[]{:S(2)}, u32[]{:S(2)}) %all-to-all-start.3) | async-done | bytes 1048608 | tf_op jit(solution)/shard_map/all_to_all | solution.py:398
  599.5 11.3 %psum.29 = f32[5120]{0:T(1024)S(1)} all-reduce(f32[5120]{0:T(1024)S(1)} %pad_maximum_fusion.16), channel_id=1, replica_groups=mesh['fsdp'=4,'ctx'=2,'tp'=4] {'tp'}, use_global_device_ids=true, to_apply=%region_17.18 | all-reduce | flops 5120 | bytes 40960 | tf_op jit(solution)/shard_map/psum | solution.py:645
  622.8 4.4 fusion.6
  627.3 3.6 all-to-all-start.4
  633.6 3.9 fusion.5
  641.0 11.0 %collective-permute-done.71 = bf16[128,2048]{1,0:T(8,128)(2,1)S(1)} collective-permute-done((bf16[128,2048]{1,0:T(8,128)(2,1)S(1)}, bf16[128,2048]{1,0:T(8,128)(2,1)S(1)}, u32[]{:S(2)}, u32[]{:S(2)}) %collective-permute-start.71) | collective-permute-done | bytes 524320 | tf_op jit(solution)/shard_map/ppermute | solution.py:251
  658.0 29.7 %collective-permute-done.78.other_ref = bf16[4,256,512]{2,1,0:T(8,128)(2,1)} collective-permute-done((bf16[4,256,512]{2,1,0:T(8,128)(2,1)}, bf16[4,256,512]{2,1,0:T(8,128)(2,1)}, u32[]{:S(2)}, u32[]{:S(2)}) %collective-permute-start.78) | collective-permute-done | bytes 1048608 | tf_op jit(solution)/shard_map/ppermute | solution.py:251
  687.7 4.2 shard_map.242
  694.7 18.2 %all-to-all-done.4.own_ref = bf16[4,256,1024]{2,1,0:T(8,128)(2,1)S(1)} async-done(((bf16[4,256,1024]{2,1,0:T(8,128)(2,1)}), bf16[4,256,1024]{2,1,0:T(8,128)(2,1)S(1)}, u32[]{:S(2)}, u32[]{:S(2)}) %all-to-all-start.4) | async-done | bytes 2097184 | tf_op jit(solution)/shard_map/all_to_all | solution.py:398
  712.9 4.3 all-to-all-start.6
  721.0 12.3 %collective-permute-done.75 = bf16[4,272,512]{2,1,0:T(8,128)(2,1)} collective-permute-done((bf16[4,272,512]{2,1,0:T(8,128)(2,1)}, bf16[4,272,512]{2,1,0:T(8,128)(2,1)}, u32[]{:S(2)}, u32[]{:S(2)}) %collective-permute-start.75) | collective-permute-done | bytes 1114144 | tf_op jit(solution)/shard_map/ppermute | solution.py:251
  736.0 7.5 all-to-all-done.6
  743.5 3.5 all-to-all-start.5
  752.0 21.7 %all-to-all-done.5 = bf16[4,272,512]{2,1,0:T(8,128)(2,1)S(1)} async-done(((bf16[4,272,512]{2,1,0:T(8,128)(2,1)}), bf16[4,272,512]{2,1,0:T(8,128)(2,1)S(1)}, u32[]{:S(2)}, u32[]{:S(2)}) %all-to-all-start.5) | async-done | bytes 1114144 | tf_op jit(solution)/shard_map/all_to_all | solution.py:398
  775.4 24.8 %collective-permute-done.79.other_ref = bf16[4,256,1024]{2,1,0:T(8,128)(2,1)} collective-permute-done((bf16[4,256,1024]{2,1,0:T(8,128)(2,1)S(1)}, bf16[4,256,1024]{2,1,0:T(8,128)(2,1)}, u32[]{:S(2)}, u32[]{:S(2)}) %collective-permute-start.79) | collective-permute-done | bytes 2097184 | tf_op jit(solution)/shard_map/ppermute | solution.py:251
  800.1 5.9 shard_map.243
  806.1 5.3 all-reduce.6.cloned.1.call-done
  820.8 5.2 maximum_select_fusion
  826.0 3.4 fusion.8
  (590 shorter events, 275.6 us)
Async XLA Ops:
  18.9 15.0 %collective-permute-start.4 = (bf16[256,1024]{1,0:T(8,128)(2,1)S(1)}, bf16[256,1024]{1,0:T(8,128)(2,1)}, u32[]{:S(2)}, u32[]{:S(2)}) collective-permute-start(bf16[256,1024]{1,0:T(8,128)(2,1)S(1)} %fusion.77), channel_id=1, source_target_pairs={{0,24},{8,0},{16,8},{24,16},{1,25},{9,1},{17,9},{25,17},{2,26},{10... | collective-permute-start | bytes 1572872 | tf_op jit(solution)/shard_map/ppermute | solution.py:264
  20.4 24.8 %collective-permute-start = (bf16[256,1024]{1,0:T(8,128)(2,1)}, bf16[256,1024]{1,0:T(8,128)(2,1)}, u32[]{:S(2)}, u32[]{:S(2)}) collective-permute-start(bf16[256,1024]{1,0:T(8,128)(2,1)} %constant_dynamic-slice_fusion.18), channel_id=1, source_target_pairs={{0,24},{8,0},{16,8},{24,16},{1,25},{9,1},{17,9},{25,17},{2,26},{10... | collective-permute-start | bytes 1572872 | tf_op jit(solution)/shard_map/ppermute | solution.py:264
  33.9 31.7 %collective-permute-start.6 = (bf16[256,1024]{1,0:T(8,128)(2,1)}, bf16[256,1024]{1,0:T(8,128)(2,1)}, u32[]{:S(2)}, u32[]{:S(2)}) collective-permute-start(bf16[256,1024]{1,0:T(8,128)(2,1)} %collective-permute-done.4), channel_id=1, source_target_pairs={{0,24},{8,0},{16,8},{24,16},{1,25},{9,1},{17,9},{25,17},{2,26},{10... | collective-permute-start | bytes 1572872 | tf_op jit(solution)/shard_map/ppermute | solution.py:264
  47.7 19.9 %collective-permute-start.14 = (bf16[256,1024]{1,0:T(8,128)(2,1)}, bf16[256,1024]{1,0:T(8,128)(2,1)}, u32[]{:S(2)}, u32[]{:S(2)}) collective-permute-start(bf16[256,1024]{1,0:T(8,128)(2,1)} %collective-permute-done), channel_id=1, source_target_pairs={{0,24},{8,0},{16,8},{24,16},{1,25},{9,1},{17,9},{25,17},{2,26},{10... | collective-permute-start | bytes 1572872 | tf_op jit(solution)/shard_map/ppermute | solution.py:264
  50.6 19.3 %collective-permute-start.5 = (bf16[256,1024]{1,0:T(8,128)(2,1)}, bf16[256,1024]{1,0:T(8,128)(2,1)}, u32[]{:S(2)}, u32[]{:S(2)}) collective-permute-start(bf16[256,1024]{1,0:T(8,128)(2,1)} %collective-permute-done.4), channel_id=1, source_target_pairs={{0,4},{4,0},{1,5},{5,1},{2,6},{6,2},{3,7},{7,3},{8,12},{12,8},{9,1... | collective-permute-start | bytes 1572872 | tf_op jit(solution)/shard_map/ppermute | solution.py:251
  51.2 26.7 %collective-permute-start.10 = (bf16[256,1024]{1,0:T(8,128)(2,1)}, bf16[256,1024]{1,0:T(8,128)(2,1)}, u32[]{:S(2)}, u32[]{:S(2)}) collective-permute-start(bf16[256,1024]{1,0:T(8,128)(2,1)} %collective-permute-done), channel_id=1, source_target_pairs={{0,4},{4,0},{1,5},{5,1},{2,6},{6,2},{3,7},{7,3},{8,12},{12,8},{9,1... | collective-permute-start | bytes 1572872 | tf_op jit(solution)/shard_map/ppermute | solution.py:251
  65.7 28.3 %collective-permute-start.8 = (bf16[256,1024]{1,0:T(8,128)(2,1)}, bf16[256,1024]{1,0:T(8,128)(2,1)}, u32[]{:S(2)}, u32[]{:S(2)}) collective-permute-start(bf16[256,1024]{1,0:T(8,128)(2,1)} %collective-permute-done.6), channel_id=1, source_target_pairs={{0,24},{8,0},{16,8},{24,16},{1,25},{9,1},{17,9},{25,17},{2,26},{10... | collective-permute-start | bytes 1572872 | tf_op jit(solution)/shard_map/ppermute | solution.py:264
  65.8 16.8 %collective-permute-start.3 = (bf16[128,2048]{1,0:T(8,128)(2,1)S(1)}, bf16[128,2048]{1,0:T(8,128)(2,1)S(1)}, u32[]{:S(2)}, u32[]{:S(2)}) collective-permute-start(bf16[128,2048]{1,0:T(8,128)(2,1)S(1)} %pad_maximum_fusion.12), channel_id=1, source_target_pairs={{0,1},{1,0},{2,3},{3,2},{4,5},{5,4},{6,7},{7,6},{8,9},{9,8},{10,11... | collective-permute-start | bytes 1572872 | tf_op jit(solution)/shard_map/ppermute | solution.py:251
  67.7 20.4 %collective-permute-start.16 = (bf16[256,1024]{1,0:T(8,128)(2,1)}, bf16[256,1024]{1,0:T(8,128)(2,1)}, u32[]{:S(2)}, u32[]{:S(2)}) collective-permute-start(bf16[256,1024]{1,0:T(8,128)(2,1)} %collective-permute-done.14), channel_id=1, source_target_pairs={{0,24},{8,0},{16,8},{24,16},{1,25},{9,1},{17,9},{25,17},{2,26},{10... | collective-permute-start | bytes 1572872 | tf_op jit(solution)/shard_map/ppermute | solution.py:264
  69.9 24.6 %collective-permute-start.7 = (bf16[256,1024]{1,0:T(8,128)(2,1)}, bf16[256,1024]{1,0:T(8,128)(2,1)}, u32[]{:S(2)}, u32[]{:S(2)}) collective-permute-start(bf16[256,1024]{1,0:T(8,128)(2,1)} %collective-permute-done.6), channel_id=1, source_target_pairs={{0,4},{4,0},{1,5},{5,1},{2,6},{6,2},{3,7},{7,3},{8,12},{12,8},{9,1... | collective-permute-start | bytes 1572872 | tf_op jit(solution)/shard_map/ppermute | solution.py:251
  77.9 22.5 %collective-permute-start.15 = (bf16[256,1024]{1,0:T(8,128)(2,1)}, bf16[256,1024]{1,0:T(8,128)(2,1)}, u32[]{:S(2)}, u32[]{:S(2)}) collective-permute-start(bf16[256,1024]{1,0:T(8,128)(2,1)} %collective-permute-done.14), channel_id=1, source_target_pairs={{0,4},{4,0},{1,5},{5,1},{2,6},{6,2},{3,7},{7,3},{8,12},{12,8},{9,1... | collective-permute-start | bytes 1572872 | tf_op jit(solution)/shard_map/ppermute | solution.py:251
  88.1 41.0 %all-to-all-start = ((bf16[4,256,512]{2,1,0:T(8,128)(2,1)}), bf16[4,256,512]{2,1,0:T(8,128)(2,1)}, u32[]{:S(2)}, u32[]{:S(2)}) async-start(bf16[4,256,512]{2,1,0:T(8,128)(2,1)} %get-tuple-element.76), calls=%async_computation | async-start | bytes 2097152 | tf_op jit(solution)/shard_map/all_to_all | solution.py:398
  92.3 19.2 %collective-permute-start.17 = (bf16[256,1024]{1,0:T(8,128)(2,1)}, bf16[256,1024]{1,0:T(8,128)(2,1)S(1)}, u32[]{:S(2)}, u32[]{:S(2)}) collective-permute-start(bf16[256,1024]{1,0:T(8,128)(2,1)} %collective-permute-done.16), channel_id=1, source_target_pairs={{0,4},{4,0},{1,5},{5,1},{2,6},{6,2},{3,7},{7,3},{8,12},{12,8},{9,1... | collective-permute-start | bytes 1572872 | tf_op jit(solution)/shard_map/ppermute | solution.py:251
  93.9 29.0 %collective-permute-start.9 = (bf16[256,1024]{1,0:T(8,128)(2,1)}, bf16[256,1024]{1,0:T(8,128)(2,1)}, u32[]{:S(2)}, u32[]{:S(2)}) collective-permute-start(bf16[256,1024]{1,0:T(8,128)(2,1)} %collective-permute-done.8), channel_id=1, source_target_pairs={{0,4},{4,0},{1,5},{5,1},{2,6},{6,2},{3,7},{7,3},{8,12},{12,8},{9,1... | collective-permute-start | bytes 1572872 | tf_op jit(solution)/shard_map/ppermute | solution.py:251
  129.1 33.0 %all-to-all-start.1 = ((bf16[4,256,512]{2,1,0:T(8,128)(2,1)}), bf16[4,256,512]{2,1,0:T(8,128)(2,1)}, u32[]{:S(2)}, u32[]{:S(2)}) async-start(bf16[4,256,512]{2,1,0:T(8,128)(2,1)} %get-tuple-element.79), calls=%async_computation.1 | async-start | bytes 2097152 | tf_op jit(solution)/shard_map/all_to_all | solution.py:398
  136.7 25.3 %collective-permute-start.18 = (bf16[4,256,512]{2,1,0:T(8,128)(2,1)}, bf16[4,256,512]{2,1,0:T(8,128)(2,1)}, u32[]{:S(2)}, u32[]{:S(2)}) collective-permute-start(bf16[4,256,512]{2,1,0:T(8,128)(2,1)} %all-to-all-done.gate_a), channel_id=1, source_target_pairs={{0,4},{4,0},{1,5},{5,1},{2,6},{6,2},{3,7},{7,3},{8,12},{12,8},{9,1... | collective-permute-start | bytes 3145736 | tf_op jit(solution)/shard_map/ppermute | solution.py:251
  170.4 31.0 %all-to-all-start.2 = ((bf16[4,256,512]{2,1,0:T(8,128)(2,1)}), bf16[4,256,512]{2,1,0:T(8,128)(2,1)}, u32[]{:S(2)}, u32[]{:S(2)}) async-start(bf16[4,256,512]{2,1,0:T(8,128)(2,1)} %get-tuple-element.85), calls=%async_computation.2 | async-start | bytes 2097152 | tf_op jit(solution)/shard_map/all_to_all | solution.py:398
  175.2 360.3 %reduce-scatter.5.cloned.1.call-start = ((), (), s32[]{:S(2)}) async-start(), calls=%async_computation.11 | async-start | bytes 3145728 | tf_op jit(solution)/shard_map/reduce_scatter | solution.py:583
  186.1 16.7 %collective-permute-start.21 = (bf16[128,2048]{1,0:T(8,128)(2,1)S(1)}, bf16[128,2048]{1,0:T(8,128)(2,1)}, u32[]{:S(2)}, u32[]{:S(2)}) collective-permute-start(bf16[128,2048]{1,0:T(8,128)(2,1)S(1)} %fusion.74), channel_id=1, source_target_pairs={{0,2},{1,3},{2,0},{3,1},{4,6},{5,7},{6,4},{7,5},{8,10},{9,11},{10,... | collective-permute-start | bytes 1572872 | tf_op jit(solution)/shard_map/ppermute | solution.py:251
  187.7 29.7 %collective-permute-start.23 = (bf16[4,256,512]{2,1,0:T(8,128)(2,1)}, bf16[4,256,512]{2,1,0:T(8,128)(2,1)}, u32[]{:S(2)}, u32[]{:S(2)}) collective-permute-start(bf16[4,256,512]{2,1,0:T(8,128)(2,1)} %all-to-all-done.1.up_a), channel_id=1, source_target_pairs={{0,4},{4,0},{1,5},{5,1},{2,6},{6,2},{3,7},{7,3},{8,12},{12,8},{9,1... | collective-permute-start | bytes 3145736 | tf_op jit(solution)/shard_map/ppermute | solution.py:251
  201.4 33.1 %collective-permute-start.24 = (bf16[4,256,512]{2,1,0:T(8,128)(2,1)}, bf16[4,256,512]{2,1,0:T(8,128)(2,1)}, u32[]{:S(2)}, u32[]{:S(2)}) collective-permute-start(bf16[4,256,512]{2,1,0:T(8,128)(2,1)} %all-to-all-done.2.own_ref), channel_id=1, source_target_pairs={{0,4},{4,0},{1,5},{5,1},{2,6},{6,2},{3,7},{7,3},{8,12},{12,8},{9,1... | collective-permute-start | bytes 3145736 | tf_op jit(solution)/shard_map/ppermute | solution.py:251
  204.0 40.7 %collective-permute-start.22 = (bf16[256,2048]{1,0:T(8,128)(2,1)S(1)}, bf16[256,2048]{1,0:T(8,128)(2,1)}, u32[]{:S(2)}, u32[]{:S(2)}) collective-permute-start(bf16[256,2048]{1,0:T(8,128)(2,1)S(1)} %pad_maximum_fusion.7), channel_id=1, source_target_pairs={{0,1},{1,0},{2,3},{3,2},{4,5},{5,4},{6,7},{7,6},{8,9},{9,8},{10,11... | collective-permute-start | bytes 3145736 | tf_op jit(solution)/shard_map/ppermute | solution.py:251
  213.9 24.4 %collective-permute-start.28 = (bf16[128,2048]{1,0:T(8,128)(2,1)S(1)}, bf16[128,2048]{1,0:T(8,128)(2,1)S(1)}, u32[]{:S(2)}, u32[]{:S(2)}) collective-permute-start(bf16[128,2048]{1,0:T(8,128)(2,1)S(1)} %collective-permute-done.27), channel_id=1, source_target_pairs={{0,2},{1,3},{2,0},{3,1},{4,6},{5,7},{6,4},{7,5},{8,10},{9,11},{10,... | collective-permute-start | bytes 1572872 | tf_op jit(solution)/shard_map/ppermute | solution.py:251
  214.5 24.6 %collective-permute-start.33 = (bf16[128,2048]{1,0:T(8,128)(2,1)S(1)}, bf16[128,2048]{1,0:T(8,128)(2,1)}, u32[]{:S(2)}, u32[]{:S(2)}) collective-permute-start(bf16[128,2048]{1,0:T(8,128)(2,1)S(1)} %collective-permute-done.27), channel_id=1, source_target_pairs={{0,24},{8,0},{16,8},{24,16},{1,25},{9,1},{17,9},{25,17},{2,26},{10... | collective-permute-start | bytes 1572872 | tf_op jit(solution)/shard_map/ppermute | solution.py:264
  239.1 20.0 %collective-permute-start.29 = (bf16[256,2048]{1,0:T(8,128)(2,1)}, bf16[256,2048]{1,0:T(8,128)(2,1)S(1)}, u32[]{:S(2)}, u32[]{:S(2)}) collective-permute-start(bf16[256,2048]{1,0:T(8,128)(2,1)} %constant_dynamic-update-slice_fusion.5), channel_id=1, source_target_pairs={{0,1},{1,0},{2,3},{3,2},{4,5},{5,4},{6,7},{7,6},{8,9},{9,8},{10,11... | collective-permute-start | bytes 3145736 | tf_op jit(solution)/shard_map/ppermute | solution.py:251
  239.1 17.8 %collective-permute-start.34 = (bf16[128,2048]{1,0:T(8,128)(2,1)}, bf16[128,2048]{1,0:T(8,128)(2,1)S(1)}, u32[]{:S(2)}, u32[]{:S(2)}) collective-permute-start(bf16[128,2048]{1,0:T(8,128)(2,1)} %collective-permute-done.33), channel_id=1, source_target_pairs={{0,2},{1,3},{2,0},{3,1},{4,6},{5,7},{6,4},{7,5},{8,10},{9,11},{10,... | collective-permute-start | bytes 1572872 | tf_op jit(solution)/shard_map/ppermute | solution.py:251
  239.6 17.9 %collective-permute-start.39 = (bf16[128,2048]{1,0:T(8,128)(2,1)}, bf16[128,2048]{1,0:T(8,128)(2,1)S(1)}, u32[]{:S(2)}, u32[]{:S(2)}) collective-permute-start(bf16[128,2048]{1,0:T(8,128)(2,1)} %collective-permute-done.33), channel_id=1, source_target_pairs={{0,24},{8,0},{16,8},{24,16},{1,25},{9,1},{17,9},{25,17},{2,26},{10... | collective-permute-start | bytes 1572872 | tf_op jit(solution)/shard_map/ppermute | solution.py:264
  257.0 15.5 %collective-permute-start.35 = (bf16[256,2048]{1,0:T(8,128)(2,1)S(1)}, bf16[256,2048]{1,0:T(8,128)(2,1)S(1)}, u32[]{:S(2)}, u32[]{:S(2)}) collective-permute-start(bf16[256,2048]{1,0:T(8,128)(2,1)S(1)} %constant_dynamic-update-slice_fusion.7), channel_id=1, source_target_pairs={{0,1},{1,0},{2,3},{3,2},{4,5},{5,4},{6,7},{7,6},{8,9},{9,8},{10,11... | collective-permute-start | bytes 3145736 | tf_op jit(solution)/shard_map/ppermute | solution.py:251
  263.1 19.7 %collective-permute-start.26 = (bf16[128,2048]{1,0:T(8,128)(2,1)S(1)}, bf16[128,2048]{1,0:T(8,128)(2,1)S(1)}, u32[]{:S(2)}, u32[]{:S(2)}) collective-permute-start(bf16[128,2048]{1,0:T(8,128)(2,1)S(1)} %slice.692), channel_id=1, source_target_pairs={{0,2},{1,3},{2,0},{3,1},{4,6},{5,7},{6,4},{7,5},{8,10},{9,11},{10,... | collective-permute-start | bytes 1572872 | tf_op jit(solution)/shard_map/ppermute | solution.py:251
  264.4 20.9 %collective-permute-start.30 = (bf16[256,2048]{1,0:T(8,128)(2,1)S(1)}, bf16[256,2048]{1,0:T(8,128)(2,1)S(1)}, u32[]{:S(2)}, u32[]{:S(2)}) collective-permute-start(bf16[256,2048]{1,0:T(8,128)(2,1)S(1)} %convolution_convert_fusion.6), channel_id=1, source_target_pairs={{0,1},{1,0},{2,3},{3,2},{4,5},{5,4},{6,7},{7,6},{8,9},{9,8},{10,11... | collective-permute-start | bytes 3145736 | tf_op jit(solution)/shard_map/ppermute | solution.py:251
  272.4 16.4 %collective-permute-start.41 = (bf16[256,2048]{1,0:T(8,128)(2,1)S(1)}, bf16[256,2048]{1,0:T(8,128)(2,1)S(1)}, u32[]{:S(2)}, u32[]{:S(2)}) collective-permute-start(bf16[256,2048]{1,0:T(8,128)(2,1)S(1)} %constant_dynamic-update-slice_fusion.9), channel_id=1, source_target_pairs={{0,1},{1,0},{2,3},{3,2},{4,5},{5,4},{6,7},{7,6},{8,9},{9,8},{10,11... | collective-permute-start | bytes 3145736 | tf_op jit(solution)/shard_map/ppermute | solution.py:251
  288.7 15.4 %collective-permute-start.36 = (bf16[256,2048]{1,0:T(8,128)(2,1)S(1)}, bf16[256,2048]{1,0:T(8,128)(2,1)S(1)}, u32[]{:S(2)}, u32[]{:S(2)}) collective-permute-start(bf16[256,2048]{1,0:T(8,128)(2,1)S(1)} %convolution_convert_fusion.5), channel_id=1, source_target_pairs={{0,1},{1,0},{2,3},{3,2},{4,5},{5,4},{6,7},{7,6},{8,9},{9,8},{10,11... | collective-permute-start | bytes 3145736 | tf_op jit(solution)/shard_map/ppermute | solution.py:251
  307.6 23.0 %collective-permute-start.43 = (bf16[128,2048]{1,0:T(8,128)(2,1)S(1)}, bf16[128,2048]{1,0:T(8,128)(2,1)S(1)}, u32[]{:S(2)}, u32[]{:S(2)}) collective-permute-start(bf16[128,2048]{1,0:T(8,128)(2,1)S(1)} %slice.689), channel_id=1, source_target_pairs={{0,2},{1,3},{2,0},{3,1},{4,6},{5,7},{6,4},{7,5},{8,10},{9,11},{10,... | collective-permute-start | bytes 1572872 | tf_op jit(solution)/shard_map/ppermute | solution.py:251
  310.1 24.2 %collective-permute-start.32 = (bf16[128,2048]{1,0:T(8,128)(2,1)}, bf16[128,2048]{1,0:T(8,128)(2,1)}, u32[]{:S(2)}, u32[]{:S(2)}) collective-permute-start(bf16[128,2048]{1,0:T(8,128)(2,1)} %fusion.69), channel_id=1, source_target_pairs={{0,8},{8,16},{16,24},{24,0},{1,9},{9,17},{17,25},{25,1},{2,10},{10... | collective-permute-start | bytes 1572872 | tf_op jit(solution)/shard_map/ppermute | solution.py:264
  320.6 27.8 %collective-permute-start.38 = (bf16[128,2048]{1,0:T(8,128)(2,1)}, bf16[128,2048]{1,0:T(8,128)(2,1)}, u32[]{:S(2)}, u32[]{:S(2)}) collective-permute-start(bf16[128,2048]{1,0:T(8,128)(2,1)} %fusion.68), channel_id=1, source_target_pairs={{0,16},{8,24},{16,0},{24,8},{1,17},{9,25},{17,1},{25,9},{2,18},{10... | collective-permute-start | bytes 1572872 | tf_op jit(solution)/shard_map/ppermute | solution.py:264
  331.5 25.0 %collective-permute-start.44 = (bf16[128,2048]{1,0:T(8,128)(2,1)}, bf16[128,2048]{1,0:T(8,128)(2,1)}, u32[]{:S(2)}, u32[]{:S(2)}) collective-permute-start(bf16[128,2048]{1,0:T(8,128)(2,1)} %fusion.67), channel_id=1, source_target_pairs={{0,24},{8,0},{16,8},{24,16},{1,25},{9,1},{17,9},{25,17},{2,26},{10... | collective-permute-start | bytes 1572872 | tf_op jit(solution)/shard_map/ppermute | solution.py:264
  333.9 25.0 %collective-permute-start.45 = (bf16[128,2048]{1,0:T(8,128)(2,1)S(1)}, bf16[128,2048]{1,0:T(8,128)(2,1)S(1)}, u32[]{:S(2)}, u32[]{:S(2)}) collective-permute-start(bf16[128,2048]{1,0:T(8,128)(2,1)S(1)} %dynamic-slice_bitcast_fusion.3), channel_id=1, source_target_pairs={{0,4},{4,0},{1,5},{5,1},{2,6},{6,2},{3,7},{7,3},{8,12},{12,8},{9,1... | collective-permute-start | bytes 1572872 | tf_op jit(solution)/shard_map/ppermute | solution.py:251
  374.4 22.0 %collective-permute-start.47 = (bf16[256,2048]{1,0:T(8,128)(2,1)S(1)}, bf16[256,2048]{1,0:T(8,128)(2,1)S(1)}, u32[]{:S(2)}, u32[]{:S(2)}) collective-permute-start(bf16[256,2048]{1,0:T(8,128)(2,1)S(1)} %pad_maximum_fusion.8), channel_id=1, source_target_pairs={{0,1},{1,0},{2,3},{3,2},{4,5},{5,4},{6,7},{7,6},{8,9},{9,8},{10,11... | collective-permute-start | bytes 3145736 | tf_op jit(solution)/shard_map/ppermute | solution.py:251
  390.7 17.8 %collective-permute-start.52 = (bf16[256,2048]{1,0:T(8,128)(2,1)S(1)}, bf16[256,2048]{1,0:T(8,128)(2,1)S(1)}, u32[]{:S(2)}, u32[]{:S(2)}) collective-permute-start(bf16[256,2048]{1,0:T(8,128)(2,1)S(1)} %constant_dynamic-update-slice_fusion.11), channel_id=1, source_target_pairs={{0,1},{1,0},{2,3},{3,2},{4,5},{5,4},{6,7},{7,6},{8,9},{9,8},{10,11... | collective-permute-start | bytes 3145736 | tf_op jit(solution)/shard_map/ppermute | solution.py:251
  405.6 16.5 %collective-permute-start.58 = (bf16[256,2048]{1,0:T(8,128)(2,1)S(1)}, bf16[256,2048]{1,0:T(8,128)(2,1)S(1)}, u32[]{:S(2)}, u32[]{:S(2)}) collective-permute-start(bf16[256,2048]{1,0:T(8,128)(2,1)S(1)} %constant_dynamic-update-slice_fusion.13), channel_id=1, source_target_pairs={{0,1},{1,0},{2,3},{3,2},{4,5},{5,4},{6,7},{7,6},{8,9},{9,8},{10,11... | collective-permute-start | bytes 3145736 | tf_op jit(solution)/shard_map/ppermute | solution.py:251
  411.5 19.7 %collective-permute-start.53 = (bf16[256,2048]{1,0:T(8,128)(2,1)S(1)}, bf16[256,2048]{1,0:T(8,128)(2,1)S(1)}, u32[]{:S(2)}, u32[]{:S(2)}) collective-permute-start(bf16[256,2048]{1,0:T(8,128)(2,1)S(1)} %convolution_convert_fusion.11), channel_id=1, source_target_pairs={{0,1},{1,0},{2,3},{3,2},{4,5},{5,4},{6,7},{7,6},{8,9},{9,8},{10,11... | collective-permute-start | bytes 3145736 | tf_op jit(solution)/shard_map/ppermute | solution.py:251
  413.0 18.2 %collective-permute-start.49 = (bf16[128,2048]{1,0:T(8,128)(2,1)S(1)}, bf16[128,2048]{1,0:T(8,128)(2,1)S(1)}, u32[]{:S(2)}, u32[]{:S(2)}) collective-permute-start(bf16[128,2048]{1,0:T(8,128)(2,1)S(1)} %slice.688), channel_id=1, source_target_pairs={{0,2},{1,3},{2,0},{3,1},{4,6},{5,7},{6,4},{7,5},{8,10},{9,11},{10,... | collective-permute-start | bytes 1572872 | tf_op jit(solution)/shard_map/ppermute | solution.py:251
  421.9 16.1 %collective-permute-start.64 = (bf16[256,2048]{1,0:T(8,128)(2,1)S(1)}, bf16[256,2048]{1,0:T(8,128)(2,1)S(1)}, u32[]{:S(2)}, u32[]{:S(2)}) collective-permute-start(bf16[256,2048]{1,0:T(8,128)(2,1)S(1)} %constant_dynamic-update-slice_fusion.15), channel_id=1, source_target_pairs={{0,1},{1,0},{2,3},{3,2},{4,5},{5,4},{6,7},{7,6},{8,9},{9,8},{10,11... | collective-permute-start | bytes 3145736 | tf_op jit(solution)/shard_map/ppermute | solution.py:251
  464.6 128.8 %reduce-scatter.7.cloned.1.call-start = ((), (), s32[]{:S(2)}) async-start(), calls=%async_computation.12 | async-start | bytes 6291456 | tf_op jit(solution)/shard_map/reduce_scatter | solution.py:586
  481.0 15.0 %collective-permute-start.60 = (bf16[128,2048]{1,0:T(8,128)(2,1)}, bf16[128,2048]{1,0:T(8,128)(2,1)S(1)}, u32[]{:S(2)}, u32[]{:S(2)}) collective-permute-start(bf16[128,2048]{1,0:T(8,128)(2,1)} %slice.686), channel_id=1, source_target_pairs={{0,2},{1,3},{2,0},{3,1},{4,6},{5,7},{6,4},{7,5},{8,10},{9,11},{10,... | collective-permute-start | bytes 1572872 | tf_op jit(solution)/shard_map/ppermute | solution.py:251
  482.8 24.1 %collective-permute-start.66 = (bf16[128,2048]{1,0:T(8,128)(2,1)}, bf16[128,2048]{1,0:T(8,128)(2,1)S(1)}, u32[]{:S(2)}, u32[]{:S(2)}) collective-permute-start(bf16[128,2048]{1,0:T(8,128)(2,1)} %slice.685), channel_id=1, source_target_pairs={{0,2},{1,3},{2,0},{3,1},{4,6},{5,7},{6,4},{7,5},{8,10},{9,11},{10,... | collective-permute-start | bytes 1572872 | tf_op jit(solution)/shard_map/ppermute | solution.py:251
  484.3 22.8 %collective-permute-start.55 = (bf16[128,2048]{1,0:T(8,128)(2,1)S(1)}, bf16[128,2048]{1,0:T(8,128)(2,1)S(1)}, u32[]{:S(2)}, u32[]{:S(2)}) collective-permute-start(bf16[128,2048]{1,0:T(8,128)(2,1)S(1)} %fusion.63), channel_id=1, source_target_pairs={{0,8},{8,16},{16,24},{24,0},{1,9},{9,17},{17,25},{25,1},{2,10},{10... | collective-permute-start | bytes 1572872 | tf_op jit(solution)/shard_map/ppermute | solution.py:264
  497.4 27.1 %collective-permute-start.61 = (bf16[128,2048]{1,0:T(8,128)(2,1)S(1)}, bf16[128,2048]{1,0:T(8,128)(2,1)S(1)}, u32[]{:S(2)}, u32[]{:S(2)}) collective-permute-start(bf16[128,2048]{1,0:T(8,128)(2,1)S(1)} %fusion.62), channel_id=1, source_target_pairs={{0,16},{8,24},{16,0},{24,8},{1,17},{9,25},{17,1},{25,9},{2,18},{10... | collective-permute-start | bytes 1572872 | tf_op jit(solution)/shard_map/ppermute | solution.py:264
  507.1 23.9 %collective-permute-start.67 = (bf16[128,2048]{1,0:T(8,128)(2,1)S(1)}, bf16[128,2048]{1,0:T(8,128)(2,1)S(1)}, u32[]{:S(2)}, u32[]{:S(2)}) collective-permute-start(bf16[128,2048]{1,0:T(8,128)(2,1)S(1)} %fusion.61), channel_id=1, source_target_pairs={{0,24},{8,0},{16,8},{24,16},{1,25},{9,1},{17,9},{25,17},{2,26},{10... | collective-permute-start | bytes 1572872 | tf_op jit(solution)/shard_map/ppermute | solution.py:264
  549.6 43.8 %all-to-all-start.3 = ((bf16[4,256,512]{2,1,0:T(8,128)(2,1)}), bf16[4,256,512]{2,1,0:T(8,128)(2,1)}, u32[]{:S(2)}, u32[]{:S(2)}) async-start(bf16[4,256,512]{2,1,0:T(8,128)(2,1)} %bitcast.18), calls=%async_computation.4 | async-start | bytes 2097152 | tf_op jit(solution)/shard_map/all_to_all | solution.py:398
  557.6 178.4 %reduce-scatter.9.cloned.1.call-start = ((), (), s32[]{:S(2)}) async-start(), calls=%async_computation.13 | async-start | bytes 2621440 | tf_op jit(solution)/shard_map/reduce_scatter | solution.py:661
  571.6 164.4 %reduce-scatter.11.cloned.1.call-start = ((), (), s32[]{:S(2)}) async-start(), calls=%async_computation.14 | async-start | bytes 2621440 | tf_op jit(solution)/shard_map/reduce_scatter | solution.py:661
  627.3 85.6 %all-to-all-start.4 = ((bf16[4,256,1024]{2,1,0:T(8,128)(2,1)}), bf16[4,256,1024]{2,1,0:T(8,128)(2,1)S(1)}, u32[]{:S(2)}, u32[]{:S(2)}) async-start(bf16[4,256,1024]{2,1,0:T(8,128)(2,1)} %bitcast.164), calls=%async_computation.8 | async-start | bytes 4194304 | tf_op jit(solution)/shard_map/all_to_all | solution.py:398
  639.0 53.0 %collective-permute-start.77 = (bf16[4,256,512]{2,1,0:T(8,128)(2,1)}, bf16[4,256,512]{2,1,0:T(8,128)(2,1)}, u32[]{:S(2)}, u32[]{:S(2)}) collective-permute-start(bf16[4,256,512]{2,1,0:T(8,128)(2,1)} %dynamic-slice_bitcast_fusion.1), channel_id=1, source_target_pairs={{0,4},{4,0},{1,5},{5,1},{2,6},{6,2},{3,7},{7,3},{8,12},{12,8},{9,1... | collective-permute-start | bytes 3145736 | tf_op jit(solution)/shard_map/ppermute | solution.py:251
  639.0 48.8 %collective-permute-start.78 = (bf16[4,256,512]{2,1,0:T(8,128)(2,1)}, bf16[4,256,512]{2,1,0:T(8,128)(2,1)}, u32[]{:S(2)}, u32[]{:S(2)}) collective-permute-start(bf16[4,256,512]{2,1,0:T(8,128)(2,1)} %all-to-all-done.3.own_ref), channel_id=1, source_target_pairs={{0,4},{4,0},{1,5},{5,1},{2,6},{6,2},{3,7},{7,3},{8,12},{12,8},{9,1... | collective-permute-start | bytes 3145736 | tf_op jit(solution)/shard_map/ppermute | solution.py:251
  653.3 63.9 %collective-permute-start.72 = (bf16[2,128,2048]{2,1,0:T(8,128)(2,1)}, bf16[2,128,2048]{2,1,0:T(8,128)(2,1)}, u32[]{:S(2)}, u32[]{:S(2)}) collective-permute-start(bf16[2,128,2048]{2,1,0:T(8,128)(2,1)} %pad_maximum_fusion.11), channel_id=1, source_target_pairs={{2,4},{4,2},{3,5},{5,3},{10,12},{12,10},{11,13},{13,11},{18,20},{2... | collective-permute-start | bytes 3145736 | tf_op jit(solution)/shard_map/ppermute | solution.py:555
  655.0 78.3 %collective-permute-start.75 = (bf16[4,272,512]{2,1,0:T(8,128)(2,1)}, bf16[4,272,512]{2,1,0:T(8,128)(2,1)}, u32[]{:S(2)}, u32[]{:S(2)}) collective-permute-start(bf16[4,272,512]{2,1,0:T(8,128)(2,1)} %pad_maximum_fusion.1), channel_id=1, source_target_pairs={{0,4},{4,0},{1,5},{5,1},{2,6},{6,2},{3,7},{7,3},{8,12},{12,8},{9,1... | collective-permute-start | bytes 3342344 | tf_op jit(solution)/shard_map/ppermute | solution.py:251
  712.9 30.6 %all-to-all-start.6 = ((bf16[4,256,512]{2,1,0:T(8,128)(2,1)}), bf16[4,256,512]{2,1,0:T(8,128)(2,1)}, u32[]{:S(2)}, u32[]{:S(2)}) async-start(bf16[4,256,512]{2,1,0:T(8,128)(2,1)} %fusion.25), calls=%async_computation.10 | async-start | bytes 2097152 | tf_op jit(solution)/shard_map/all_to_all | solution.py:398
  719.5 27.8 %collective-permute-start.73 = (bf16[2,128,2048]{2,1,0:T(8,128)(2,1)}, bf16[2,128,2048]{2,1,0:T(8,128)(2,1)}, u32[]{:S(2)}, u32[]{:S(2)}) collective-permute-start(bf16[2,128,2048]{2,1,0:T(8,128)(2,1)} %broadcast_select_fusion.1), channel_id=1, source_target_pairs={{0,2},{1,3},{2,0},{3,1},{4,6},{5,7},{6,4},{7,5},{8,10},{9,11},{10,... | collective-permute-start | bytes 3145736 | tf_op jit(solution)/shard_map/ppermute | solution.py:251
  736.0 64.2 %collective-permute-start.79 = (bf16[4,256,1024]{2,1,0:T(8,128)(2,1)S(1)}, bf16[4,256,1024]{2,1,0:T(8,128)(2,1)}, u32[]{:S(2)}, u32[]{:S(2)}) collective-permute-start(bf16[4,256,1024]{2,1,0:T(8,128)(2,1)S(1)} %all-to-all-done.4.own_ref), channel_id=1, source_target_pairs={{0,4},{4,0},{1,5},{5,1},{2,6},{6,2},{3,7},{7,3},{8,12},{12,8},{9,1... | collective-permute-start | bytes 6291464 | tf_op jit(solution)/shard_map/ppermute | solution.py:251
  743.5 30.3 %all-to-all-start.5 = ((bf16[4,272,512]{2,1,0:T(8,128)(2,1)}), bf16[4,272,512]{2,1,0:T(8,128)(2,1)S(1)}, u32[]{:S(2)}, u32[]{:S(2)}) async-start(bf16[4,272,512]{2,1,0:T(8,128)(2,1)} %add_convert_fusion), calls=%async_computation.9 | async-start | bytes 2228224 | tf_op jit(solution)/shard_map/all_to_all | solution.py:398
  747.0 64.4 %all-reduce.6.cloned.1.call-start = ((), (), s32[]{:S(2)}) async-start(), calls=%async_computation.15 | async-start | bytes 2097152 | tf_op jit(solution)/shard_map/psum | solution.py:702
  750.6 70.2 %collective-permute-start.74 = (bf16[2,2,128,2048]{3,2,0,1:T(8,128)(2,1)}, bf16[2,2,128,2048]{3,2,0,1:T(8,128)(2,1)}, u32[]{:S(2)}, u32[]{:S(2)}) collective-permute-start(bf16[2,2,128,2048]{3,2,0,1:T(8,128)(2,1)} %maximum_select_fusion.1), channel_id=1, source_target_pairs={{0,1},{1,0},{2,3},{3,2},{4,5},{5,4},{6,7},{7,6},{8,9},{9,8},{10,11... | collective-permute-start | bytes 6291464 | tf_op jit(solution)/shard_map/ppermute | solution.py:251
  774.0 39.0 %collective-permute-start.76 = (bf16[256,512]{1,0:T(8,128)(2,1)S(1)}, bf16[256,512]{1,0:T(8,128)(2,1)S(1)}, u32[]{:S(2)}, u32[]{:S(2)}) collective-permute-start(bf16[256,512]{1,0:T(8,128)(2,1)S(1)} %slice.694), channel_id=1, source_target_pairs={{0,4},{4,0},{1,5},{5,1},{2,6},{6,2},{3,7},{7,3},{8,12},{12,8},{9,1... | collective-permute-start | bytes 786440 | tf_op jit(solution)/shard_map/ppermute | solution.py:251
  (141 other events, 1284.7 us)
Sparse Core Ops, SparseCore 0:
  464.7 31.5 reduce-scatter.4
  499.3 54.3 reduce-scatter.6
  571.7 47.0 reduce-scatter.8
  627.4 73.3 reduce-scatter.10
  750.8 60.5 all-reduce.5
